TPU v7x, 128 devices: a whole 4x4x4 slice. The times are simulated.
128 devices in a mesh: dp: 32 (over z, x, core), sy: 2 (over y_hi), sx: 2 (over y_lo).
Axes of the slice: x: 4, y: 4 (y_hi: 2, y_lo: 2; y = y_hi * 2 + y_lo), z: 4, core: 2. Of those that a mesh axis runs over, the one named last changes fastest.
Arguments:
- features: bfloat16 [32, 16, 32, 640], P('dp', 'sy', 'sx'), may hold values from -6 to 6
- bucket_ids: int32 [32], P('dp'), may hold values from 0 to 7
- bucket_sizes: int32 [8, 2], replicated, may hold values from 8 to 32, as said below
- conv_weight: bfloat16 [5760, 640], replicated, may hold values from -0.078125 to 0.078125
- norm_gain: float32 [640], replicated, may hold values from 0.25 to 1.75
- query_weight: bfloat16 [640, 640], replicated, may hold values from -0.25 to 0.25
- key_weight: bfloat16 [640, 640], replicated, may hold values from -0.25 to 0.25
- value_weight: bfloat16 [640, 640], replicated, may hold values from -0.25 to 0.25
- out_weight: bfloat16 [640, 640], replicated, may hold values from -0.25 to 0.25
- out_grad: bfloat16 [32, 16, 32, 640], P('dp', 'sy', 'sx'), may hold values from -6 to 6
Outputs:
- block_out: bfloat16 [32, 16, 32, 640], P('dp', 'sy', 'sx')
- grad_conv: float32 [5760, 640], P('dp', ('sy', 'sx'))
- grad_query: float32 [640, 640], P('dp', ('sy', 'sx'))
- grad_key: float32 [640, 640], P('dp', ('sy', 'sx'))
- grad_value: float32 [640, 640], P('dp', ('sy', 'sx'))
- grad_out: float32 [640, 640], P('dp', ('sy', 'sx'))
Inputs may be any that keep to these rules, and one draw needn't show every extreme that they name: Each row of bucket_sizes holds a bucket's latent rows, from 8 to 16, and columns, from 16 to 32; bucket 0 is the full 16 x 32 grid and bucket 1 is 8 x 16.
All inputs are finite; a program needn't handle non-finite values.
Results may differ from a plain program's by a relative error of at most 0.013.
Values may be sent and summed in bfloat16 or wider, within the bound.
No kernel may reach another device: no remote copies, remote signals or barrier semaphores. Data moves between devices by JAX's collectives and lax.ppermute only.
A program may use at most 192 MiB of HBM per device.

v0:
```python
import jax
import jax.numpy as jnp
from jax import lax
from jax.sharding import PartitionSpec as P

HEADS = 10


def extended(block, sides, width):
    for axis, dim in sides:
        count = lax.axis_size(axis)
        forward = [(i, i + 1) for i in range(count - 1)]
        backward = [(target, source) for source, target in forward]
        low = lax.ppermute(
            lax.slice_in_dim(block, block.shape[dim] - width, None, axis=dim), axis, forward
        )
        high = lax.ppermute(lax.slice_in_dim(block, 0, width, axis=dim), axis, backward)
        block = jnp.concatenate([low, block, high], axis=dim)
    return block


def sent_together(arrays, axis, dim, along):
    widths = [a.shape[along] for a in arrays]
    both = jnp.concatenate(arrays, axis=along)
    out = lax.all_gather(both, axis, axis=dim, tiled=True)
    return tuple(jnp.split(out, [sum(widths[:k]) for k in range(1, len(widths))], axis=along))


def cut_along(array, dim, count):
    lengths = array.shape
    pieces = array.reshape(*lengths[:dim], count, lengths[dim] // count, *lengths[dim + 1 :])
    return jnp.moveaxis(pieces, dim, 0)


def summed_on_arrival(array, axis, dim):
    count = lax.axis_size(axis)
    pieces = lax.all_to_all(cut_along(array, dim, count), axis, 0, 0, tiled=True)
    return jnp.sum(pieces, axis=0)


def sent_together_2(arrays, axis, dim, along):
    ends, at = ([], 0)
    for a in arrays[:-1]:
        at += a.shape[along]
        ends.append(at)
    both = jnp.concatenate(arrays, axis=along)
    return tuple(jnp.split(summed_on_arrival(both, axis, dim), ends, axis=along))


def layer_norm(hidden, gain):
    mean = jnp.mean(hidden, axis=-1, keepdims=True)
    centred = hidden - mean
    spread = jnp.mean(centred * centred, axis=-1, keepdims=True)
    return centred * lax.rsqrt(spread + 1e-05) * gain


def patch_rows(padded, rows, cols):
    taps = [padded[dy : dy + rows, dx : dx + cols, :] for dy in range(3) for dx in range(3)]
    return jnp.concatenate(taps, axis=-1).reshape(rows * cols, -1)


def masked_scores(query, keys, key_valid, start, width, scale):
    scores = (
        jnp.dot(
            query[:, start : start + width],
            keys[:, start : start + width].T,
            preferred_element_type=jnp.float32,
        )
        * scale
    )
    return jnp.where(key_valid[None, :], scores, -1e30)


def head_probs(query, keys, key_valid, start, width, scale):
    return jax.nn.softmax(masked_scores(query, keys, key_valid, start, width, scale), axis=-1)


def attend(query, keys, values, key_valid, heads):
    width = query.shape[1] // heads
    scale = width ** (-0.5)
    parts = []
    for head in range(heads):
        start = head * width
        probs = head_probs(query, keys, key_valid, start, width, scale)
        parts.append(
            jnp.dot(
                probs.astype(jnp.bfloat16),
                values[:, start : start + width],
                preferred_element_type=jnp.float32,
            ).astype(jnp.bfloat16)
        )
    return jnp.concatenate(parts, axis=-1)


def query_side(query, keys, values, key_valid, grad_context, heads):
    width = query.shape[1] // heads
    scale = width ** (-0.5)
    dq_parts, lse_parts, delta_parts = ([], [], [])
    for head in range(heads):
        start = head * width
        scores = masked_scores(query, keys, key_valid, start, width, scale)
        top = jnp.max(scores, axis=-1, keepdims=True)
        expo = jnp.exp(scores - top)
        total = jnp.sum(expo, axis=-1, keepdims=True)
        probs = expo / total
        grad_slice = grad_context[:, start : start + width]
        dprob = jnp.dot(
            grad_slice, values[:, start : start + width].T, preferred_element_type=jnp.float32
        )
        delta = jnp.sum(probs * dprob, axis=-1, keepdims=True)
        dscore = (probs * (dprob - delta) * scale).astype(jnp.bfloat16)
        dq_parts.append(
            jnp.dot(dscore, keys[:, start : start + width], preferred_element_type=jnp.float32)
        )
        lse_parts.append(top + jnp.log(total))
        delta_parts.append(delta)
    return (
        jnp.concatenate(dq_parts, axis=-1),
        jnp.concatenate(lse_parts, axis=-1),
        jnp.concatenate(delta_parts, axis=-1),
    )


def key_side(query_all, grad_all, lse_all, delta_all, keys, values, key_valid, heads):
    width = keys.shape[1] // heads
    scale = width ** (-0.5)
    dk_parts, dv_parts = ([], [])
    for head in range(heads):
        start = head * width
        scores = masked_scores(query_all, keys, key_valid, start, width, scale)
        probs = jnp.exp(scores - lse_all[:, head : head + 1])
        probs_b = probs.astype(jnp.bfloat16)
        grad_slice = grad_all[:, start : start + width]
        dprob = jnp.dot(
            grad_slice, values[:, start : start + width].T, preferred_element_type=jnp.float32
        )
        dscore = (probs * (dprob - delta_all[:, head : head + 1]) * scale).astype(jnp.bfloat16)
        dk_parts.append(
            jnp.dot(
                dscore.T, query_all[:, start : start + width], preferred_element_type=jnp.float32
            )
        )
        dv_parts.append(jnp.dot(probs_b.T, grad_slice, preferred_element_type=jnp.float32))
    return (jnp.concatenate(dk_parts, axis=-1), jnp.concatenate(dv_parts, axis=-1))


def body(
    features,
    bucket_ids,
    bucket_sizes,
    conv_weight,
    norm_gain,
    query_weight,
    key_weight,
    value_weight,
    out_weight,
    out_grad,
):
    rows_dev = features.shape[1]
    cols_dev = features.shape[2]
    width = features.shape[3]
    count_y = lax.axis_size("sy")
    count_x = lax.axis_size("sx")
    chosen = jnp.arange(bucket_sizes.shape[0], dtype=jnp.int32) == bucket_ids[0]
    height = jnp.sum(jnp.where(chosen, bucket_sizes[:, 0], 0))
    breadth = jnp.sum(jnp.where(chosen, bucket_sizes[:, 1], 0))
    local_rows = lax.axis_index("sy") * rows_dev + jnp.arange(rows_dev, dtype=jnp.int32)
    local_cols = lax.axis_index("sx") * cols_dev + jnp.arange(cols_dev, dtype=jnp.int32)
    valid = (local_rows[:, None] < height) & (local_cols[None, :] < breadth)
    valid_flat = valid.reshape(-1, 1).astype(jnp.float32)
    members = jnp.arange(count_y * count_x, dtype=jnp.int32)
    key_rows = (members // count_x)[:, None, None] * rows_dev + jnp.arange(
        rows_dev, dtype=jnp.int32
    )[None, :, None]
    key_cols = (members % count_x)[:, None, None] * cols_dev + jnp.arange(
        cols_dev, dtype=jnp.int32
    )[None, None, :]
    key_valid = ((key_rows < height) & (key_cols < breadth)).reshape(-1)
    xin = (features[0].astype(jnp.float32) * valid[:, :, None].astype(jnp.float32)).astype(
        jnp.bfloat16
    )
    padded = extended(xin, (("sy", 0), ("sx", 1)), 1)
    patches = patch_rows(padded, rows_dev, cols_dev)
    pre = jnp.dot(patches, conv_weight, preferred_element_type=jnp.float32)
    hidden = (valid_flat * (xin.reshape(-1, width).astype(jnp.float32) + jax.nn.silu(pre))).astype(
        jnp.bfloat16
    )
    hidden_f = hidden.astype(jnp.float32)
    normed_f, pullback = jax.vjp(lambda value: layer_norm(value, norm_gain), hidden_f)
    normed = normed_f.astype(jnp.bfloat16)
    query = jnp.dot(normed, query_weight, preferred_element_type=jnp.float32).astype(jnp.bfloat16)
    keys = jnp.dot(normed, key_weight, preferred_element_type=jnp.float32).astype(jnp.bfloat16)
    values = jnp.dot(normed, value_weight, preferred_element_type=jnp.float32).astype(jnp.bfloat16)
    keys_all, values_all = sent_together((keys, values), ("sy", "sx"), 0, 1)
    context = attend(query, keys_all, values_all, key_valid, HEADS)
    block = (
        valid_flat * (hidden_f + jnp.dot(context, out_weight, preferred_element_type=jnp.float32))
    ).astype(jnp.bfloat16)
    grad_b = (out_grad[0].reshape(-1, width).astype(jnp.float32) * valid_flat).astype(jnp.bfloat16)
    grad_wo = jnp.dot(context.T, grad_b, preferred_element_type=jnp.float32)
    grad_context = jnp.dot(grad_b, out_weight.T, preferred_element_type=jnp.float32).astype(
        jnp.bfloat16
    )
    dquery, row_lse, row_delta = query_side(
        query, keys_all, values_all, key_valid, grad_context, HEADS
    )
    query_all, grad_all = sent_together((query, grad_context), ("sy", "sx"), 0, 1)
    lse_all, delta_all = sent_together((row_lse, row_delta), ("sy", "sx"), 0, 1)
    dkey, dvalue = key_side(
        query_all, grad_all, lse_all, delta_all, keys, values, valid.reshape(-1), HEADS
    )
    dquery = dquery.astype(jnp.bfloat16)
    dkey = dkey.astype(jnp.bfloat16)
    dvalue = dvalue.astype(jnp.bfloat16)
    grad_wq = jnp.dot(normed.T, dquery, preferred_element_type=jnp.float32)
    grad_wk = jnp.dot(normed.T, dkey, preferred_element_type=jnp.float32)
    grad_wv = jnp.dot(normed.T, dvalue, preferred_element_type=jnp.float32)
    dnormed = jnp.dot(dquery, query_weight.T, preferred_element_type=jnp.float32)
    dnormed = dnormed + jnp.dot(dkey, key_weight.T, preferred_element_type=jnp.float32)
    dnormed = dnormed + jnp.dot(dvalue, value_weight.T, preferred_element_type=jnp.float32)
    dhidden = grad_b.astype(jnp.float32) + pullback(dnormed)[0]
    sig = jax.nn.sigmoid(pre)
    dpre = (valid_flat * dhidden * sig * (1.0 + pre * (1.0 - sig))).astype(jnp.bfloat16)
    grad_cv = jnp.dot(patches.T, dpre, preferred_element_type=jnp.float32)
    summed = (
        lax.psum_scatter(grad_cv, "dp", scatter_dimension=0, tiled=True),
        lax.psum_scatter(grad_wq, "dp", scatter_dimension=0, tiled=True),
        lax.psum_scatter(grad_wk, "dp", scatter_dimension=0, tiled=True),
        lax.psum_scatter(grad_wv, "dp", scatter_dimension=0, tiled=True),
        lax.psum_scatter(grad_wo, "dp", scatter_dimension=0, tiled=True),
    )
    summed = sent_together_2(
        (summed[0], summed[1], summed[2], summed[3], summed[4]), ("sy", "sx"), 1, 0
    )
    block_out = block.reshape(1, rows_dev, cols_dev, width)
    return (block_out, summed[0], summed[1], summed[2], summed[3], summed[4])


def solution(mesh):
    placed = (
        P("dp", "sy", "sx", None),
        P("dp"),
        P(),
        P(),
        P(),
        P(),
        P(),
        P(),
        P(),
        P("dp", "sy", "sx", None),
    )
    return jax.shard_map(
        body,
        mesh=mesh,
        in_specs=placed,
        out_specs=(
            P("dp", "sy", "sx", None),
            P("dp", ("sy", "sx")),
            P("dp", ("sy", "sx")),
            P("dp", ("sy", "sx")),
            P("dp", ("sy", "sx")),
            P("dp", ("sy", "sx")),
        ),
        check_vma=False,
    )
```

profile of v0, /device:TPU:0, one launch (start us, length us, event | category | flops | bytes accessed | tf_op | source)
XLA Modules:
  0.0 395.3 jit_solution(14760608367965485095)
XLA Ops:
  7.9 1.4 fusion.383
  11.8 5.3 %collective-permute-start = (bf16[1,16,640]{2,1,0:T(8,128)(2,1)S(1)}, bf16[1,16,640]{2,1,0:T(8,128)(2,1)S(1)}, u32[]{:S(2)}, u32[]{:S(2)}) collective-permute-start(bf16[1,16,640]{2,1,0:T(8,128)(2,1)S(1)} %get-tuple-element.48), channel_id=1, source_target_pairs={{0,2},{1,3},{4,6},{5,7},{8,10},{9,11},{12,14},{13,15},{16,18},{17,... | collective-permute-start | bytes 61448 | tf_op jit(solution)/shard_map/ppermute | solution.py:14
  18.8 5.5 %collective-permute-done.1 = bf16[1,16,640]{2,1,0:T(8,128)(2,1)S(1)} collective-permute-done((bf16[1,16,640]{2,1,0:T(8,128)(2,1)S(1)}, bf16[1,16,640]{2,1,0:T(8,128)(2,1)S(1)}, u32[]{:S(2)}, u32[]{:S(2)}) %collective-permute-start.1) | collective-permute-done | bytes 20512 | tf_op jit(solution)/shard_map/ppermute | solution.py:17
  24.3 2.6 collective-permute-start.2
  28.8 3.8 collective-permute-done.3
  33.8 5.3 %convert_reduce_fusion = (f32[128]{0:T(128)S(1)}, bf16[128,640]{1,0:T(8,128)(2,1)S(1)}, bf16[128,640]{1,0:T(8,128)(2,1)S(1)}, f32[128,640]{1,0:T(8,128)}) fusion(f32[128]{0:T(128)S(1)} %get-tuple-element.72, bf16[1,8,16,640]{3,2,1,0:T(8,128)(2,1)S(1)} %copy-done.7, f32[128]{0:T(128)S(1)} %get-tuple-element.38, bf16[1,8,16,640]{3,2,1,0:T(8,128)(2,1)S(1)} %copy-done.62, ...), kind=kOutput, calls=%fused_computation.202 | convolution fusion | flops 945028992 | bytes 9831936 | tf_op jit(solution)/shard_map/dot_general | solution.py:184
  43.9 1.6 convolution_convert_fusion.3
  46.9 19.7 %all-gather.3.cloned.1.call-done = bf16[512,1280]{1,0:T(8,128)(2,1)} async-done(((bf16[128,1280]{1,0:T(8,128)(2,1)}), bf16[512,1280]{1,0:T(8,128)(2,1)}) %all-gather.3.cloned.1.call-update) | async-done | bytes 1310736 | tf_op jit(solution)/shard_map/all_gather | solution.py:25
  66.6 1.4 fusion.451
  76.4 1.4 multiply_reduce_fusion
  77.8 1.5 multiply_reduce_fusion.1
  79.3 1.5 multiply_reduce_fusion.2
  80.8 1.4 multiply_reduce_fusion.3
  82.2 1.5 multiply_reduce_fusion.4
  83.7 1.4 multiply_reduce_fusion.5
  85.1 1.5 multiply_reduce_fusion.6
  86.6 1.4 multiply_reduce_fusion.7
  88.0 1.5 multiply_reduce_fusion.8
  89.5 1.4 multiply_reduce_fusion.9
  90.9 2.1 concatenate.60
  93.1 1.5 fusion.123
  94.6 1.4 fusion.122
  97.5 12.1 %all_gather.11 = f32[512,20]{0,1:T(8,128)S(1)} all-gather(f32[128,20]{0,1:T(8,128)S(1)} %concatenate.60), channel_id=1, replica_groups=mesh['dp'=32,'sy'=2,'sx'=2] {'sy','sx'}, dimensions={0}, use_global_device_ids=true | all-gather | bytes 51200 | tf_op jit(solution)/shard_map/all_gather | solution.py:25
  114.1 1.6 fusion.432
  125.6 1.7 fusion.428
  127.3 2.0 fusion.85
  129.4 2.1 fusion.87
  131.5 2.0 fusion.89
  133.5 2.1 fusion.91
  135.6 2.0 fusion.93
  137.7 2.1 fusion.95
  139.7 2.0 fusion.97
  141.8 2.1 fusion.99
  143.9 2.0 fusion.101
  145.9 2.1 fusion.103
  148.0 2.7 fusion.430
  155.9 1.6 fusion.453
  157.5 1.7 convolution_add_fusion.1
  160.2 7.7 %fusion.165 = f32[5760,640]{1,0:T(8,128)} fusion(bf16[128,5760]{1,0:T(8,128)(2,1)S(1)} %bitcast.102, f32[128,640]{1,0:T(8,128)S(1)} %copy-done.12, bf16[128,640]{1,0:T(8,128)(2,1)S(1)} %get-tuple-element.71, f32[128]{0:T(128)S(1)} %negate_multiply_fusion, f32[128]{0:T(128)S(1)} %get-tuple-element.38, bf16[128,640]{1,0:T(8,128)(2,1)S(1)} %get-tuple-element.37, ...), kind=kOutput, calls=%fused_computation.274 | convolution fusion | flops 945274880 | bytes 17205760 | tf_op jit(solution)/shard_map/dot_general | solution.py:224
  168.0 111.1 %fusion = f32[192,640]{1,0:T(8,128)S(1)} fusion(f32[5760,640]{1,0:T(8,128)} %fusion.165), kind=kCustom, calls=%all-reduce-scatter | all-reduce-scatter fusion | flops 3932161 | bytes 15237632
  279.0 1.3 collective-permute-start.4
  280.4 2.1 collective-permute-start.5
  284.4 10.6 %collective-permute-done.5 = f32[180,640]{1,0:T(8,128)} collective-permute-done((f32[180,640]{1,0:T(8,128)S(1)}, f32[180,640]{1,0:T(8,128)}, u32[]{:S(2)}, u32[]{:S(2)}) %collective-permute-start.5) | collective-permute-done | bytes 460832
  295.0 6.2 %concatenate.64 = f32[564,640]{1,0:T(8,128)} concatenate(f32[180,640]{1,0:T(8,128)} %collective-permute-done.5, f32[192,640]{1,0:T(8,128)S(1)} %collective-permute-done.4, f32[192,640]{1,0:T(8,128)S(1)} %fusion), dimensions={0} | concatenate | bytes 2887680
  302.2 57.8 %all-reduce.9.cloned.1.call-done = (f32[640,640]{1,0:T(8,128)}, f32[640,640]{1,0:T(8,128)}, f32[640,640]{1,0:T(8,128)}, f32[640,640]{1,0:T(8,128)}) async-done(((f32[640,640]{1,0:T(8,128)}, f32[640,640]{1,0:T(8,128)}, f32[640,640]{1,0:T(8,128)}, f32[640,640]{1,0:T(8,128)}), (f32[640,640]{1,0:T(8,128)}, f32[640,640]{1,0:T(8,128)}, f32[640,640]{1,0:T(8,128)}, ...) | async-done | bytes 6553616
  364.9 1.5 copy.20
  366.5 4.4 %all-to-all-start = ((f32[4,260,160]{1,2,0:T(8,128)}), f32[4,260,160]{1,2,0:T(8,128)S(1)}, u32[]{:S(2)}, u32[]{:S(2)}) async-start(f32[4,260,160]{1,2,0:T(8,128)} %copy.20), calls=%async_computation | async-start | bytes 1966080 | tf_op jit(solution)/shard_map/all_to_all | solution.py:37
  371.9 13.2 %all-to-all-done = f32[4,260,160]{1,2,0:T(8,128)S(1)} async-done(((f32[4,260,160]{1,2,0:T(8,128)}), f32[4,260,160]{1,2,0:T(8,128)S(1)}, u32[]{:S(2)}, u32[]{:S(2)}) %all-to-all-start) | async-done | bytes 665632 | tf_op jit(solution)/shard_map/all_to_all | solution.py:37
  (396 shorter events, 54.1 us)
Async XLA Ops:
  7.2 32.5 %copy-start = (bf16[640,640]{1,0:T(8,128)(2,1)S(1)}, bf16[640,640]{1,0:T(8,128)(2,1)}, u32[]{:S(2)}) copy-start(bf16[640,640]{1,0:T(8,128)(2,1)} %param.17) | copy-start | bytes 2457604
  7.2 59.5 %all-gather.3.cloned.1.call-start = ((), (), s32[]{:S(2)}) async-start(), calls=%async_computation.1 | async-start | bytes 1638400 | tf_op jit(solution)/shard_map/all_gather | solution.py:25
  11.7 21.2 %copy-start.6 = (bf16[1,8,16,640]{3,2,1,0:T(8,128)(2,1)S(1)}, bf16[1,8,16,640]{3,2,1,0:T(8,128)(2,1)}, u32[]{:S(2)}) copy-start(bf16[1,8,16,640]{3,2,1,0:T(8,128)(2,1)} %param.10) | copy-start | bytes 491524
  11.8 7.0 %collective-permute-start = (bf16[1,16,640]{2,1,0:T(8,128)(2,1)S(1)}, bf16[1,16,640]{2,1,0:T(8,128)(2,1)S(1)}, u32[]{:S(2)}, u32[]{:S(2)}) collective-permute-start(bf16[1,16,640]{2,1,0:T(8,128)(2,1)S(1)} %get-tuple-element.48), channel_id=1, source_target_pairs={{0,2},{1,3},{4,6},{5,7},{8,10},{9,11},{12,14},{13,15},{16,18},{17,... | collective-permute-start | bytes 61448 | tf_op jit(solution)/shard_map/ppermute | solution.py:14
  17.1 7.2 %collective-permute-start.1 = (bf16[1,16,640]{2,1,0:T(8,128)(2,1)S(1)}, bf16[1,16,640]{2,1,0:T(8,128)(2,1)S(1)}, u32[]{:S(2)}, u32[]{:S(2)}) collective-permute-start(bf16[1,16,640]{2,1,0:T(8,128)(2,1)S(1)} %get-tuple-element.49), channel_id=1, source_target_pairs={{2,0},{3,1},{6,4},{7,5},{10,8},{11,9},{14,12},{15,13},{18,16},{19,... | collective-permute-start | bytes 61448 | tf_op jit(solution)/shard_map/ppermute | solution.py:17
  24.3 4.5 %collective-permute-start.2 = (bf16[10,1,640]{2,1,0:T(2,128)(2,1)S(1)}, bf16[10,1,640]{2,1,0:T(2,128)(2,1)S(1)}, u32[]{:S(2)}, u32[]{:S(2)}) collective-permute-start(bf16[10,1,640]{2,1,0:T(2,128)(2,1)S(1)} %get-tuple-element.47), channel_id=1, source_target_pairs={{0,1},{2,3},{4,5},{6,7},{8,9},{10,11},{12,13},{14,15},{16,17},{18,... | collective-permute-start | bytes 38408 | tf_op jit(solution)/shard_map/ppermute | solution.py:14
  26.9 5.7 %collective-permute-start.3 = (bf16[10,1,640]{2,1,0:T(2,128)(2,1)S(1)}, bf16[10,1,640]{2,1,0:T(2,128)(2,1)S(1)}, u32[]{:S(2)}, u32[]{:S(2)}) collective-permute-start(bf16[10,1,640]{2,1,0:T(2,128)(2,1)S(1)} %get-tuple-element.46), channel_id=1, source_target_pairs={{1,0},{3,2},{5,4},{7,6},{9,8},{11,10},{13,12},{15,14},{17,16},{19,... | collective-permute-start | bytes 38408 | tf_op jit(solution)/shard_map/ppermute | solution.py:17
  41.8 74.0 %all-gather.5.cloned.1.call-start = ((), (), s32[]{:S(2)}) async-start(), calls=%async_computation.2 | async-start | bytes 1638400 | tf_op jit(solution)/shard_map/all_gather | solution.py:25
  46.9 313.2 %all-reduce.9.cloned.1.call-start = ((), (), s32[]{:S(2)}) async-start(), calls=%async_computation.3 | async-start | bytes 13107200
  68.0 8.3 %copy-start.13 = (f32[128,512]{1,0:T(8,128)}, f32[128,512]{1,0:T(8,128)S(1)}, u32[]{:S(2)}) copy-start(f32[128,512]{1,0:T(8,128)S(1)} %get-tuple-element.93) | copy-start | bytes 786436
  68.2 8.2 %copy-start.65 = (f32[128]{0:T(128)}, f32[128]{0:T(128)S(1)}, u32[]{:S(2)}) copy-start(f32[128]{0:T(128)S(1)} %fusion.164) | copy-start | bytes 1540
  69.4 8.4 %copy-start.16 = (f32[128,512]{1,0:T(8,128)}, f32[128,512]{1,0:T(8,128)S(1)}, u32[]{:S(2)}) copy-start(f32[128,512]{1,0:T(8,128)S(1)} %get-tuple-element.91) | copy-start | bytes 786436
  69.6 8.2 %copy-start.67 = (f32[128]{0:T(128)}, f32[128]{0:T(128)S(1)}, u32[]{:S(2)}) copy-start(f32[128]{0:T(128)S(1)} %fusion.162) | copy-start | bytes 1540
  70.9 8.4 %copy-start.19 = (f32[128,512]{1,0:T(8,128)}, f32[128,512]{1,0:T(8,128)S(1)}, u32[]{:S(2)}) copy-start(f32[128,512]{1,0:T(8,128)S(1)} %get-tuple-element.89) | copy-start | bytes 786436
  71.1 8.2 %copy-start.69 = (f32[128]{0:T(128)}, f32[128]{0:T(128)S(1)}, u32[]{:S(2)}) copy-start(f32[128]{0:T(128)S(1)} %fusion.160) | copy-start | bytes 1540
  71.4 9.4 %copy-start.22 = (f32[128,512]{1,0:T(8,128)}, f32[128,512]{1,0:T(8,128)S(1)}, u32[]{:S(2)}) copy-start(f32[128,512]{1,0:T(8,128)S(1)} %get-tuple-element.87) | copy-start | bytes 786436
  71.6 9.2 %copy-start.72 = (f32[128]{0:T(128)}, f32[128]{0:T(128)S(1)}, u32[]{:S(2)}) copy-start(f32[128]{0:T(128)S(1)} %fusion.158) | copy-start | bytes 1540
  72.0 10.2 %copy-start.25 = (f32[128,512]{1,0:T(8,128)}, f32[128,512]{1,0:T(8,128)S(1)}, u32[]{:S(2)}) copy-start(f32[128,512]{1,0:T(8,128)S(1)} %get-tuple-element.85) | copy-start | bytes 786436
  72.2 10.0 %copy-start.75 = (f32[128]{0:T(128)}, f32[128]{0:T(128)S(1)}, u32[]{:S(2)}) copy-start(f32[128]{0:T(128)S(1)} %fusion.156) | copy-start | bytes 1540
  72.5 11.2 %copy-start.28 = (f32[128,512]{1,0:T(8,128)}, f32[128,512]{1,0:T(8,128)S(1)}, u32[]{:S(2)}) copy-start(f32[128,512]{1,0:T(8,128)S(1)} %get-tuple-element.83) | copy-start | bytes 786436
  72.7 24.2 %copy-start.78 = (f32[128]{0:T(128)}, f32[128]{0:T(128)S(1)}, u32[]{:S(2)}) copy-start(f32[128]{0:T(128)S(1)} %fusion.154) | copy-start | bytes 1540
  73.6 11.6 %copy-start.31 = (f32[128,512]{1,0:T(8,128)}, f32[128,512]{1,0:T(8,128)S(1)}, u32[]{:S(2)}) copy-start(f32[128,512]{1,0:T(8,128)S(1)} %get-tuple-element.81) | copy-start | bytes 786436
  73.8 22.7 %copy-start.80 = (f32[128]{0:T(128)}, f32[128]{0:T(128)S(1)}, u32[]{:S(2)}) copy-start(f32[128]{0:T(128)S(1)} %fusion.152) | copy-start | bytes 1540
  74.0 12.6 %copy-start.34 = (f32[128,512]{1,0:T(8,128)}, f32[128,512]{1,0:T(8,128)S(1)}, u32[]{:S(2)}) copy-start(f32[128,512]{1,0:T(8,128)S(1)} %get-tuple-element.79) | copy-start | bytes 786436
  74.2 21.8 %copy-start.82 = (f32[128]{0:T(128)}, f32[128]{0:T(128)S(1)}, u32[]{:S(2)}) copy-start(f32[128]{0:T(128)S(1)} %fusion.150) | copy-start | bytes 1540
  75.1 12.9 %copy-start.37 = (f32[128,512]{1,0:T(8,128)}, f32[128,512]{1,0:T(8,128)S(1)}, u32[]{:S(2)}) copy-start(f32[128,512]{1,0:T(8,128)S(1)} %get-tuple-element.77) | copy-start | bytes 786436
  75.3 19.3 %copy-start.84 = (f32[128]{0:T(128)}, f32[128]{0:T(128)S(1)}, u32[]{:S(2)}) copy-start(f32[128]{0:T(128)S(1)} %fusion.148) | copy-start | bytes 1540
  75.6 13.9 %copy-start.39 = (f32[128,512]{1,0:T(8,128)}, f32[128,512]{1,0:T(8,128)S(1)}, u32[]{:S(2)}) copy-start(f32[128,512]{1,0:T(8,128)S(1)} %get-tuple-element.75) | copy-start | bytes 786436
  75.6 17.4 %copy-start.63 = (f32[128]{0:T(128)}, f32[128]{0:T(128)S(1)}, u32[]{:S(2)}) copy-start(f32[128]{0:T(128)S(1)} %get-tuple-element.74) | copy-start | bytes 1540
  75.8 17.2 %copy-start.86 = (f32[128]{0:T(128)}, f32[128]{0:T(128)S(1)}, u32[]{:S(2)}) copy-start(f32[128]{0:T(128)S(1)} %fusion.146) | copy-start | bytes 1540
  96.5 13.8 %copy-start.26 = (f32[128,512]{1,0:T(8,128)S(1)}, f32[128,512]{1,0:T(8,128)}, u32[]{:S(2)}) copy-start(f32[128,512]{1,0:T(8,128)} %copy-done.25) | copy-start | bytes 786436
  96.5 13.8 %copy-start.76 = (f32[128]{0:T(128)S(1)}, f32[128]{0:T(128)}, u32[]{:S(2)}) copy-start(f32[128]{0:T(128)} %copy-done.75) | copy-start | bytes 1540
  96.5 13.8 %copy-start.116 = (f32[128]{0:T(128)S(1)}, f32[128]{0:T(128)}, u32[]{:S(2)}) copy-start(f32[128]{0:T(128)} %get-tuple-element.104) | copy-start | bytes 1540
  96.5 13.8 %copy-start.126 = (f32[128,512]{1,0:T(8,128)S(1)}, f32[128,512]{1,0:T(8,128)}, u32[]{:S(2)}) copy-start(f32[128,512]{1,0:T(8,128)} %get-tuple-element.105) | copy-start | bytes 786436
  97.2 13.5 %copy-start.23 = (f32[128,512]{1,0:T(8,128)S(1)}, f32[128,512]{1,0:T(8,128)}, u32[]{:S(2)}) copy-start(f32[128,512]{1,0:T(8,128)} %copy-done.22) | copy-start | bytes 786436
  97.2 13.5 %copy-start.73 = (f32[128]{0:T(128)S(1)}, f32[128]{0:T(128)}, u32[]{:S(2)}) copy-start(f32[128]{0:T(128)} %copy-done.72) | copy-start | bytes 1540
  97.2 13.5 %copy-start.115 = (f32[128]{0:T(128)S(1)}, f32[128]{0:T(128)}, u32[]{:S(2)}) copy-start(f32[128]{0:T(128)} %get-tuple-element.106) | copy-start | bytes 1540
  97.2 13.5 %copy-start.125 = (f32[128,512]{1,0:T(8,128)S(1)}, f32[128,512]{1,0:T(8,128)}, u32[]{:S(2)}) copy-start(f32[128,512]{1,0:T(8,128)} %get-tuple-element.107) | copy-start | bytes 786436
  127.3 8.3 %copy-start.93 = (f32[512,1]{0,1:T(1,128)S(1)}, f32[512,1]{0,1:T(1,128)}, u32[]{:S(2)}) copy-start(f32[512,1]{0,1:T(1,128)} %get-tuple-element.60) | copy-start | bytes 6148
  129.4 8.3 %copy-start.92 = (f32[512,1]{0,1:T(1,128)S(1)}, f32[512,1]{0,1:T(1,128)}, u32[]{:S(2)}) copy-start(f32[512,1]{0,1:T(1,128)} %get-tuple-element.58) | copy-start | bytes 6148
  129.4 10.4 %copy-start.91 = (f32[512,1]{0,1:T(1,128)S(1)}, f32[512,1]{0,1:T(1,128)}, u32[]{:S(2)}) copy-start(f32[512,1]{0,1:T(1,128)} %get-tuple-element.56) | copy-start | bytes 6148
  131.5 10.3 %copy-start.90 = (f32[512,1]{0,1:T(1,128)S(1)}, f32[512,1]{0,1:T(1,128)}, u32[]{:S(2)}) copy-start(f32[512,1]{0,1:T(1,128)} %get-tuple-element.54) | copy-start | bytes 6148
  133.5 10.4 %copy-start.89 = (f32[512,1]{0,1:T(1,128)S(1)}, f32[512,1]{0,1:T(1,128)}, u32[]{:S(2)}) copy-start(f32[512,1]{0,1:T(1,128)} %get-tuple-element.52) | copy-start | bytes 6148
  135.6 10.3 %copy-start.88 = (f32[512,1]{0,1:T(1,128)S(1)}, f32[512,1]{0,1:T(1,128)}, u32[]{:S(2)}) copy-start(f32[512,1]{0,1:T(1,128)} %get-tuple-element.50) | copy-start | bytes 6148
  167.9 114.5 %copy-start.109 = (u32[128]{0:T(128)S(1)}, u32[128]{0:T(128)}, u32[]{:S(2)}) copy-start(u32[128]{0:T(128)} %constant.71) | copy-start | bytes 1540
  279.0 16.0 %collective-permute-start.4 = (f32[192,640]{1,0:T(8,128)S(1)}, f32[192,640]{1,0:T(8,128)S(1)}, u32[]{:S(2)}, u32[]{:S(2)}) collective-permute-start(f32[192,640]{1,0:T(8,128)S(1)} %fusion), channel_id=1, source_target_pairs={{0,4},{4,8},{8,12},{12,16},{16,20},{20,24},{24,28},{28,32},{32,36}... | collective-permute-start | bytes 1474568
  280.4 14.6 %collective-permute-start.5 = (f32[180,640]{1,0:T(8,128)S(1)}, f32[180,640]{1,0:T(8,128)}, u32[]{:S(2)}, u32[]{:S(2)}) collective-permute-start(f32[180,640]{1,0:T(8,128)S(1)} %slice.682), channel_id=1, source_target_pairs={{0,8},{4,12},{8,16},{12,20},{16,24},{20,28},{24,32},{28,36},{32,40... | collective-permute-start | bytes 1382408
  366.5 18.6 %all-to-all-start = ((f32[4,260,160]{1,2,0:T(8,128)}), f32[4,260,160]{1,2,0:T(8,128)S(1)}, u32[]{:S(2)}, u32[]{:S(2)}) async-start(f32[4,260,160]{1,2,0:T(8,128)} %copy.20), calls=%async_computation | async-start | bytes 1966080 | tf_op jit(solution)/shard_map/all_to_all | solution.py:37
  (93 other events, 206.8 us)
Sparse Core Ops, SparseCore 0:
  41.9 24.6 all-gather.2
  68.3 25.6 all-gather.4
  168.1 191.9 all-reduce.8
where the time goes:
time: 397 us; the launch traced here: 395 us
  blocking collectives  123 us (31%)
  waiting for transfers between devices  111 us (28%)
  matrix products  85.7 us (22%)
  local copies, waits for them, and re-layouts  28.2 us (7%)
  starting transfers between devices  18.4 us (5%)
  between operations  17.2 us (4%)
  other arithmetic  11.8 us (3%)
    unnamed x1, blocking collectives  111 us
    unnamed x6, waiting for transfers between devices  68.5 us
    unnamed x277, local copies, waits for them, and re-layouts  21.3 us
    dot_general x10, matrix products, key_side(): jnp.dot(dscore.T, query_all[:, start:start + width], preferred_element_ty...  20.6 us
    all_gather x2, waiting for transfers between devices, sent_together(): out = lax.all_gather(both, axis, axis=dim, tiled=True)  19.7 us
    dot_general x10, matrix products, query_side(): jnp.dot(grad_slice, values[:, start:start + width].T, preferred_element_t...  14.5 us
    all_to_all x1, waiting for transfers between devices, summed_on_arrival(): lax.all_to_all(cut_along(array, dim, count), axis, 0, 0, tiled=True)  13.2 us
    all_gather x1, blocking collectives, sent_together(): out = lax.all_gather(both, axis, axis=dim, tiled=True)  12.1 us
  transfers between devices with their start and end apart: 10, of which 6 were waited for; matrix products, arithmetic and copies ran while one was open for 41% of the time, Pallas kernels for 0%

commit v1 on v0

v1 whole, which is shorter than its diff:
```python
import jax
import jax.numpy as jnp
from jax import lax
from jax.experimental import pallas as pl
from jax.experimental.pallas import tpu as pltpu
from jax.sharding import PartitionSpec as P

HEADS = 10
EPS = 1e-05
ROWS, COLS, CH = 16, 32, 640
CELLS = ROWS * COLS
TILE_ROWS, TILE_COLS = 8, 16
WIDTH = CH // HEADS
PART = CH // 4
MAIN, REST = 128, 32
PIECES = 32
CONV_ROWS = 9 * CH // PIECES
QUARTER = CONV_ROWS // 4
PROJ_ROWS = CH // PIECES
AT_PROJ_REST = 4 * PROJ_ROWS
AT_CONV = 112
AT_CONV_REST = 304
PIECE = 352

f32 = jnp.float32
bf16 = jnp.bfloat16


def dot(a, b):
    return jnp.dot(a, b, preferred_element_type=f32)


def dot_t(a, b):
    return lax.dot_general(a, b, (((1,), (1,)), ((), ())), preferred_element_type=f32)


def iota(shape, dim):
    return lax.broadcasted_iota(jnp.int32, shape, dim)


def valid_rows(meta, start, count):
    cell = start + iota((count, 1), 0)
    return ((cell >> 5) < meta[0]) & ((cell & 31) < meta[1])


def tile_row(ref, r):
    base = (r >> 3) * (2 * TILE_ROWS * TILE_COLS) + (r & 7) * TILE_COLS
    left = ref[pl.ds(pl.multiple_of(base, 16), 16), :]
    right = ref[pl.ds(pl.multiple_of(base + TILE_ROWS * TILE_COLS, 16), 16), :]
    return jnp.concatenate([left, right], axis=0)


def front_kernel(
    meta, xg, conv_hbm, gain, wq_hbm, wk_hbm, wv_hbm,
    xin_o, pre_o, hid_o, nrm_o, q_o, k_o, v_o,
    taps, conv, proj, sems,
):
    third = 3 * CH
    copies = [
        pltpu.make_async_copy(
            conv_hbm.at[pl.ds(i * third, third)], conv.at[pl.ds(i * third, third)], sems.at[i]
        )
        for i in range(3)
    ]
    copies += [
        pltpu.make_async_copy(w, proj.at[i], sems.at[3 + i])
        for i, w in enumerate((wq_hbm, wk_hbm, wv_hbm))
    ]
    for copy in copies:
        copy.start()
    taps[0:COLS, :] = jnp.zeros((COLS, third), bf16)
    taps[CELLS + COLS :, :] = jnp.zeros((COLS, third), bf16)
    col = iota((COLS, 1), 0)

    def place(r, carry):
        x = tile_row(xg, r).astype(f32)
        x = jnp.where((r < meta[0]) & (col < meta[1]), x, 0.0)
        xb = x.astype(bf16)
        at = pl.multiple_of(r * COLS, COLS)
        xin_o[pl.ds(at, COLS), :] = xb
        to = pl.ds(at + COLS, COLS)
        taps[to, 0:CH] = jnp.where(col == 0, 0.0, pltpu.roll(x, 1, 0)).astype(bf16)
        taps[to, CH : 2 * CH] = xb
        taps[to, 2 * CH :] = jnp.where(col == COLS - 1, 0.0, pltpu.roll(x, COLS - 1, 0)).astype(bf16)
        return carry

    lax.fori_loop(0, ROWS, place, 0)
    for dy in range(3):
        copies[dy].wait()
        part = dot(taps[dy * COLS : dy * COLS + CELLS, :], conv[dy * third : (dy + 1) * third, :])
        if dy == 0:
            pre_o[...] = part
        else:
            pre_o[...] += part

    step = 64

    def norm(i, carry):
        at = pl.multiple_of(i * step, step)
        rows = pl.ds(at, step)
        pre = pre_o[rows, :]
        act = pre / (1.0 + jnp.exp(-pre))
        hid = jnp.where(valid_rows(meta, at, step), xin_o[rows, :].astype(f32) + act, 0.0)
        hid = hid.astype(bf16)
        hid_o[rows, :] = hid
        hid = hid.astype(f32)
        centred = hid - jnp.mean(hid, axis=1, keepdims=True)
        spread = jnp.mean(centred * centred, axis=1, keepdims=True)
        nrm_o[rows, :] = (centred * lax.rsqrt(spread + EPS) * gain[...]).astype(bf16)
        return carry

    lax.fori_loop(0, CELLS // step, norm, 0)
    for copy in copies[3:]:
        copy.wait()
    nrm = nrm_o[...]
    q_o[...] = (dot(nrm, proj[0]).astype(bf16).astype(f32) * (WIDTH**-0.5)).astype(bf16)
    k_o[...] = dot(nrm, proj[1]).astype(bf16)
    v_o[...] = dot(nrm, proj[2]).astype(bf16)


def back_kernel(
    meta, og, xin, hid, nrm, pre, q, k, v, gain, wq, wk, wv, wo,
    blk_o, mine_o, theirs_o,
    gb, gc, kt, vt, ctxt, dqt, dk, dv, bias, dn, dpre, wide, padm, padr, gmain, grest, gproj, stage, half,
):
    sy, sx, core = meta[2], meta[3], meta[4]
    col = iota((COLS, 1), 0)

    def place(r, carry):
        g = tile_row(og, r)
        g = jnp.where((r < meta[0]) & (col < meta[1]), g, jnp.zeros_like(g))
        gb[pl.ds(pl.multiple_of(r * COLS, COLS), COLS), :] = g
        return carry

    lax.fori_loop(0, ROWS, place, 0)
    gc[...] = dot_t(gb[...], wo[...]).astype(bf16)
    kt[...] = k[...].T
    vt[...] = v[...].T
    lane = iota((1, 2 * WIDTH), 1)
    ok = valid_rows(meta, 0, CELLS)
    for e in range(2):
        bias[e] = jnp.where((lane == WIDTH * (1 - e)) & ~ok, -1e30, 0.0).astype(bf16)
    block = 256

    def pair(hp, carry):
        lanes = pl.ds(pl.multiple_of(hp * 2 * WIDTH, 2 * WIDTH), 2 * WIDTH)
        k2 = k[:, lanes]
        v2 = v[:, lanes]
        dk2 = jnp.zeros((CELLS, 2 * WIDTH), f32)
        dv2 = jnp.zeros((CELLS, 2 * WIDTH), f32)
        for e in range(2):
            own = (lane >= WIDTH * e) & (lane < WIDTH * (e + 1))
            ka = jnp.where(own, k2, bias[e])
            rows = pl.ds(pl.multiple_of(hp * 2 * WIDTH + e * WIDTH, WIDTH), WIDTH)
            for qb in range(CELLS // block):
                cells = slice(qb * block, (qb + 1) * block)
                q2 = q[cells, lanes]
                g2 = gc[cells, lanes]
                qm = jnp.where(own, q2, jnp.zeros_like(q2))
                gm = jnp.where(own, g2, jnp.zeros_like(g2))
                one = jnp.where(lane == WIDTH * (1 - e), 1.0, 0.0).astype(bf16)
                qa = jnp.where(own, q2, one)
                s = dot_t(ka, qa)
                ex = jnp.exp(s - jnp.max(s, axis=0, keepdims=True))
                p = ex * (1.0 / jnp.sum(ex, axis=0, keepdims=True))
                pb = p.astype(bf16)
                ctxt[rows, cells] = dot(vt[rows, :], pb).astype(bf16)
                dp = dot_t(v2, gm)
                delta = jnp.sum(p * dp, axis=0, keepdims=True)
                ds = (p * (dp - delta)).astype(bf16)
                dqt[rows, cells] = (dot(kt[rows, :], ds) * (WIDTH**-0.5)).astype(bf16)
                dk2 = dk2 + dot(ds, qm)
                dv2 = dv2 + dot(pb, gm)
        dk[:, lanes] = dk2.astype(bf16)
        dv[:, lanes] = dv2.astype(bf16)
        return carry

    lax.fori_loop(0, HEADS // 2, pair, 0)

    part = CELLS // 2
    at = pl.multiple_of(sy * part, part)
    ctx_half = ctxt[:, pl.ds(at, part)].T
    half[...] = hid[pl.ds(at, part), :].astype(f32) + dot(ctx_half, wo[...])
    for r in range(TILE_ROWS):
        rows = half[pl.ds(pl.multiple_of(r * COLS + sx * TILE_COLS, 16), TILE_COLS), :]
        cells = sx * TILE_COLS + iota((TILE_COLS, 1), 0)
        keep = (sy * TILE_ROWS + r < meta[0]) & (cells < meta[1])
        blk_o[r * TILE_COLS : (r + 1) * TILE_COLS, :] = jnp.where(keep, rows, 0.0).astype(bf16)

    dq = dqt[...].T
    dn[...] = dot_t(dq, wq[...]) + dot_t(dk[...], wk[...]) + dot_t(dv[...], wv[...])
    step = 64

    def norm_back(i, carry):
        at = pl.multiple_of(i * step, step)
        rows = pl.ds(at, step)
        h = hid[rows, :].astype(f32)
        centred = h - jnp.mean(h, axis=1, keepdims=True)
        rstd = lax.rsqrt(jnp.mean(centred * centred, axis=1, keepdims=True) + EPS)
        xhat = centred * rstd
        dx = dn[rows, :] * gain[...]
        m1 = jnp.mean(dx, axis=1, keepdims=True)
        m2 = jnp.mean(dx * xhat, axis=1, keepdims=True)
        dh = gb[rows, :].astype(f32) + rstd * (dx - m1 - xhat * m2)
        a = pre[rows, :]
        sig = 1.0 / (1.0 + jnp.exp(-a))
        out = dh * sig * (1.0 + a * (1.0 - sig))
        dpre[rows, :] = jnp.where(valid_rows(meta, at, step), out, 0.0).astype(bf16)
        return carry

    lax.fori_loop(0, CELLS // step, norm_back, 0)

    first = (sy * 2 + sx) * PART
    row = iota((CH, 1), 0) - first

    def pick(lo, lanes, group=None):
        n = iota((1, lanes), 1)
        want = n + lo if group is None else (n & (REST - 1)) + lo
        hit = row == want
        if group is not None and group >= 0:
            hit = hit & ((n >> 5) == group)
        return jnp.where(hit, 1.0, 0.0).astype(bf16)

    nt = nrm[...].T
    main = pick(0, MAIN)
    grads = (dq, dk[...], dv[...], gb[...])
    mains, rests = [], []
    for w, g in enumerate(grads):
        both = dot(g, jnp.concatenate([main, pick(MAIN, 4 * REST, w)], axis=1))
        mains.append(both[:, :MAIN].astype(bf16))
        rests.append(both[:, MAIN:])
    qkv = dot(nt, jnp.concatenate(mains[:3] + [(rests[0] + rests[1] + rests[2]).astype(bf16)], axis=1))
    out = dot(ctxt[...], jnp.concatenate([mains[3], rests[3].astype(bf16)], axis=1))
    for w in range(3):
        gproj[w * CH : (w + 1) * CH, :] = qkv[:, w * MAIN : (w + 1) * MAIN]
    gproj[3 * CH : 4 * CH, :] = out[:, :MAIN]
    gproj[4 * CH :, :] = qkv[:, 3 * MAIN :] + out[:, MAIN:]

    ccol = iota((CELLS, 1), 0) & (COLS - 1)
    dmain = dot(dpre[...], main)
    drest = dot(dpre[...], pick(MAIN, 3 * MAIN, -1))
    up = lambda x: jnp.where(ccol == COLS - 1, 0.0, pltpu.roll(x, CELLS - 1, 0))
    down = lambda x: jnp.where(ccol == 0, 0.0, pltpu.roll(x, 1, 0))
    padm[...] = jnp.zeros_like(padm)
    padr[...] = jnp.zeros_like(padr)
    inner = slice(COLS, COLS + CELLS)
    padm[0, inner, :] = up(dmain).astype(bf16)
    padm[1, inner, :] = dmain.astype(bf16)
    padm[2, inner, :] = down(dmain).astype(bf16)
    tap = iota((1, 3 * MAIN), 1) >> 5
    tap_dx = tap % 3
    tap_dy = tap // 3
    padr[inner, :] = jnp.where(tap_dx == 0, up(drest), jnp.where(tap_dx == 1, drest, down(drest)))
    for t in range(9):
        lo = (2 - t // 3) * COLS
        wide[:, t * MAIN : (t + 1) * MAIN] = padm[t % 3, lo : lo + CELLS, :]
    wide[:, 9 * MAIN :] = jnp.where(
        tap_dy == 0,
        padr[2 * COLS :, :],
        jnp.where(tap_dy == 1, padr[inner, :], padr[0:CELLS, :]),
    ).astype(bf16)
    xt = xin[...].T
    for j in range(6):
        g = dot(xt, wide[:, j * 256 : (j + 1) * 256])
        for i in range(2):
            t = 2 * j + i
            val = g[:, i * MAIN : (i + 1) * MAIN]
            if t < 9:
                gmain[t * CH : (t + 1) * CH, :] = val
            else:
                for u in range(4):
                    n = (t - 9) * 4 + u
                    if n < 9:
                        grest[n * CH : (n + 1) * CH, 0:REST] = val[:, u * REST : (u + 1) * REST]

    stage[...] = jnp.zeros_like(stage)
    for j in range(PIECES // 2):
        for c in range(2):
            d = 2 * j + c
            for w in range(4):
                stage[c, w * PROJ_ROWS : (w + 1) * PROJ_ROWS, :] = gproj[
                    w * CH + d * PROJ_ROWS : w * CH + (d + 1) * PROJ_ROWS, :
                ]
            stage[c, AT_PROJ_REST : AT_PROJ_REST + PROJ_ROWS, :] = gproj[
                4 * CH + d * PROJ_ROWS : 4 * CH + (d + 1) * PROJ_ROWS, :
            ]
            stage[c, AT_CONV : AT_CONV + CONV_ROWS, :] = gmain[d * CONV_ROWS : (d + 1) * CONV_ROWS, :]
            stage[c, AT_CONV_REST : AT_CONV_REST + QUARTER, :] = jnp.concatenate(
                [
                    grest[d * CONV_ROWS + g * QUARTER : d * CONV_ROWS + (g + 1) * QUARTER, 0:REST]
                    for g in range(4)
                ],
                axis=1,
            )
        zero, one = stage[0], stage[1]
        mine_o[j] = jnp.where(core == 0, zero, one).astype(bf16)
        theirs_o[j] = jnp.where(core == 0, one, zero).astype(bf16)


def last_kernel(pieces, conv_o, q_o, k_o, v_o, o_o, total):
    acc = pieces[0].astype(f32)
    for j in range(1, pieces.shape[0]):
        acc = acc + pieces[j].astype(f32)
    total[...] = acc
    conv_o[:, :MAIN] = total[AT_CONV : AT_CONV + CONV_ROWS, :]
    for g in range(4):
        conv_o[g * QUARTER : (g + 1) * QUARTER, MAIN:] = total[
            AT_CONV_REST : AT_CONV_REST + QUARTER, g * REST : (g + 1) * REST
        ]
    for w, out in enumerate((q_o, k_o, v_o, o_o)):
        out[:, :MAIN] = total[w * PROJ_ROWS : (w + 1) * PROJ_ROWS, :]
        out[:, MAIN:] = total[AT_PROJ_REST : AT_PROJ_REST + PROJ_ROWS, w * REST : (w + 1) * REST]


VM = pl.BlockSpec(memory_space=pltpu.VMEM)
SM = pl.BlockSpec(memory_space=pltpu.SMEM)
AN = pl.BlockSpec(memory_space=pl.ANY)


def shape(dims, dtype):
    return jax.ShapeDtypeStruct(dims, dtype)


def front(meta, xg, conv_weight, gain, wq, wk, wv):
    flat = (CELLS, CH)
    return pl.pallas_call(
        front_kernel,
        name="front",
        out_shape=[shape(flat, bf16), shape(flat, f32)] + [shape(flat, bf16)] * 5,
        in_specs=[SM, VM, AN, VM, AN, AN, AN],
        out_specs=[VM] * 7,
        scratch_shapes=[
            pltpu.VMEM((CELLS + 2 * COLS, 3 * CH), bf16),
            pltpu.VMEM((9 * CH, CH), bf16),
            pltpu.VMEM((3, CH, CH), bf16),
            pltpu.SemaphoreType.DMA((6,)),
        ],
        compiler_params=pltpu.CompilerParams(vmem_limit_bytes=40 * 2**20),
    )(meta, xg, conv_weight, gain, wq, wk, wv)


def back(meta, og, xin, hid, nrm, pre, q, k, v, gain, wq, wk, wv, wo):
    flat, turned = (CELLS, CH), (CH, CELLS)
    return pl.pallas_call(
        back_kernel,
        name="back",
        out_shape=[
            shape((TILE_ROWS * TILE_COLS, CH), bf16),
            shape((PIECES // 2, PIECE, 128), bf16),
            shape((PIECES // 2, PIECE, 128), bf16),
        ],
        in_specs=[SM] + [VM] * 13,
        out_specs=[VM] * 3,
        scratch_shapes=[
            pltpu.VMEM(flat, bf16),
            pltpu.VMEM(flat, bf16),
            pltpu.VMEM(turned, bf16),
            pltpu.VMEM(turned, bf16),
            pltpu.VMEM(turned, bf16),
            pltpu.VMEM(turned, bf16),
            pltpu.VMEM(flat, bf16),
            pltpu.VMEM(flat, bf16),
            pltpu.VMEM((2, CELLS, 128), bf16),
            pltpu.VMEM(flat, f32),
            pltpu.VMEM(flat, bf16),
            pltpu.VMEM((CELLS, 12 * 128), bf16),
            pltpu.VMEM((3, CELLS + 2 * COLS, 128), bf16),
            pltpu.VMEM((CELLS + 2 * COLS, 3 * 128), f32),
            pltpu.VMEM((9 * CH, 128), f32),
            pltpu.VMEM((9 * CH, 128), f32),
            pltpu.VMEM((5 * CH, 128), f32),
            pltpu.VMEM((2, PIECE, 128), f32),
            pltpu.VMEM((CELLS // 2, CH), f32),
        ],
        compiler_params=pltpu.CompilerParams(vmem_limit_bytes=50 * 2**20),
    )(meta, og, xin, hid, nrm, pre, q, k, v, gain, wq, wk, wv, wo)


def last(pieces):
    small = shape((PROJ_ROWS, PART), f32)
    return pl.pallas_call(
        last_kernel,
        name="last",
        out_shape=[shape((CONV_ROWS, PART), f32), small, small, small, small],
        in_specs=[VM],
        out_specs=[VM] * 5,
        scratch_shapes=[pltpu.VMEM((PIECE, 128), f32)],
    )(pieces)


def body(
    features, bucket_ids, bucket_sizes, conv_weight, norm_gain,
    query_weight, key_weight, value_weight, out_weight, out_grad,
):
    chosen = jnp.arange(bucket_sizes.shape[0], dtype=jnp.int32) == bucket_ids[0]
    size = jnp.sum(jnp.where(chosen[:, None], bucket_sizes, 0), axis=0)
    core = lax.axis_index("dp") % 2
    meta = jnp.stack([size[0], size[1], lax.axis_index("sy"), lax.axis_index("sx"), core])
    meta = meta.astype(jnp.int32)
    gain = norm_gain.reshape(1, CH)
    tiles = ("sy", "sx")
    xg = lax.all_gather(features.reshape(-1, CH), tiles, axis=0, tiled=True)
    og = lax.all_gather(out_grad.reshape(-1, CH), tiles, axis=0, tiled=True)
    xin, pre, hid, nrm, q, k, v = front(
        meta, xg, conv_weight, gain, query_weight, key_weight, value_weight
    )
    block, mine, theirs = back(
        meta, og, xin, hid, nrm, pre, q, k, v, gain,
        query_weight, key_weight, value_weight, out_weight,
    )
    count = lax.axis_size("dp")
    other = lax.ppermute(theirs, "dp", [(i, i ^ 1) for i in range(count)])
    both = (mine.astype(f32) + other.astype(f32)).astype(bf16)
    groups = [[c + 2 * i for i in range(count // 2)] for c in range(2)]
    pieces = lax.all_to_all(both, "dp", 0, 0, tiled=True, axis_index_groups=groups)
    grads = last(pieces)
    return (block.reshape(features.shape), *grads)


def solution(mesh):
    tiles = P("dp", "sy", "sx", None)
    grad = P("dp", ("sy", "sx"))
    return jax.shard_map(
        body,
        mesh=mesh,
        in_specs=(tiles, P("dp"), P(), P(), P(), P(), P(), P(), P(), tiles),
        out_specs=(tiles, grad, grad, grad, grad, grad),
        check_vma=False,
    )
```

time: 397 us -> 122 us (0.31)
  waiting for transfers between devices: 111 us -> 3.43 us
  matrix products: 85.7 us -> 0 us
  blocking collectives: 123 us -> 57 us
  Pallas kernels: 0 us -> 51.7 us
  local copies, waits for them, and re-layouts: 28.2 us -> 5.45 us
  starting transfers between devices: 18.4 us -> 0.01 us
  between operations: 17.2 us -> 1.47 us
  other arithmetic: 11.8 us -> 2.03 us
    unnamed x1 -> x0, blocking collectives: 111 us -> none
    dot_general x84 -> x0, matrix products: 85.7 us -> none  [the longest x10 20.6 us: key_side(): jnp.dot(dscore.T, query_all[:, start:start + width], preferred_element_ty...]
    unnamed x6 -> x0, waiting for transfers between devices: 68.5 us -> none
    pallas_call x0 -> x3, Pallas kernels: none -> 51.7 us  [the longest x1 36.1 us: back(): pl.pallas_call(back_kernel, name='back', out_shape=[shape((TILE_ROWS * TI...]
    all_to_all x0 -> x1, blocking collectives: none -> 29.4 us  [body(): lax.all_to_all(both, 'dp', 0, 0, tiled=True, axis_index_groups=groups)]
    all_gather x2 -> x0, waiting for transfers between devices: 19.7 us -> none  [sent_together(): out = lax.all_gather(both, axis, axis=dim, tiled=True)]
    unnamed x277 -> x13, local copies, waits for them, and re-layouts: 21.3 us -> 4.76 us
    all_gather x1 -> x2, blocking collectives: 12.1 us -> 27.6 us  [the longest x1 13.8 us: body(): xg = lax.all_gather(features.reshape(-1, CH), tiles, axis=0, tiled=True)]
  transfers between devices with their start and end apart: 10 -> 1, of which waited for: 6 -> 1; matrix products, arithmetic and copies ran while one was open for 41% -> 0% of each run, Pallas kernels for 0% -> 0%
where the time goes in v1:
time: 122 us; the launch traced here: 121 us
  blocking collectives  57 us (47%)
  Pallas kernels  51.7 us (42%)
  local copies, waits for them, and re-layouts  5.45 us (4%)
  waiting for transfers between devices  3.43 us (3%)
  other arithmetic  2.03 us (2%)
  between operations  1.47 us (1%)
    pallas_call x1, Pallas kernels, back(): pl.pallas_call(back_kernel, name='back', out_shape=[shape((TILE_ROWS * TI...  36.1 us
    all_to_all x1, blocking collectives, body(): lax.all_to_all(both, 'dp', 0, 0, tiled=True, axis_index_groups=groups)  29.4 us
    all_gather x1, blocking collectives, body(): xg = lax.all_gather(features.reshape(-1, CH), tiles, axis=0, tiled=True)  13.8 us
    all_gather x1, blocking collectives, body(): og = lax.all_gather(out_grad.reshape(-1, CH), tiles, axis=0, tiled=True)  13.7 us
    pallas_call x1, Pallas kernels, front(): pl.pallas_call(front_kernel, name='front', out_shape=[shape(flat, bf16),...  13.3 us
    unnamed x13, local copies, waits for them, and re-layouts  4.76 us
    ppermute x1, waiting for transfers between devices, body(): other = lax.ppermute(theirs, 'dp', [(i, i ^ 1) for i in range(count)])  3.43 us
  transfers between devices with their start and end apart: 1, of which 1 were waited for; matrix products, arithmetic and copies ran while one was open for 0% of the time, Pallas kernels for 0%

profile of v1, /device:TPU:0, one launch (start us, length us, event | category | flops | bytes accessed | tf_op | source)
XLA Modules:
  0.0 121.1 jit_solution(10094839673552908710)
XLA Ops:
  0.6 0.0 copy-start.5
  0.6 0.0 copy-start.1
  0.7 0.0 copy-start
  1.5 0.7 reshape.30.gain
  2.1 13.8 %all_gather.7.xg = bf16[512,640]{1,0:T(8,128)(2,1)S(1)} all-gather(bf16[128,640]{1,0:T(8,128)(2,1)} %bitcast.8), channel_id=1, replica_groups=mesh['dp'=32,'sy'=2,'sx'=2] {'sy','sx'}, dimensions={0}, use_global_device_ids=true | all-gather | bytes 819200 | tf_op jit(solution)/shard_map/all_gather | solution.py:402
  16.0 13.7 %all_gather.6.og = bf16[512,640]{1,0:T(8,128)(2,1)S(1)} all-gather(bf16[128,640]{1,0:T(8,128)(2,1)} %bitcast.9), channel_id=1, replica_groups=mesh['dp'=32,'sy'=2,'sx'=2] {'sy','sx'}, dimensions={0}, use_global_device_ids=true | all-gather | bytes 819200 | tf_op jit(solution)/shard_map/all_gather | solution.py:403
  29.7 0.0 copy-done.5
  29.7 0.1 select_reduce_fusion
  29.8 0.1 pad_add_fusion.meta
  29.9 0.0 copy-done.1
  29.9 0.0 copy-done
  29.9 0.0 copy-start.2
  29.9 1.1 copy-done.2
  31.1 13.3 %front.1 = (bf16[512,640]{1,0:T(8,128)(2,1)S(1)}, f32[512,640]{1,0:T(8,128)S(1)}, bf16[512,640]{1,0:T(8,128)(2,1)S(1)}, bf16[512,640]{1,0:T(8,128)(2,1)S(1)}, bf...) custom-call(s32[5]{0:T(128)S(1)} %pad_add_fusion.meta, ...), custom_call_target="tpu_custom_call" | custom-call | tf_op jit(solution)/shard_map/front/pallas_call | solution.py:326
  44.4 0.0 copy-start.3
  44.4 1.1 copy-done.3
  45.5 0.0 copy-start.4
  45.5 0.8 copy-done.4
  46.3 36.1 %back.1 = (bf16[128,640]{1,0:T(8,128)(2,1)}, bf16[16,352,128]{2,1,0:T(8,128)(2,1)}, bf16[16,352,128]{2,1,0:T(8,128)(2,1)}) custom-call(s32[5]{0:T(128)S(1)} %pad_add_fusion.meta, bf16[512,640]{1,0:T(8,128)(2,1)S(1)} %all_gather.6.og, bf16[512,640]{1,0:T(8,128)(2,1)S(1)} %get-tuple-element.21.xin, bf16[512,640]{1,0:T(8,128)(2,1)S(1)} %get-tuple-element.22.hid, ...), custom_call_target="tpu_custom_call" | custom-call | tf_op jit(solution)/shard_map/back/pallas_call | solution.py:344
  82.4 0.0 collective-permute-start
  82.5 3.4 %collective-permute-done = bf16[16,352,128]{2,1,0:T(8,128)(2,1)S(1)} collective-permute-done((bf16[16,352,128]{2,1,0:T(8,128)(2,1)}, bf16[16,352,128]{2,1,0:T(8,128)(2,1)S(1)}, u32[]{:S(2)}, u32[]{:S(2)}) %collective-permute-start) | collective-permute-done | bytes 1441824 | tf_op jit(solution)/shard_map/ppermute | solution.py:412
  85.9 1.8 %add_convert_fusion = bf16[16,352,128]{2,1,0:T(8,128)(2,1)S(1)} fusion(bf16[16,352,128]{2,1,0:T(8,128)(2,1)S(1)} %collective-permute-done, bf16[16,352,128]{2,1,0:T(8,128)(2,1)} %get-tuple-element.29), kind=kLoop, calls=%fused_computation | loop fusion | flops 2883584 | bytes 4325376 | tf_op jit(solution)/shard_map/convert_element_type | solution.py:413
  87.7 29.4 %all_to_all.5.pieces = bf16[16,352,128]{2,1,0:T(8,128)(2,1)} all-to-all(bf16[16,352,128]{2,1,0:T(8,128)(2,1)S(1)} %add_convert_fusion), channel_id=1, replica_groups={{0,8,16,24,32,40,48,56,64,72,80,88,96,104,112,120},{4,12,20,28,36,44,52..., dimensions={0} | all-to-all | bytes 2883584 | tf_op jit(solution)/shard_map/all_to_all | solution.py:415
  117.1 2.2 %last.1 = (f32[180,160]{1,0:T(8,128)}, f32[20,160]{1,0:T(8,128)}, f32[20,160]{1,0:T(8,128)}, f32[20,160]{1,0:T(8,128)}, f32[20,160]{1,0:T(8,128)}) custom-call(bf16[16,352,128]{2,1,0:T(8,128)(2,1)} %all_to_all.5.pieces), custom_call_target="tpu_custom_call" | custom-call | tf_op jit(solution)/shard_map/last/pallas_call | solution.py:381
  119.4 1.7 %copy.16 = f32[180,160]{0,1:T(8,128)} copy(f32[180,160]{1,0:T(8,128)} %get-tuple-element.37) | data formatting | bytes 230400
  (1 shorter events, 0.0 us)
Async XLA Ops:
  0.6 29.1 %copy-start.5 = (s32[8,2]{0,1:T(2,128)S(1)}, s32[8,2]{0,1:T(2,128)}, u32[]{:S(2)}) copy-start(s32[8,2]{0,1:T(2,128)} %param.12) | copy-start | bytes 196
  0.6 29.3 %copy-start.1 = (bf16[640,640]{1,0:T(8,128)(2,1)S(1)}, bf16[640,640]{1,0:T(8,128)(2,1)}, u32[]{:S(2)}) copy-start(bf16[640,640]{1,0:T(8,128)(2,1)} %wk.1) | copy-start | bytes 2457604
  0.7 29.3 %copy-start = (bf16[640,640]{1,0:T(8,128)(2,1)S(1)}, bf16[640,640]{1,0:T(8,128)(2,1)}, u32[]{:S(2)}) copy-start(bf16[640,640]{1,0:T(8,128)(2,1)} %wq.1) | copy-start | bytes 2457604
  29.9 1.2 copy-start.2
  44.4 1.1 copy-start.3
  45.5 0.8 copy-start.4
  82.4 3.4 %collective-permute-start = (bf16[16,352,128]{2,1,0:T(8,128)(2,1)}, bf16[16,352,128]{2,1,0:T(8,128)(2,1)S(1)}, u32[]{:S(2)}, u32[]{:S(2)}) collective-permute-start(bf16[16,352,128]{2,1,0:T(8,128)(2,1)} %get-tuple-element.30), channel_id=1, source_target_pairs={{0,4},{4,0},{8,12},{12,8},{16,20},{20,16},{24,28},{28,24},{32,36},... | collective-permute-start | bytes 4325384 | tf_op jit(solution)/shard_map/ppermute | solution.py:412

commit v2 on v1

--- a/solution.py
+++ b/solution.py
@@ -7,6 +7,8 @@
 
 HEADS = 10
 EPS = 1e-05
+LOG2E = 1.4426950408889634
+SLOT = 64 + 16
 ROWS, COLS, CH = 16, 32, 640
 CELLS = ROWS * COLS
 TILE_ROWS, TILE_COLS = 8, 16
@@ -43,50 +45,37 @@
     return ((cell >> 5) < meta[0]) & ((cell & 31) < meta[1])
 
 
-def tile_row(ref, r):
-    base = (r >> 3) * (2 * TILE_ROWS * TILE_COLS) + (r & 7) * TILE_COLS
-    left = ref[pl.ds(pl.multiple_of(base, 16), 16), :]
-    right = ref[pl.ds(pl.multiple_of(base + TILE_ROWS * TILE_COLS, 16), 16), :]
-    return jnp.concatenate([left, right], axis=0)
+def place_tiles(meta, tiles, out):
+    edge = iota((TILE_COLS, 1), 0)
+    for shift, ref in enumerate(tiles):
+        tile = (meta[2] * 2 + meta[3] - shift) & 3
+        left = (tile & 1) * TILE_COLS
+        for r in range(TILE_ROWS):
+            row = (tile >> 1) * TILE_ROWS + r
+            x = ref[r * TILE_COLS : (r + 1) * TILE_COLS, :]
+            x = jnp.where((row < meta[0]) & (left + edge < meta[1]), x, jnp.zeros_like(x))
+            out[pl.ds(pl.multiple_of(row * COLS + left, TILE_COLS), TILE_COLS), :] = x
 
 
 def front_kernel(
-    meta, xg, conv_hbm, gain, wq_hbm, wk_hbm, wv_hbm,
+    meta, xg0, xg1, xg2, xg3, conv, gain, wq, wk, wv,
     xin_o, pre_o, hid_o, nrm_o, q_o, k_o, v_o,
-    taps, conv, proj, sems,
+    taps,
 ):
     third = 3 * CH
-    copies = [
-        pltpu.make_async_copy(
-            conv_hbm.at[pl.ds(i * third, third)], conv.at[pl.ds(i * third, third)], sems.at[i]
-        )
-        for i in range(3)
-    ]
-    copies += [
-        pltpu.make_async_copy(w, proj.at[i], sems.at[3 + i])
-        for i, w in enumerate((wq_hbm, wk_hbm, wv_hbm))
-    ]
-    for copy in copies:
-        copy.start()
     taps[0:COLS, :] = jnp.zeros((COLS, third), bf16)
     taps[CELLS + COLS :, :] = jnp.zeros((COLS, third), bf16)
     col = iota((COLS, 1), 0)
 
-    def place(r, carry):
-        x = tile_row(xg, r).astype(f32)
-        x = jnp.where((r < meta[0]) & (col < meta[1]), x, 0.0)
-        xb = x.astype(bf16)
-        at = pl.multiple_of(r * COLS, COLS)
-        xin_o[pl.ds(at, COLS), :] = xb
-        to = pl.ds(at + COLS, COLS)
+    place_tiles(meta, (xg0, xg1, xg2, xg3), xin_o)
+    for r in range(ROWS):
+        xb = xin_o[r * COLS : (r + 1) * COLS, :]
+        x = xb.astype(f32)
+        to = slice((r + 1) * COLS, (r + 2) * COLS)
         taps[to, 0:CH] = jnp.where(col == 0, 0.0, pltpu.roll(x, 1, 0)).astype(bf16)
         taps[to, CH : 2 * CH] = xb
         taps[to, 2 * CH :] = jnp.where(col == COLS - 1, 0.0, pltpu.roll(x, COLS - 1, 0)).astype(bf16)
-        return carry
-
-    lax.fori_loop(0, ROWS, place, 0)
     for dy in range(3):
-        copies[dy].wait()
         part = dot(taps[dy * COLS : dy * COLS + CELLS, :], conv[dy * third : (dy + 1) * third, :])
         if dy == 0:
             pre_o[...] = part
@@ -110,73 +99,88 @@
         return carry
 
     lax.fori_loop(0, CELLS // step, norm, 0)
-    for copy in copies[3:]:
-        copy.wait()
     nrm = nrm_o[...]
-    q_o[...] = (dot(nrm, proj[0]).astype(bf16).astype(f32) * (WIDTH**-0.5)).astype(bf16)
-    k_o[...] = dot(nrm, proj[1]).astype(bf16)
-    v_o[...] = dot(nrm, proj[2]).astype(bf16)
+    q_o[...] = (dot(nrm, wq[...]) * (WIDTH**-0.5 * LOG2E)).astype(bf16)
+    k_o[...] = dot(nrm, wk[...]).astype(bf16)
+    v_o[...] = dot(nrm, wv[...]).astype(bf16)
 
 
 def back_kernel(
-    meta, og, xin, hid, nrm, pre, q, k, v, gain, wq, wk, wv, wo,
+    meta, og0, og1, og2, og3, xin, hid, nrm, pre, q, k, v, gain, wq, wk, wv, wo,
     blk_o, mine_o, theirs_o,
-    gb, gc, kt, vt, ctxt, dqt, dk, dv, bias, dn, dpre, wide, padm, padr, gmain, grest, gproj, stage, half,
+    gb, gc, kt, vt, gt, ctxt, dqt, dk, dv, bias, dn, dpre, wide, padm, padr, gmain, grest, gproj, stage, half,
 ):
     sy, sx, core = meta[2], meta[3], meta[4]
     col = iota((COLS, 1), 0)
 
-    def place(r, carry):
-        g = tile_row(og, r)
-        g = jnp.where((r < meta[0]) & (col < meta[1]), g, jnp.zeros_like(g))
-        gb[pl.ds(pl.multiple_of(r * COLS, COLS), COLS), :] = g
-        return carry
-
-    lax.fori_loop(0, ROWS, place, 0)
+    place_tiles(meta, (og0, og1, og2, og3), gb)
     gc[...] = dot_t(gb[...], wo[...]).astype(bf16)
     kt[...] = k[...].T
-    vt[...] = v[...].T
+    gt[...] = gc[...].T
+    for h in range(HEADS):
+        vt[h * SLOT : h * SLOT + WIDTH, :] = v[:, h * WIDTH : (h + 1) * WIDTH].T
+        vt[h * SLOT + WIDTH : (h + 1) * SLOT, :] = jnp.ones((SLOT - WIDTH, CELLS), bf16)
     lane = iota((1, 2 * WIDTH), 1)
     ok = valid_rows(meta, 0, CELLS)
     for e in range(2):
         bias[e] = jnp.where((lane == WIDTH * (1 - e)) & ~ok, -1e30, 0.0).astype(bf16)
-    block = 256
-
-    def pair(hp, carry):
-        lanes = pl.ds(pl.multiple_of(hp * 2 * WIDTH, 2 * WIDTH), 2 * WIDTH)
-        k2 = k[:, lanes]
-        v2 = v[:, lanes]
-        dk2 = jnp.zeros((CELLS, 2 * WIDTH), f32)
-        dv2 = jnp.zeros((CELLS, 2 * WIDTH), f32)
-        for e in range(2):
-            own = (lane >= WIDTH * e) & (lane < WIDTH * (e + 1))
-            ka = jnp.where(own, k2, bias[e])
-            rows = pl.ds(pl.multiple_of(hp * 2 * WIDTH + e * WIDTH, WIDTH), WIDTH)
-            for qb in range(CELLS // block):
-                cells = slice(qb * block, (qb + 1) * block)
-                q2 = q[cells, lanes]
-                g2 = gc[cells, lanes]
-                qm = jnp.where(own, q2, jnp.zeros_like(q2))
-                gm = jnp.where(own, g2, jnp.zeros_like(g2))
-                one = jnp.where(lane == WIDTH * (1 - e), 1.0, 0.0).astype(bf16)
-                qa = jnp.where(own, q2, one)
-                s = dot_t(ka, qa)
-                ex = jnp.exp(s - jnp.max(s, axis=0, keepdims=True))
-                p = ex * (1.0 / jnp.sum(ex, axis=0, keepdims=True))
-                pb = p.astype(bf16)
-                ctxt[rows, cells] = dot(vt[rows, :], pb).astype(bf16)
-                dp = dot_t(v2, gm)
-                delta = jnp.sum(p * dp, axis=0, keepdims=True)
-                ds = (p * (dp - delta)).astype(bf16)
-                dqt[rows, cells] = (dot(kt[rows, :], ds) * (WIDTH**-0.5)).astype(bf16)
-                dk2 = dk2 + dot(ds, qm)
-                dv2 = dv2 + dot(pb, gm)
-        dk[:, lanes] = dk2.astype(bf16)
-        dv[:, lanes] = dv2.astype(bf16)
-        return carry
-
-    lax.fori_loop(0, HEADS // 2, pair, 0)
-
+
+    def stage_a(h):
+        lanes = slice(h // 2 * 2 * WIDTH, (h // 2 + 1) * 2 * WIDTH)
+        e = h % 2
+        own = (lane >= WIDTH * e) & (lane < WIDTH * (e + 1))
+        one = jnp.where(lane == WIDTH * (1 - e), 1.0, 0.0).astype(bf16)
+        zero = jnp.zeros((), bf16)
+        q2, g2 = q[:, lanes], gc[:, lanes]
+        s = dot_t(jnp.where(own, k[:, lanes], bias[e]), jnp.where(own, q2, one))
+        dp = dot_t(v[:, lanes], jnp.where(own, g2, zero))
+        return dict(h=h, s=s, dp=dp, qm=jnp.where(own, q2, zero), gm=jnp.where(own, g2, zero))
+
+    def stage_b(t):
+        s = t.pop("s")
+        t["ex"] = jnp.exp2(s - jnp.max(s, axis=0, keepdims=True))
+        t["eb"] = t["ex"].astype(bf16)
+
+    def stage_c(t):
+        h = t["h"]
+        rows = slice(h * WIDTH, (h + 1) * WIDTH)
+        ctx = dot(vt[h * SLOT : (h + 1) * SLOT, :], t["eb"])
+        inv = 1.0 / ctx[WIDTH : WIDTH + 1, :]
+        ctx = ctx[:WIDTH, :] * inv
+        ctxt[rows, :] = ctx.astype(bf16)
+        t["delta"] = jnp.sum(gt[rows, :].astype(f32) * ctx, axis=0, keepdims=True)
+        t["inv"] = inv
+
+    def stage_d(t):
+        t["ds"] = (t.pop("ex") * (t.pop("dp") - t.pop("delta"))).astype(bf16)
+
+    def stage_e(t):
+        h, ds, inv = t["h"], t.pop("ds"), t.pop("inv")
+        rows = slice(h * WIDTH, (h + 1) * WIDTH)
+        dqt[rows, :] = (dot(kt[rows, :], ds) * (inv * WIDTH**-0.5)).astype(bf16)
+        col = jnp.broadcast_to(inv, (8, CELLS)).T[:, 0:1]
+        t["dk"] = dot(ds, (t.pop("qm").astype(f32) * col).astype(bf16))
+        t["dv"] = dot(t.pop("eb"), (t.pop("gm").astype(f32) * col).astype(bf16))
+
+    def stage_f(t, u):
+        lanes = slice(t["h"] * WIDTH, (t["h"] + 2) * WIDTH)
+        dk[:, lanes] = ((t["dk"] + u["dk"]) * (1.0 / LOG2E)).astype(bf16)
+        dv[:, lanes] = (t["dv"] + u["dv"]).astype(bf16)
+
+
+    heads = [stage_a(0)]
+    for h in range(HEADS + 1):
+        if h + 1 < HEADS:
+            heads.append(stage_a(h + 1))
+        if h < HEADS:
+            stage_b(heads[h])
+        if h > 0:
+            stage_e(heads[h - 1])
+        if h < HEADS:
+            stage_c(heads[h])
+            stage_d(heads[h])
+        if h > 0 and h % 2 == 0:
+            stage_f(heads[h - 2], heads[h - 1])
     part = CELLS // 2
     at = pl.multiple_of(sy * part, part)
     ctx_half = ctxt[:, pl.ds(at, part)].T
@@ -302,11 +306,15 @@
     for j in range(1, pieces.shape[0]):
         acc = acc + pieces[j].astype(f32)
     total[...] = acc
-    conv_o[:, :MAIN] = total[AT_CONV : AT_CONV + CONV_ROWS, :]
-    for g in range(4):
-        conv_o[g * QUARTER : (g + 1) * QUARTER, MAIN:] = total[
-            AT_CONV_REST : AT_CONV_REST + QUARTER, g * REST : (g + 1) * REST
-        ]
+    conv_o[:MAIN, :] = total[AT_CONV : AT_CONV + CONV_ROWS, :].T
+    rest = jnp.concatenate(
+        [
+            total[AT_CONV_REST : AT_CONV_REST + QUARTER, g * REST : (g + 1) * REST]
+            for g in range(4)
+        ],
+        axis=0,
+    )
+    conv_o[MAIN:, :] = rest.T
     for w, out in enumerate((q_o, k_o, v_o, o_o)):
         out[:, :MAIN] = total[w * PROJ_ROWS : (w + 1) * PROJ_ROWS, :]
         out[:, MAIN:] = total[AT_PROJ_REST : AT_PROJ_REST + PROJ_ROWS, w * REST : (w + 1) * REST]
@@ -327,16 +335,13 @@
         front_kernel,
         name="front",
         out_shape=[shape(flat, bf16), shape(flat, f32)] + [shape(flat, bf16)] * 5,
-        in_specs=[SM, VM, AN, VM, AN, AN, AN],
+        in_specs=[SM] + [VM] * 9,
         out_specs=[VM] * 7,
         scratch_shapes=[
             pltpu.VMEM((CELLS + 2 * COLS, 3 * CH), bf16),
-            pltpu.VMEM((9 * CH, CH), bf16),
-            pltpu.VMEM((3, CH, CH), bf16),
-            pltpu.SemaphoreType.DMA((6,)),
         ],
-        compiler_params=pltpu.CompilerParams(vmem_limit_bytes=40 * 2**20),
-    )(meta, xg, conv_weight, gain, wq, wk, wv)
+        compiler_params=pltpu.CompilerParams(vmem_limit_bytes=24 * 2**20),
+    )(meta, *xg, conv_weight, gain, wq, wk, wv)
 
 
 def back(meta, og, xin, hid, nrm, pre, q, k, v, gain, wq, wk, wv, wo):
@@ -349,12 +354,13 @@
             shape((PIECES // 2, PIECE, 128), bf16),
             shape((PIECES // 2, PIECE, 128), bf16),
         ],
-        in_specs=[SM] + [VM] * 13,
+        in_specs=[SM] + [VM] * 16,
         out_specs=[VM] * 3,
         scratch_shapes=[
             pltpu.VMEM(flat, bf16),
             pltpu.VMEM(flat, bf16),
             pltpu.VMEM(turned, bf16),
+            pltpu.VMEM((HEADS * SLOT, CELLS), bf16),
             pltpu.VMEM(turned, bf16),
             pltpu.VMEM(turned, bf16),
             pltpu.VMEM(turned, bf16),
@@ -372,8 +378,8 @@
             pltpu.VMEM((2, PIECE, 128), f32),
             pltpu.VMEM((CELLS // 2, CH), f32),
         ],
-        compiler_params=pltpu.CompilerParams(vmem_limit_bytes=50 * 2**20),
-    )(meta, og, xin, hid, nrm, pre, q, k, v, gain, wq, wk, wv, wo)
+        compiler_params=pltpu.CompilerParams(vmem_limit_bytes=32 * 2**20),
+    )(meta, *og, xin, hid, nrm, pre, q, k, v, gain, wq, wk, wv, wo)
 
 
 def last(pieces):
@@ -381,11 +387,19 @@
     return pl.pallas_call(
         last_kernel,
         name="last",
-        out_shape=[shape((CONV_ROWS, PART), f32), small, small, small, small],
+        out_shape=[shape((PART, CONV_ROWS), f32), small, small, small, small],
         in_specs=[VM],
         out_specs=[VM] * 5,
         scratch_shapes=[pltpu.VMEM((PIECE, 128), f32)],
     )(pieces)
+
+
+def from_ring(own):
+    got = [
+        lax.ppermute(own, ("sy", "sx"), [(i, (i + shift) % 4) for i in range(4)])
+        for shift in (2, 1, 3)
+    ]
+    return own, got[1], got[0], got[2]
 
 
 def body(
@@ -398,9 +412,8 @@
     meta = jnp.stack([size[0], size[1], lax.axis_index("sy"), lax.axis_index("sx"), core])
     meta = meta.astype(jnp.int32)
     gain = norm_gain.reshape(1, CH)
-    tiles = ("sy", "sx")
-    xg = lax.all_gather(features.reshape(-1, CH), tiles, axis=0, tiled=True)
-    og = lax.all_gather(out_grad.reshape(-1, CH), tiles, axis=0, tiled=True)
+    xg = from_ring(features.reshape(-1, CH))
+    og = from_ring(out_grad.reshape(-1, CH))
     xin, pre, hid, nrm, q, k, v = front(
         meta, xg, conv_weight, gain, query_weight, key_weight, value_weight
     )
@@ -413,8 +426,8 @@
     both = (mine.astype(f32) + other.astype(f32)).astype(bf16)
     groups = [[c + 2 * i for i in range(count // 2)] for c in range(2)]
     pieces = lax.all_to_all(both, "dp", 0, 0, tiled=True, axis_index_groups=groups)
-    grads = last(pieces)
-    return (block.reshape(features.shape), *grads)
+    conv_t, *grads = last(pieces)
+    return (block.reshape(features.shape), conv_t.T, *grads)
 
 
 def solution(mesh):

time: 122 us -> 90.9 us (0.75)
  blocking collectives: 57 us -> 29.5 us
  Pallas kernels: 51.7 us -> 33.2 us
  starting transfers between devices: 0.01 us -> 8.73 us
  waiting for transfers between devices: 3.43 us -> 8.32 us
  local copies, waits for them, and re-layouts: 5.45 us -> 8.14 us
    all_gather x2 -> x0, blocking collectives: 27.6 us -> none  [the longest x1 13.8 us: body(): xg = lax.all_gather(features.reshape(-1, CH), tiles, axis=0, tiled=True)]
    pallas_call x1, Pallas kernels: 36.1 us -> 20.1 us  [back(): pl.pallas_call(back_kernel, name='back', out_shape=[shape((TILE_ROWS * TI...]
    ppermute x0 -> x6, starting transfers between devices: none -> 8.72 us  [from_ring(): lax.ppermute(own, ('sy', 'sx'), [(i, (i + shift) % 4) for i in range(4)])]
    ppermute x0 -> x6, waiting for transfers between devices: none -> 5.1 us  [from_ring(): lax.ppermute(own, ('sy', 'sx'), [(i, (i + shift) % 4) for i in range(4)])]
    unnamed x13 -> x16, local copies, waits for them, and re-layouts: 4.76 us -> 7.45 us
    pallas_call x1, Pallas kernels: 13.3 us -> 10.8 us  [front(): pl.pallas_call(front_kernel, name='front', out_shape=[shape(flat, bf16),...]
    convert_element_type x1, other arithmetic: 1.83 us -> 0.37 us  [body(): both = (mine.astype(f32) + other.astype(f32)).astype(bf16)]
  transfers between devices with their start and end apart: 1 -> 7, of which waited for: 1 -> 3; matrix products, arithmetic and copies ran while one was open for 0% -> 2% of each run, Pallas kernels for 0% -> 12%
where the time goes in v2:
time: 90.9 us; the launch traced here: 90.5 us
  Pallas kernels  33.2 us (37%)
  blocking collectives  29.5 us (32%)
  starting transfers between devices  8.73 us (10%)
  waiting for transfers between devices  8.32 us (9%)
  local copies, waits for them, and re-layouts  8.14 us (9%)
  between operations  1.36 us (1%)
  other arithmetic  1.25 us (1%)
    all_to_all x1, blocking collectives, body(): lax.all_to_all(both, 'dp', 0, 0, tiled=True, axis_index_groups=groups)  29.5 us
    pallas_call x1, Pallas kernels, back(): pl.pallas_call(back_kernel, name='back', out_shape=[shape((TILE_ROWS * TI...  20.1 us
    pallas_call x1, Pallas kernels, front(): pl.pallas_call(front_kernel, name='front', out_shape=[shape(flat, bf16),...  10.8 us
    ppermute x6, starting transfers between devices, from_ring(): lax.ppermute(own, ('sy', 'sx'), [(i, (i + shift) % 4) for i in range(4)])  8.72 us
    unnamed x16, local copies, waits for them, and re-layouts  7.45 us
    ppermute x6, waiting for transfers between devices, from_ring(): lax.ppermute(own, ('sy', 'sx'), [(i, (i + shift) % 4) for i in range(4)])  5.1 us
    ppermute x1, waiting for transfers between devices, body(): other = lax.ppermute(theirs, 'dp', [(i, i ^ 1) for i in range(count)])  3.22 us
    pallas_call x1, Pallas kernels, last(): pl.pallas_call(last_kernel, name='last', out_shape=[shape((PART, CONV_ROW...  2.26 us
  transfers between devices with their start and end apart: 7, of which 3 were waited for; matrix products, arithmetic and copies ran while one was open for 2% of the time, Pallas kernels for 12%

profile of v2, /device:TPU:0, one launch (start us, length us, event | category | flops | bytes accessed | tf_op | source)
XLA Modules:
  0.0 90.5 jit_solution(6166142638613806817)
XLA Ops:
  0.6 3.2 %collective-permute-start.5 = (bf16[128,640]{1,0:T(8,128)(2,1)}, bf16[128,640]{1,0:T(8,128)(2,1)S(1)}, u32[]{:S(2)}, u32[]{:S(2)}) collective-permute-start(bf16[128,640]{1,0:T(8,128)(2,1)} %bitcast.9), channel_id=1, source_target_pairs={{0,3},{1,0},{2,1},{3,2},{4,7},{5,4},{6,5},{7,6},{8,11},{9,8},{10,9... | collective-permute-start | bytes 491528 | tf_op jit(solution)/shard_map/ppermute | solution.py:399
  3.8 0.6 collective-permute-start.4
  4.4 1.0 %collective-permute-start.3 = (bf16[128,640]{1,0:T(8,128)(2,1)}, bf16[128,640]{1,0:T(8,128)(2,1)S(1)}, u32[]{:S(2)}, u32[]{:S(2)}) collective-permute-start(bf16[128,640]{1,0:T(8,128)(2,1)} %bitcast.11), channel_id=1, source_target_pairs={{0,1},{1,2},{2,3},{3,0},{4,5},{5,6},{6,7},{7,4},{8,9},{9,10},{10,1... | collective-permute-start | bytes 491528 | tf_op jit(solution)/shard_map/ppermute | solution.py:399
  5.4 2.3 %collective-permute-start.2 = (bf16[128,640]{1,0:T(8,128)(2,1)}, bf16[128,640]{1,0:T(8,128)(2,1)S(1)}, u32[]{:S(2)}, u32[]{:S(2)}) collective-permute-start(bf16[128,640]{1,0:T(8,128)(2,1)} %bitcast.13), channel_id=1, source_target_pairs={{0,3},{1,0},{2,1},{3,2},{4,7},{5,4},{6,5},{7,6},{8,11},{9,8},{10,9... | collective-permute-start | bytes 491528 | tf_op jit(solution)/shard_map/ppermute | solution.py:399
  7.7 1.7 %collective-permute-start.1 = (bf16[128,640]{1,0:T(8,128)(2,1)}, bf16[128,640]{1,0:T(8,128)(2,1)S(1)}, u32[]{:S(2)}, u32[]{:S(2)}) collective-permute-start(bf16[128,640]{1,0:T(8,128)(2,1)} %bitcast.14), channel_id=1, source_target_pairs={{0,2},{1,3},{2,0},{3,1},{4,6},{5,7},{6,4},{7,5},{8,10},{9,11},{10,... | collective-permute-start | bytes 491528 | tf_op jit(solution)/shard_map/ppermute | solution.py:399
  10.0 2.1 %collective-permute-done.5.xg3 = bf16[128,640]{1,0:T(8,128)(2,1)S(1)} collective-permute-done((bf16[128,640]{1,0:T(8,128)(2,1)}, bf16[128,640]{1,0:T(8,128)(2,1)S(1)}, u32[]{:S(2)}, u32[]{:S(2)}) %collective-permute-start.5) | collective-permute-done | bytes 163872 | tf_op jit(solution)/shard_map/ppermute | solution.py:399
  12.1 0.0 collective-permute-start
  12.1 0.8 select_reduce_fusion
  12.9 0.7 reshape.30.gain
  13.6 0.1 pad_add_fusion.meta
  13.7 0.0 collective-permute-done.4.xg2
  13.7 3.0 %collective-permute-done.3.xg1 = bf16[128,640]{1,0:T(8,128)(2,1)S(1)} collective-permute-done((bf16[128,640]{1,0:T(8,128)(2,1)}, bf16[128,640]{1,0:T(8,128)(2,1)S(1)}, u32[]{:S(2)}, u32[]{:S(2)}) %collective-permute-start.3) | collective-permute-done | bytes 163872 | tf_op jit(solution)/shard_map/ppermute | solution.py:399
  16.7 0.0 copy-start
  16.7 3.1 %copy-done = bf16[5760,640]{1,0:T(8,128)(2,1)S(1)} copy-done((bf16[5760,640]{1,0:T(8,128)(2,1)S(1)}, bf16[5760,640]{1,0:T(8,128)(2,1)}, u32[]{:S(2)}) %copy-start) | copy-done | bytes 7372824
  19.8 0.0 copy-start.1
  19.8 1.1 %copy-done.1 = bf16[640,640]{1,0:T(8,128)(2,1)S(1)} copy-done((bf16[640,640]{1,0:T(8,128)(2,1)S(1)}, bf16[640,640]{1,0:T(8,128)(2,1)}, u32[]{:S(2)}) %copy-start.1) | copy-done | bytes 819224
  20.9 0.0 copy-start.3
  20.9 1.1 %copy-done.3 = bf16[640,640]{1,0:T(8,128)(2,1)S(1)} copy-done((bf16[640,640]{1,0:T(8,128)(2,1)S(1)}, bf16[640,640]{1,0:T(8,128)(2,1)}, u32[]{:S(2)}) %copy-start.3) | copy-done | bytes 819224
  22.1 0.0 copy-start.4
  22.1 1.1 %copy-done.4 = bf16[640,640]{1,0:T(8,128)(2,1)S(1)} copy-done((bf16[640,640]{1,0:T(8,128)(2,1)S(1)}, bf16[640,640]{1,0:T(8,128)(2,1)}, u32[]{:S(2)}) %copy-start.4) | copy-done | bytes 819224
  23.2 0.0 copy-start.6
  23.2 0.9 %copy-done.6 = bf16[1,8,16,640]{3,2,1,0:T(8,128)(2,1)S(1)} copy-done((bf16[1,8,16,640]{3,2,1,0:T(8,128)(2,1)S(1)}, bf16[1,8,16,640]{3,2,1,0:T(8,128)(2,1)}, u32[]{:S(2)}) %copy-start.6) | copy-done | bytes 163864
  24.1 0.0 copy-start.2
  24.1 0.0 copy-start.5
  24.1 0.0 copy-start.7
  24.1 10.8 %front.1 = (bf16[512,640]{1,0:T(8,128)(2,1)S(1)}, f32[512,640]{1,0:T(8,128)S(1)}, bf16[512,640]{1,0:T(8,128)(2,1)S(1)}, bf16[512,640]{1,0:T(8,128)(2,1)S(1)}, bf...) custom-call(s32[5]{0:T(128)S(1)} %pad_add_fusion.meta, ...), custom_call_target="tpu_custom_call" | custom-call | tf_op jit(solution)/shard_map/front/pallas_call | solution.py:334
  35.0 0.0 collective-permute-done.2.og3
  35.0 0.0 collective-permute-done.1.og2
  35.0 0.0 collective-permute-done.og1
  35.0 0.0 copy-done.2
  35.0 0.0 copy-done.5
  35.0 0.0 copy-done.7
  35.1 20.1 %back.1 = (bf16[128,640]{1,0:T(8,128)(2,1)}, bf16[16,352,128]{2,1,0:T(8,128)(2,1)S(1)}, bf16[16,352,128]{2,1,0:T(8,128)(2,1)S(1)}) custom-call(s32[5]{0:T(128)S(1)} %pad_add_fusion.meta, bf16[128,640]{1,0:T(8,128)(2,1)S(1)} %bitcast.16, bf16[128,640]{1,0:T(8,128)(2,1)S(1)} %collective-permute-done.og1, bf16[128,640]{1,0:T(8,128)(2,1)S(1)} %collective-permute-done.1.og2, ...), custom_call_target="tpu_custom_call" | custom-call | tf_op jit(solution)/shard_map/back/pallas_call | solution.py:349
  55.2 0.0 collective-permute-start.6
  55.2 3.2 %collective-permute-done.6 = bf16[16,352,128]{2,1,0:T(8,128)(2,1)S(1)} collective-permute-done((bf16[16,352,128]{2,1,0:T(8,128)(2,1)S(1)}, bf16[16,352,128]{2,1,0:T(8,128)(2,1)S(1)}, u32[]{:S(2)}, u32[]{:S(2)}) %collective-permute-start.6) | collective-permute-done | bytes 1441824 | tf_op jit(solution)/shard_map/ppermute | solution.py:425
  58.4 0.4 add_convert_fusion
  58.8 29.5 %all_to_all.5.pieces = bf16[16,352,128]{2,1,0:T(8,128)(2,1)} all-to-all(bf16[16,352,128]{2,1,0:T(8,128)(2,1)S(1)} %add_convert_fusion), channel_id=1, replica_groups={{0,8,16,24,32,40,48,56,64,72,80,88,96,104,112,120},{4,12,20,28,36,44,52..., dimensions={0} | all-to-all | bytes 2883584 | tf_op jit(solution)/shard_map/all_to_all | solution.py:428
  88.2 2.3 %last.1 = (f32[160,180]{1,0:T(8,128)}, f32[20,160]{1,0:T(8,128)}, f32[20,160]{1,0:T(8,128)}, f32[20,160]{1,0:T(8,128)}, f32[20,160]{1,0:T(8,128)}) custom-call(bf16[16,352,128]{2,1,0:T(8,128)(2,1)} %all_to_all.5.pieces), custom_call_target="tpu_custom_call" | custom-call | tf_op jit(solution)/shard_map/last/pallas_call | solution.py:387
  (1 shorter events, 0.0 us)
Async XLA Ops:
  0.6 11.5 %collective-permute-start.5 = (bf16[128,640]{1,0:T(8,128)(2,1)}, bf16[128,640]{1,0:T(8,128)(2,1)S(1)}, u32[]{:S(2)}, u32[]{:S(2)}) collective-permute-start(bf16[128,640]{1,0:T(8,128)(2,1)} %bitcast.9), channel_id=1, source_target_pairs={{0,3},{1,0},{2,1},{3,2},{4,7},{5,4},{6,5},{7,6},{8,11},{9,8},{10,9... | collective-permute-start | bytes 491528 | tf_op jit(solution)/shard_map/ppermute | solution.py:399
  3.8 9.9 %collective-permute-start.4 = (bf16[128,640]{1,0:T(8,128)(2,1)}, bf16[128,640]{1,0:T(8,128)(2,1)S(1)}, u32[]{:S(2)}, u32[]{:S(2)}) collective-permute-start(bf16[128,640]{1,0:T(8,128)(2,1)} %bitcast.10), channel_id=1, source_target_pairs={{0,2},{1,3},{2,0},{3,1},{4,6},{5,7},{6,4},{7,5},{8,10},{9,11},{10,... | collective-permute-start | bytes 491528 | tf_op jit(solution)/shard_map/ppermute | solution.py:399
  4.4 12.3 %collective-permute-start.3 = (bf16[128,640]{1,0:T(8,128)(2,1)}, bf16[128,640]{1,0:T(8,128)(2,1)S(1)}, u32[]{:S(2)}, u32[]{:S(2)}) collective-permute-start(bf16[128,640]{1,0:T(8,128)(2,1)} %bitcast.11), channel_id=1, source_target_pairs={{0,1},{1,2},{2,3},{3,0},{4,5},{5,6},{6,7},{7,4},{8,9},{9,10},{10,1... | collective-permute-start | bytes 491528 | tf_op jit(solution)/shard_map/ppermute | solution.py:399
  5.4 29.6 %collective-permute-start.2 = (bf16[128,640]{1,0:T(8,128)(2,1)}, bf16[128,640]{1,0:T(8,128)(2,1)S(1)}, u32[]{:S(2)}, u32[]{:S(2)}) collective-permute-start(bf16[128,640]{1,0:T(8,128)(2,1)} %bitcast.13), channel_id=1, source_target_pairs={{0,3},{1,0},{2,1},{3,2},{4,7},{5,4},{6,5},{7,6},{8,11},{9,8},{10,9... | collective-permute-start | bytes 491528 | tf_op jit(solution)/shard_map/ppermute | solution.py:399
  7.7 27.3 %collective-permute-start.1 = (bf16[128,640]{1,0:T(8,128)(2,1)}, bf16[128,640]{1,0:T(8,128)(2,1)S(1)}, u32[]{:S(2)}, u32[]{:S(2)}) collective-permute-start(bf16[128,640]{1,0:T(8,128)(2,1)} %bitcast.14), channel_id=1, source_target_pairs={{0,2},{1,3},{2,0},{3,1},{4,6},{5,7},{6,4},{7,5},{8,10},{9,11},{10,... | collective-permute-start | bytes 491528 | tf_op jit(solution)/shard_map/ppermute | solution.py:399
  12.1 22.9 %collective-permute-start = (bf16[128,640]{1,0:T(8,128)(2,1)}, bf16[128,640]{1,0:T(8,128)(2,1)S(1)}, u32[]{:S(2)}, u32[]{:S(2)}) collective-permute-start(bf16[128,640]{1,0:T(8,128)(2,1)} %bitcast.15), channel_id=1, source_target_pairs={{0,1},{1,2},{2,3},{3,0},{4,5},{5,6},{6,7},{7,4},{8,9},{9,10},{10,1... | collective-permute-start | bytes 491528 | tf_op jit(solution)/shard_map/ppermute | solution.py:399
  16.7 3.1 %copy-start = (bf16[5760,640]{1,0:T(8,128)(2,1)S(1)}, bf16[5760,640]{1,0:T(8,128)(2,1)}, u32[]{:S(2)}) copy-start(bf16[5760,640]{1,0:T(8,128)(2,1)} %conv.1) | copy-start | bytes 22118404
  19.8 1.1 %copy-start.1 = (bf16[640,640]{1,0:T(8,128)(2,1)S(1)}, bf16[640,640]{1,0:T(8,128)(2,1)}, u32[]{:S(2)}) copy-start(bf16[640,640]{1,0:T(8,128)(2,1)} %wq.3) | copy-start | bytes 2457604
  20.9 1.1 %copy-start.3 = (bf16[640,640]{1,0:T(8,128)(2,1)S(1)}, bf16[640,640]{1,0:T(8,128)(2,1)}, u32[]{:S(2)}) copy-start(bf16[640,640]{1,0:T(8,128)(2,1)} %wk.3) | copy-start | bytes 2457604
  22.1 1.1 %copy-start.4 = (bf16[640,640]{1,0:T(8,128)(2,1)S(1)}, bf16[640,640]{1,0:T(8,128)(2,1)}, u32[]{:S(2)}) copy-start(bf16[640,640]{1,0:T(8,128)(2,1)} %wv.3) | copy-start | bytes 2457604
  23.2 0.9 %copy-start.6 = (bf16[1,8,16,640]{3,2,1,0:T(8,128)(2,1)S(1)}, bf16[1,8,16,640]{3,2,1,0:T(8,128)(2,1)}, u32[]{:S(2)}) copy-start(bf16[1,8,16,640]{3,2,1,0:T(8,128)(2,1)} %param.10) | copy-start | bytes 491524
  24.1 10.9 %copy-start.2 = (bf16[640,640]{1,0:T(8,128)(2,1)S(1)}, bf16[640,640]{1,0:T(8,128)(2,1)}, u32[]{:S(2)}) copy-start(bf16[640,640]{1,0:T(8,128)(2,1)} %wq.3) | copy-start | bytes 2457604
  24.1 10.9 %copy-start.5 = (bf16[640,640]{1,0:T(8,128)(2,1)S(1)}, bf16[640,640]{1,0:T(8,128)(2,1)}, u32[]{:S(2)}) copy-start(bf16[640,640]{1,0:T(8,128)(2,1)} %wo.1) | copy-start | bytes 2457604
  24.1 10.9 %copy-start.7 = (bf16[1,8,16,640]{3,2,1,0:T(8,128)(2,1)S(1)}, bf16[1,8,16,640]{3,2,1,0:T(8,128)(2,1)}, u32[]{:S(2)}) copy-start(bf16[1,8,16,640]{3,2,1,0:T(8,128)(2,1)} %param.19) | copy-start | bytes 491524
  55.2 3.2 %collective-permute-start.6 = (bf16[16,352,128]{2,1,0:T(8,128)(2,1)S(1)}, bf16[16,352,128]{2,1,0:T(8,128)(2,1)S(1)}, u32[]{:S(2)}, u32[]{:S(2)}) collective-permute-start(bf16[16,352,128]{2,1,0:T(8,128)(2,1)S(1)} %get-tuple-element.30), channel_id=1, source_target_pairs={{0,4},{4,0},{8,12},{12,8},{16,20},{20,16},{24,28},{28,24},{32,36},... | collective-permute-start | bytes 4325384 | tf_op jit(solution)/shard_map/ppermute | solution.py:425

commit v3 on v2

--- a/solution.py
+++ b/solution.py
@@ -58,11 +58,19 @@
 
 
 def front_kernel(
-    meta, xg0, xg1, xg2, xg3, conv, gain, wq, wk, wv,
+    meta, xg0, xg1, xg2, xg3, conv_hbm, gain, wq, wk, wv,
     xin_o, pre_o, hid_o, nrm_o, q_o, k_o, v_o,
-    taps,
+    taps, conv, sems,
 ):
     third = 3 * CH
+    copies = [
+        pltpu.make_async_copy(
+            conv_hbm.at[pl.ds(i * third, third)], conv.at[pl.ds(i * third, third)], sems.at[i]
+        )
+        for i in range(3)
+    ]
+    for copy in copies:
+        copy.start()
     taps[0:COLS, :] = jnp.zeros((COLS, third), bf16)
     taps[CELLS + COLS :, :] = jnp.zeros((COLS, third), bf16)
     col = iota((COLS, 1), 0)
@@ -76,6 +84,7 @@
         taps[to, CH : 2 * CH] = xb
         taps[to, 2 * CH :] = jnp.where(col == COLS - 1, 0.0, pltpu.roll(x, COLS - 1, 0)).astype(bf16)
     for dy in range(3):
+        copies[dy].wait()
         part = dot(taps[dy * COLS : dy * COLS + CELLS, :], conv[dy * third : (dy + 1) * third, :])
         if dy == 0:
             pre_o[...] = part
@@ -98,7 +107,7 @@
         nrm_o[rows, :] = (centred * lax.rsqrt(spread + EPS) * gain[...]).astype(bf16)
         return carry
 
-    lax.fori_loop(0, CELLS // step, norm, 0)
+    lax.fori_loop(0, CELLS // step, norm, 0, unroll=True)
     nrm = nrm_o[...]
     q_o[...] = (dot(nrm, wq[...]) * (WIDTH**-0.5 * LOG2E)).astype(bf16)
     k_o[...] = dot(nrm, wk[...]).astype(bf16)
@@ -107,10 +116,10 @@
 
 def back_kernel(
     meta, og0, og1, og2, og3, xin, hid, nrm, pre, q, k, v, gain, wq, wk, wv, wo,
-    blk_o, mine_o, theirs_o,
-    gb, gc, kt, vt, gt, ctxt, dqt, dk, dv, bias, dn, dpre, wide, padm, padr, gmain, grest, gproj, stage, half,
+    theirs_o, ctx_o, gproj, gmain, grest,
+    gb, gc, kt, vt, gt, ctxt, dqt, dk, dv, bias, dn, dpre, wide, padm, padr, stage,
 ):
-    sy, sx, core = meta[2], meta[3], meta[4]
+    sy, sx = meta[2], meta[3]
     col = iota((COLS, 1), 0)
 
     place_tiles(meta, (og0, og1, og2, og3), gb)
@@ -181,16 +190,7 @@
             stage_d(heads[h])
         if h > 0 and h % 2 == 0:
             stage_f(heads[h - 2], heads[h - 1])
-    part = CELLS // 2
-    at = pl.multiple_of(sy * part, part)
-    ctx_half = ctxt[:, pl.ds(at, part)].T
-    half[...] = hid[pl.ds(at, part), :].astype(f32) + dot(ctx_half, wo[...])
-    for r in range(TILE_ROWS):
-        rows = half[pl.ds(pl.multiple_of(r * COLS + sx * TILE_COLS, 16), TILE_COLS), :]
-        cells = sx * TILE_COLS + iota((TILE_COLS, 1), 0)
-        keep = (sy * TILE_ROWS + r < meta[0]) & (cells < meta[1])
-        blk_o[r * TILE_COLS : (r + 1) * TILE_COLS, :] = jnp.where(keep, rows, 0.0).astype(bf16)
-
+    ctx_o[...] = ctxt[:, pl.ds(pl.multiple_of(sy * (CELLS // 2), CELLS // 2), CELLS // 2)].T
     dq = dqt[...].T
     dn[...] = dot_t(dq, wq[...]) + dot_t(dk[...], wk[...]) + dot_t(dv[...], wv[...])
     step = 64
@@ -212,7 +212,7 @@
         dpre[rows, :] = jnp.where(valid_rows(meta, at, step), out, 0.0).astype(bf16)
         return carry
 
-    lax.fori_loop(0, CELLS // step, norm_back, 0)
+    lax.fori_loop(0, CELLS // step, norm_back, 0, unroll=True)
 
     first = (sy * 2 + sx) * PART
     row = iota((CH, 1), 0) - first
@@ -277,17 +277,18 @@
                     if n < 9:
                         grest[n * CH : (n + 1) * CH, 0:REST] = val[:, u * REST : (u + 1) * REST]
 
+    pack(meta, 1, gproj, gmain, grest, stage, theirs_o)
+
+
+def pack(meta, flip, gproj, gmain, grest, stage, out):
     stage[...] = jnp.zeros_like(stage)
     for j in range(PIECES // 2):
         for c in range(2):
             d = 2 * j + c
-            for w in range(4):
+            for w in range(5):
                 stage[c, w * PROJ_ROWS : (w + 1) * PROJ_ROWS, :] = gproj[
                     w * CH + d * PROJ_ROWS : w * CH + (d + 1) * PROJ_ROWS, :
                 ]
-            stage[c, AT_PROJ_REST : AT_PROJ_REST + PROJ_ROWS, :] = gproj[
-                4 * CH + d * PROJ_ROWS : 4 * CH + (d + 1) * PROJ_ROWS, :
-            ]
             stage[c, AT_CONV : AT_CONV + CONV_ROWS, :] = gmain[d * CONV_ROWS : (d + 1) * CONV_ROWS, :]
             stage[c, AT_CONV_REST : AT_CONV_REST + QUARTER, :] = jnp.concatenate(
                 [
@@ -296,9 +297,20 @@
                 ],
                 axis=1,
             )
-        zero, one = stage[0], stage[1]
-        mine_o[j] = jnp.where(core == 0, zero, one).astype(bf16)
-        theirs_o[j] = jnp.where(core == 0, one, zero).astype(bf16)
+        out[j] = jnp.where(meta[4] == flip, stage[0], stage[1]).astype(bf16)
+
+
+def rest_kernel(meta, ctx, hid, wo, gproj, gmain, grest, blk_o, mine_o, stage, half):
+    sy, sx = meta[2], meta[3]
+    part = CELLS // 2
+    at = pl.multiple_of(sy * part, part)
+    half[...] = hid[pl.ds(at, part), :].astype(f32) + dot(ctx[...], wo[...])
+    for r in range(TILE_ROWS):
+        rows = half[pl.ds(pl.multiple_of(r * COLS + sx * TILE_COLS, 16), TILE_COLS), :]
+        cells = sx * TILE_COLS + iota((TILE_COLS, 1), 0)
+        keep = (sy * TILE_ROWS + r < meta[0]) & (cells < meta[1])
+        blk_o[r * TILE_COLS : (r + 1) * TILE_COLS, :] = jnp.where(keep, rows, 0.0).astype(bf16)
+    pack(meta, 0, gproj, gmain, grest, stage, mine_o)
 
 
 def last_kernel(pieces, conv_o, q_o, k_o, v_o, o_o, total):
@@ -322,11 +334,34 @@
 
 VM = pl.BlockSpec(memory_space=pltpu.VMEM)
 SM = pl.BlockSpec(memory_space=pltpu.SMEM)
-AN = pl.BlockSpec(memory_space=pl.ANY)
+HB = pl.BlockSpec(memory_space=pltpu.HBM)
 
 
 def shape(dims, dtype):
     return jax.ShapeDtypeStruct(dims, dtype)
+
+
+def fetch_kernel(*refs):
+    count = (len(refs) - 1) // 2
+    copies = [
+        pltpu.make_async_copy(refs[i], refs[count + i], refs[-1].at[i]) for i in range(count)
+    ]
+    for copy in copies:
+        copy.start()
+    for copy in copies:
+        copy.wait()
+
+
+def fetch(*arrays):
+    return pl.pallas_call(
+        fetch_kernel,
+        name="fetch",
+        out_shape=[shape(a.shape, a.dtype) for a in arrays],
+        in_specs=[HB] * len(arrays),
+        out_specs=[VM] * len(arrays),
+        scratch_shapes=[pltpu.SemaphoreType.DMA((len(arrays),))],
+        compiler_params=pltpu.CompilerParams(vmem_limit_bytes=16 * 2**20),
+    )(*arrays)
 
 
 def front(meta, xg, conv_weight, gain, wq, wk, wv):
@@ -335,12 +370,14 @@
         front_kernel,
         name="front",
         out_shape=[shape(flat, bf16), shape(flat, f32)] + [shape(flat, bf16)] * 5,
-        in_specs=[SM] + [VM] * 9,
+        in_specs=[SM] + [VM] * 4 + [HB] + [VM] * 4,
         out_specs=[VM] * 7,
         scratch_shapes=[
             pltpu.VMEM((CELLS + 2 * COLS, 3 * CH), bf16),
+            pltpu.VMEM((9 * CH, CH), bf16),
+            pltpu.SemaphoreType.DMA((3,)),
         ],
-        compiler_params=pltpu.CompilerParams(vmem_limit_bytes=24 * 2**20),
+        compiler_params=pltpu.CompilerParams(vmem_limit_bytes=42 * 2**20),
     )(meta, *xg, conv_weight, gain, wq, wk, wv)
 
 
@@ -350,12 +387,14 @@
         back_kernel,
         name="back",
         out_shape=[
-            shape((TILE_ROWS * TILE_COLS, CH), bf16),
             shape((PIECES // 2, PIECE, 128), bf16),
-            shape((PIECES // 2, PIECE, 128), bf16),
+            shape((CELLS // 2, CH), bf16),
+            shape((5 * CH, 128), f32),
+            shape((9 * CH, 128), f32),
+            shape((9 * CH, 128), f32),
         ],
         in_specs=[SM] + [VM] * 16,
-        out_specs=[VM] * 3,
+        out_specs=[VM] * 5,
         scratch_shapes=[
             pltpu.VMEM(flat, bf16),
             pltpu.VMEM(flat, bf16),
@@ -372,14 +411,28 @@
             pltpu.VMEM((CELLS, 12 * 128), bf16),
             pltpu.VMEM((3, CELLS + 2 * COLS, 128), bf16),
             pltpu.VMEM((CELLS + 2 * COLS, 3 * 128), f32),
-            pltpu.VMEM((9 * CH, 128), f32),
-            pltpu.VMEM((9 * CH, 128), f32),
-            pltpu.VMEM((5 * CH, 128), f32),
+            pltpu.VMEM((2, PIECE, 128), f32),
+        ],
+        compiler_params=pltpu.CompilerParams(vmem_limit_bytes=32 * 2**20),
+    )(meta, *og, xin, hid, nrm, pre, q, k, v, gain, wq, wk, wv, wo)
+
+
+def rest(meta, ctx, hid, wo, gproj, gmain, grest):
+    return pl.pallas_call(
+        rest_kernel,
+        name="rest",
+        out_shape=[
+            shape((TILE_ROWS * TILE_COLS, CH), bf16),
+            shape((PIECES // 2, PIECE, 128), bf16),
+        ],
+        in_specs=[SM] + [VM] * 6,
+        out_specs=[VM] * 2,
+        scratch_shapes=[
             pltpu.VMEM((2, PIECE, 128), f32),
             pltpu.VMEM((CELLS // 2, CH), f32),
         ],
-        compiler_params=pltpu.CompilerParams(vmem_limit_bytes=32 * 2**20),
-    )(meta, *og, xin, hid, nrm, pre, q, k, v, gain, wq, wk, wv, wo)
+        compiler_params=pltpu.CompilerParams(vmem_limit_bytes=20 * 2**20),
+    )(meta, ctx, hid, wo, gproj, gmain, grest)
 
 
 def last(pieces):
@@ -394,12 +447,15 @@
     )(pieces)
 
 
-def from_ring(own):
-    got = [
-        lax.ppermute(own, ("sy", "sx"), [(i, (i + shift) % 4) for i in range(4)])
-        for shift in (2, 1, 3)
-    ]
-    return own, got[1], got[0], got[2]
+def from_ring(own, turn):
+    ring = ("sy", "sx")
+    ahead = lax.ppermute(own, ring, [(i, (i + 3) % 4) for i in range(4)])
+    if turn:
+        across = lax.ppermute(ahead, ring, [(i, (i + 3) % 4) for i in range(4)])
+    else:
+        across = lax.ppermute(own, ring, [(i, (i + 2) % 4) for i in range(4)])
+    behind = lax.ppermute(own, ring, [(i, (i + 1) % 4) for i in range(4)])
+    return behind, across, ahead
 
 
 def body(
@@ -412,17 +468,22 @@
     meta = jnp.stack([size[0], size[1], lax.axis_index("sy"), lax.axis_index("sx"), core])
     meta = meta.astype(jnp.int32)
     gain = norm_gain.reshape(1, CH)
-    xg = from_ring(features.reshape(-1, CH))
-    og = from_ring(out_grad.reshape(-1, CH))
+    x, g = features.reshape(-1, CH), out_grad.reshape(-1, CH)
+    query_weight, key_weight, value_weight, out_weight, x_near, g_near = fetch(
+        query_weight, key_weight, value_weight, out_weight, x, g
+    )
+    xg = (x_near, *from_ring(x, False))
+    og = (g_near, *from_ring(g, True))
     xin, pre, hid, nrm, q, k, v = front(
         meta, xg, conv_weight, gain, query_weight, key_weight, value_weight
     )
-    block, mine, theirs = back(
+    theirs, ctx, *grads = back(
         meta, og, xin, hid, nrm, pre, q, k, v, gain,
         query_weight, key_weight, value_weight, out_weight,
     )
     count = lax.axis_size("dp")
     other = lax.ppermute(theirs, "dp", [(i, i ^ 1) for i in range(count)])
+    block, mine = rest(meta, ctx, hid, out_weight, *grads)
     both = (mine.astype(f32) + other.astype(f32)).astype(bf16)
     groups = [[c + 2 * i for i in range(count // 2)] for c in range(2)]
     pieces = lax.all_to_all(both, "dp", 0, 0, tiled=True, axis_index_groups=groups)

time: 90.9 us -> 87.2 us (0.959)
  waiting for transfers between devices: 8.32 us -> 1.06 us
  starting transfers between devices: 8.73 us -> 11.3 us
  Pallas kernels: 33.2 us -> 35.4 us
  local copies, waits for them, and re-layouts: 8.14 us -> 7.1 us
    ppermute x6, waiting for transfers between devices: 5.1 us -> 0.05 us  [the longest x2 0.04 us: from_ring(): ahead = lax.ppermute(own, ring, [(i, (i + 3) % 4) for i in range(4)])]
    ppermute x6, starting transfers between devices: 8.72 us -> 11.2 us  [the longest x2 3.91 us: from_ring(): ahead = lax.ppermute(own, ring, [(i, (i + 3) % 4) for i in range(4)])]
    ppermute x1, waiting for transfers between devices: 3.22 us -> 1.01 us  [body(): other = lax.ppermute(theirs, 'dp', [(i, i ^ 1) for i in range(count)])]
    pallas_call x1 -> x3, Pallas kernels: 20.1 us -> 21.5 us  [the longest x1 18.3 us: back(): pl.pallas_call(back_kernel, name='back', out_shape=[shape((PIECES // 2, P...]
    unnamed x16 -> x12, local copies, waits for them, and re-layouts: 7.45 us -> 6.41 us
  transfers between devices with their start and end apart: 7 -> 7, of which waited for: 3 -> 1; matrix products, arithmetic and copies ran while one was open for 2% -> 2% of each run, Pallas kernels for 12% -> 17%
where the time goes in v3:
time: 87.2 us; the launch traced here: 86.7 us
  Pallas kernels  35.4 us (41%)
  blocking collectives  29.3 us (34%)
  starting transfers between devices  11.3 us (13%)
  local copies, waits for them, and re-layouts  7.1 us (8%)
  between operations  1.36 us (2%)
  other arithmetic  1.25 us (1%)
  waiting for transfers between devices  1.06 us (1%)
    all_to_all x1, blocking collectives, body(): lax.all_to_all(both, 'dp', 0, 0, tiled=True, axis_index_groups=groups)  29.3 us
    pallas_call x1, Pallas kernels, back(): pl.pallas_call(back_kernel, name='back', out_shape=[shape((PIECES // 2, P...  18.3 us
    pallas_call x1, Pallas kernels, front(): pl.pallas_call(front_kernel, name='front', out_shape=[shape(flat, bf16),...  11.6 us
    unnamed x12, local copies, waits for them, and re-layouts  6.41 us
    ppermute x2, starting transfers between devices, from_ring(): ahead = lax.ppermute(own, ring, [(i, (i + 3) % 4) for i in range(4)])  3.91 us
    ppermute x1, starting transfers between devices, from_ring(): across = lax.ppermute(ahead, ring, [(i, (i + 3) % 4) for i in range(4)])  3.77 us
    ppermute x2, starting transfers between devices, from_ring(): behind = lax.ppermute(own, ring, [(i, (i + 1) % 4) for i in range(4)])  3.24 us
    pallas_call x1, Pallas kernels, last(): pl.pallas_call(last_kernel, name='last', out_shape=[shape((PART, CONV_ROW...  2.26 us
  transfers between devices with their start and end apart: 7, of which 1 were waited for; matrix products, arithmetic and copies ran while one was open for 2% of the time, Pallas kernels for 17%

profile of v3, /device:TPU:0, one launch (start us, length us, event | category | flops | bytes accessed | tf_op | source)
XLA Modules:
  0.0 86.7 jit_solution(13016545253628473889)
XLA Ops:
  0.6 3.2 %collective-permute-start.1 = (bf16[128,640]{1,0:T(8,128)(2,1)}, bf16[128,640]{1,0:T(8,128)(2,1)S(1)}, u32[]{:S(2)}, u32[]{:S(2)}) collective-permute-start(bf16[128,640]{1,0:T(8,128)(2,1)} %bitcast.13), channel_id=1, source_target_pairs={{0,3},{1,0},{2,1},{3,2},{4,7},{5,4},{6,5},{7,6},{8,11},{9,8},{10,9... | collective-permute-start | bytes 491528 | tf_op jit(solution)/shard_map/ppermute | solution.py:452
  3.8 0.7 collective-permute-start.5
  4.5 0.3 collective-permute-start.4
  4.8 1.1 %collective-permute-start.3 = (bf16[128,640]{1,0:T(8,128)(2,1)}, bf16[128,640]{1,0:T(8,128)(2,1)S(1)}, u32[]{:S(2)}, u32[]{:S(2)}) collective-permute-start(bf16[128,640]{1,0:T(8,128)(2,1)} %bitcast.11), channel_id=1, source_target_pairs={{0,1},{1,2},{2,3},{3,0},{4,5},{5,6},{6,7},{7,4},{8,9},{9,10},{10,1... | collective-permute-start | bytes 491528 | tf_op jit(solution)/shard_map/ppermute | solution.py:457
  5.8 2.2 %collective-permute-start = (bf16[128,640]{1,0:T(8,128)(2,1)}, bf16[128,640]{1,0:T(8,128)(2,1)S(1)}, u32[]{:S(2)}, u32[]{:S(2)}) collective-permute-start(bf16[128,640]{1,0:T(8,128)(2,1)} %bitcast.14), channel_id=1, source_target_pairs={{0,1},{1,2},{2,3},{3,0},{4,5},{5,6},{6,7},{7,4},{8,9},{9,10},{10,1... | collective-permute-start | bytes 491528 | tf_op jit(solution)/shard_map/ppermute | solution.py:457
  8.7 0.0 collective-permute-done.1.og3
  8.7 3.8 %collective-permute-start.2 = (bf16[128,640]{1,0:T(8,128)(2,1)S(1)}, bf16[128,640]{1,0:T(8,128)(2,1)S(1)}, u32[]{:S(2)}, u32[]{:S(2)}) collective-permute-start(bf16[128,640]{1,0:T(8,128)(2,1)S(1)} %collective-permute-done.1.og3), channel_id=1, source_target_pairs={{0,3},{1,0},{2,1},{3,2},{4,7},{5,4},{6,5},{7,6},{8,11},{9,8},{10,9... | collective-permute-start | bytes 491528 | tf_op jit(solution)/shard_map/ppermute | solution.py:454
  12.5 0.8 select_reduce_fusion
  13.3 0.7 reshape.30.gain
  14.0 0.0 copy-start
  14.0 1.1 %copy-done = bf16[640,640]{1,0:T(8,128)(2,1)S(1)} copy-done((bf16[640,640]{1,0:T(8,128)(2,1)S(1)}, bf16[640,640]{1,0:T(8,128)(2,1)}, u32[]{:S(2)}) %copy-start) | copy-done | bytes 819224
  15.1 0.0 copy-start.1
  15.1 1.1 %copy-done.1 = bf16[640,640]{1,0:T(8,128)(2,1)S(1)} copy-done((bf16[640,640]{1,0:T(8,128)(2,1)S(1)}, bf16[640,640]{1,0:T(8,128)(2,1)}, u32[]{:S(2)}) %copy-start.1) | copy-done | bytes 819224
  16.3 0.0 copy-start.2
  16.3 1.1 %copy-done.2 = bf16[640,640]{1,0:T(8,128)(2,1)S(1)} copy-done((bf16[640,640]{1,0:T(8,128)(2,1)S(1)}, bf16[640,640]{1,0:T(8,128)(2,1)}, u32[]{:S(2)}) %copy-start.2) | copy-done | bytes 819224
  17.4 0.0 copy-start.3
  17.4 1.1 %copy-done.3 = bf16[640,640]{1,0:T(8,128)(2,1)S(1)} copy-done((bf16[640,640]{1,0:T(8,128)(2,1)S(1)}, bf16[640,640]{1,0:T(8,128)(2,1)}, u32[]{:S(2)}) %copy-start.3) | copy-done | bytes 819224
  18.6 0.0 copy-start.4
  18.6 0.9 %copy-done.4 = bf16[1,8,16,640]{3,2,1,0:T(8,128)(2,1)S(1)} copy-done((bf16[1,8,16,640]{3,2,1,0:T(8,128)(2,1)S(1)}, bf16[1,8,16,640]{3,2,1,0:T(8,128)(2,1)}, u32[]{:S(2)}) %copy-start.4) | copy-done | bytes 163864
  19.5 0.0 copy-start.5
  19.5 0.9 %copy-done.5 = bf16[1,8,16,640]{3,2,1,0:T(8,128)(2,1)S(1)} copy-done((bf16[1,8,16,640]{3,2,1,0:T(8,128)(2,1)S(1)}, bf16[1,8,16,640]{3,2,1,0:T(8,128)(2,1)}, u32[]{:S(2)}) %copy-start.5) | copy-done | bytes 163864
  20.4 1.0 %fetch.1 = (bf16[640,640]{1,0:T(8,128)(2,1)S(1)}, bf16[640,640]{1,0:T(8,128)(2,1)S(1)}, bf16[640,640]{1,0:T(8,128)(2,1)S(1)}, bf16[640,640]{1,0:T(8,128)(2,1)S(1...) custom-call(bf16[640,640]{1,0:T(8,128)(2,1)S(1)} %copy-done, bf16[640,640]{1,0:T(8,128)(2,1)S(1)} %copy-done.1, ...), custom_call_target="tpu_custom_call" | custom-call | tf_op jit(solution)/shard_map/fetch/pallas_call | solution.py:356
  21.5 0.1 pad_add_fusion.meta
  21.5 0.0 collective-permute-done.5.xg3
  21.5 0.0 collective-permute-done.4.xg2
  21.5 0.0 collective-permute-done.3.xg1
  21.5 11.6 %front.1 = (bf16[512,640]{1,0:T(8,128)(2,1)S(1)}, f32[512,640]{1,0:T(8,128)S(1)}, bf16[512,640]{1,0:T(8,128)(2,1)S(1)}, bf16[512,640]{1,0:T(8,128)(2,1)S(1)}, bf...) custom-call(s32[5]{0:T(128)S(1)} %pad_add_fusion.meta, ...), custom_call_target="tpu_custom_call" | custom-call | tf_op jit(solution)/shard_map/front/pallas_call | solution.py:369
  33.2 0.0 collective-permute-done.og1
  33.2 0.0 collective-permute-done.2.og2
  33.2 18.3 %back.1 = (bf16[16,352,128]{2,1,0:T(8,128)(2,1)S(1)}, bf16[256,640]{1,0:T(8,128)(2,1)S(1)}, f32[3200,128]{1,0:T(8,128)S(1)}, f32[5760,128]{1,0:T(8,128)S(1)}, f32[5760,128]{1,0:T(8,128)S(1)}) custom-call(s32[5]{0:T(128)S(1)} %pad_add_fusion.meta, bf16[128,640]{1,0:T(8,128)(2,1)S(1)} %get-tuple-element.31.og0, bf16[128,640]{1,0:T(8,128)(2,1)S(1)} %collective-permute-done.og1, ...), custom_call_target="tpu_custom_call" | custom-call | tf_op jit(solution)/shard_map/back/pallas_call | solution.py:386
  51.5 0.1 collective-permute-start.6
  51.6 2.2 %rest.1 = (bf16[128,640]{1,0:T(8,128)(2,1)}, bf16[16,352,128]{2,1,0:T(8,128)(2,1)S(1)}) custom-call(s32[5]{0:T(128)S(1)} %pad_add_fusion.meta, bf16[256,640]{1,0:T(8,128)(2,1)S(1)} %get-tuple-element.44.ctx, bf16[512,640]{1,0:T(8,128)(2,1)S(1)} %get-tuple-element.37.hid, bf16[640,640]{1,0:T(8,128)(2,1)S(1)} %get-tuple-element.43.wo, ...), custom_call_target="tpu_custom_call" | custom-call | tf_op jit(solution)/shard_map/rest/pallas_call | solution.py:421
  53.8 1.0 %collective-permute-done.6 = bf16[16,352,128]{2,1,0:T(8,128)(2,1)S(1)} collective-permute-done((bf16[16,352,128]{2,1,0:T(8,128)(2,1)S(1)}, bf16[16,352,128]{2,1,0:T(8,128)(2,1)S(1)}, u32[]{:S(2)}, u32[]{:S(2)}) %collective-permute-start.6) | collective-permute-done | bytes 1441824 | tf_op jit(solution)/shard_map/ppermute | solution.py:485
  54.8 0.4 add_convert_fusion
  55.2 29.3 %all_to_all.5.pieces = bf16[16,352,128]{2,1,0:T(8,128)(2,1)} all-to-all(bf16[16,352,128]{2,1,0:T(8,128)(2,1)S(1)} %add_convert_fusion), channel_id=1, replica_groups={{0,8,16,24,32,40,48,56,64,72,80,88,96,104,112,120},{4,12,20,28,36,44,52..., dimensions={0} | all-to-all | bytes 2883584 | tf_op jit(solution)/shard_map/all_to_all | solution.py:489
  84.5 2.3 %last.1 = (f32[160,180]{1,0:T(8,128)}, f32[20,160]{1,0:T(8,128)}, f32[20,160]{1,0:T(8,128)}, f32[20,160]{1,0:T(8,128)}, f32[20,160]{1,0:T(8,128)}) custom-call(bf16[16,352,128]{2,1,0:T(8,128)(2,1)} %all_to_all.5.pieces), custom_call_target="tpu_custom_call" | custom-call | tf_op jit(solution)/shard_map/last/pallas_call | solution.py:440
  (1 shorter events, 0.0 us)
Async XLA Ops:
  0.6 8.1 %collective-permute-start.1 = (bf16[128,640]{1,0:T(8,128)(2,1)}, bf16[128,640]{1,0:T(8,128)(2,1)S(1)}, u32[]{:S(2)}, u32[]{:S(2)}) collective-permute-start(bf16[128,640]{1,0:T(8,128)(2,1)} %bitcast.13), channel_id=1, source_target_pairs={{0,3},{1,0},{2,1},{3,2},{4,7},{5,4},{6,5},{7,6},{8,11},{9,8},{10,9... | collective-permute-start | bytes 491528 | tf_op jit(solution)/shard_map/ppermute | solution.py:452
  3.8 17.7 %collective-permute-start.5 = (bf16[128,640]{1,0:T(8,128)(2,1)}, bf16[128,640]{1,0:T(8,128)(2,1)S(1)}, u32[]{:S(2)}, u32[]{:S(2)}) collective-permute-start(bf16[128,640]{1,0:T(8,128)(2,1)} %bitcast.9), channel_id=1, source_target_pairs={{0,3},{1,0},{2,1},{3,2},{4,7},{5,4},{6,5},{7,6},{8,11},{9,8},{10,9... | collective-permute-start | bytes 491528 | tf_op jit(solution)/shard_map/ppermute | solution.py:452
  4.5 17.0 %collective-permute-start.4 = (bf16[128,640]{1,0:T(8,128)(2,1)}, bf16[128,640]{1,0:T(8,128)(2,1)S(1)}, u32[]{:S(2)}, u32[]{:S(2)}) collective-permute-start(bf16[128,640]{1,0:T(8,128)(2,1)} %bitcast.10), channel_id=1, source_target_pairs={{0,2},{1,3},{2,0},{3,1},{4,6},{5,7},{6,4},{7,5},{8,10},{9,11},{10,... | collective-permute-start | bytes 491528 | tf_op jit(solution)/shard_map/ppermute | solution.py:456
  4.8 16.7 %collective-permute-start.3 = (bf16[128,640]{1,0:T(8,128)(2,1)}, bf16[128,640]{1,0:T(8,128)(2,1)S(1)}, u32[]{:S(2)}, u32[]{:S(2)}) collective-permute-start(bf16[128,640]{1,0:T(8,128)(2,1)} %bitcast.11), channel_id=1, source_target_pairs={{0,1},{1,2},{2,3},{3,0},{4,5},{5,6},{6,7},{7,4},{8,9},{9,10},{10,1... | collective-permute-start | bytes 491528 | tf_op jit(solution)/shard_map/ppermute | solution.py:457
  5.8 27.4 %collective-permute-start = (bf16[128,640]{1,0:T(8,128)(2,1)}, bf16[128,640]{1,0:T(8,128)(2,1)S(1)}, u32[]{:S(2)}, u32[]{:S(2)}) collective-permute-start(bf16[128,640]{1,0:T(8,128)(2,1)} %bitcast.14), channel_id=1, source_target_pairs={{0,1},{1,2},{2,3},{3,0},{4,5},{5,6},{6,7},{7,4},{8,9},{9,10},{10,1... | collective-permute-start | bytes 491528 | tf_op jit(solution)/shard_map/ppermute | solution.py:457
  8.7 24.5 %collective-permute-start.2 = (bf16[128,640]{1,0:T(8,128)(2,1)S(1)}, bf16[128,640]{1,0:T(8,128)(2,1)S(1)}, u32[]{:S(2)}, u32[]{:S(2)}) collective-permute-start(bf16[128,640]{1,0:T(8,128)(2,1)S(1)} %collective-permute-done.1.og3), channel_id=1, source_target_pairs={{0,3},{1,0},{2,1},{3,2},{4,7},{5,4},{6,5},{7,6},{8,11},{9,8},{10,9... | collective-permute-start | bytes 491528 | tf_op jit(solution)/shard_map/ppermute | solution.py:454
  14.0 1.1 %copy-start = (bf16[640,640]{1,0:T(8,128)(2,1)S(1)}, bf16[640,640]{1,0:T(8,128)(2,1)}, u32[]{:S(2)}) copy-start(bf16[640,640]{1,0:T(8,128)(2,1)} %refs_0_.1) | copy-start | bytes 2457604
  15.1 1.1 %copy-start.1 = (bf16[640,640]{1,0:T(8,128)(2,1)S(1)}, bf16[640,640]{1,0:T(8,128)(2,1)}, u32[]{:S(2)}) copy-start(bf16[640,640]{1,0:T(8,128)(2,1)} %refs_1_.1) | copy-start | bytes 2457604
  16.3 1.1 %copy-start.2 = (bf16[640,640]{1,0:T(8,128)(2,1)S(1)}, bf16[640,640]{1,0:T(8,128)(2,1)}, u32[]{:S(2)}) copy-start(bf16[640,640]{1,0:T(8,128)(2,1)} %refs_2_.1) | copy-start | bytes 2457604
  17.4 1.1 %copy-start.3 = (bf16[640,640]{1,0:T(8,128)(2,1)S(1)}, bf16[640,640]{1,0:T(8,128)(2,1)}, u32[]{:S(2)}) copy-start(bf16[640,640]{1,0:T(8,128)(2,1)} %refs_3_.1) | copy-start | bytes 2457604
  18.6 0.9 %copy-start.4 = (bf16[1,8,16,640]{3,2,1,0:T(8,128)(2,1)S(1)}, bf16[1,8,16,640]{3,2,1,0:T(8,128)(2,1)}, u32[]{:S(2)}) copy-start(bf16[1,8,16,640]{3,2,1,0:T(8,128)(2,1)} %param.10) | copy-start | bytes 491524
  19.5 0.9 %copy-start.5 = (bf16[1,8,16,640]{3,2,1,0:T(8,128)(2,1)S(1)}, bf16[1,8,16,640]{3,2,1,0:T(8,128)(2,1)}, u32[]{:S(2)}) copy-start(bf16[1,8,16,640]{3,2,1,0:T(8,128)(2,1)} %param.19) | copy-start | bytes 491524
  51.5 3.3 %collective-permute-start.6 = (bf16[16,352,128]{2,1,0:T(8,128)(2,1)S(1)}, bf16[16,352,128]{2,1,0:T(8,128)(2,1)S(1)}, u32[]{:S(2)}, u32[]{:S(2)}) collective-permute-start(bf16[16,352,128]{2,1,0:T(8,128)(2,1)S(1)} %get-tuple-element.50), channel_id=1, source_target_pairs={{0,4},{4,0},{8,12},{12,8},{16,20},{20,16},{24,28},{28,24},{32,36},... | collective-permute-start | bytes 4325384 | tf_op jit(solution)/shard_map/ppermute | solution.py:485

commit v4 on v3

--- a/solution.py
+++ b/solution.py
@@ -40,6 +40,12 @@
     return lax.broadcasted_iota(jnp.int32, shape, dim)
 
 
+def place_of(bucket, sizes):
+    core = lax.axis_index("dp") & 1
+    b = bucket[0]
+    return sizes[b, 0], sizes[b, 1], lax.axis_index("sy"), lax.axis_index("sx"), core
+
+
 def valid_rows(meta, start, count):
     cell = start + iota((count, 1), 0)
     return ((cell >> 5) < meta[0]) & ((cell & 31) < meta[1])
@@ -58,10 +64,11 @@
 
 
 def front_kernel(
-    meta, xg0, xg1, xg2, xg3, conv_hbm, gain, wq, wk, wv,
-    xin_o, pre_o, hid_o, nrm_o, q_o, k_o, v_o,
+    bucket, sizes, xg0, xg1, xg2, xg3, conv_hbm, gain,
+    xin_o, pre_o, hid_o, nrm_o,
     taps, conv, sems,
 ):
+    meta = place_of(bucket, sizes)
     third = 3 * CH
     copies = [
         pltpu.make_async_copy(
@@ -108,21 +115,22 @@
         return carry
 
     lax.fori_loop(0, CELLS // step, norm, 0, unroll=True)
-    nrm = nrm_o[...]
-    q_o[...] = (dot(nrm, wq[...]) * (WIDTH**-0.5 * LOG2E)).astype(bf16)
-    k_o[...] = dot(nrm, wk[...]).astype(bf16)
-    v_o[...] = dot(nrm, wv[...]).astype(bf16)
 
 
 def back_kernel(
-    meta, og0, og1, og2, og3, xin, hid, nrm, pre, q, k, v, gain, wq, wk, wv, wo,
+    bucket, sizes, og0, og1, og2, og3, xin, hid, nrm, pre, gain, wq, wk, wv, wo,
     theirs_o, ctx_o, gproj, gmain, grest,
-    gb, gc, kt, vt, gt, ctxt, dqt, dk, dv, bias, dn, dpre, wide, padm, padr, stage,
+    q, k, v, gb, gc, kt, vt, gt, ctxt, dqt, dk, dv, bias, dn, dpre, wide, padm, padr, stage,
 ):
+    meta = place_of(bucket, sizes)
     sy, sx = meta[2], meta[3]
     col = iota((COLS, 1), 0)
 
     place_tiles(meta, (og0, og1, og2, og3), gb)
+    normed = nrm[...]
+    q[...] = (dot(normed, wq[...]) * (WIDTH**-0.5 * LOG2E)).astype(bf16)
+    k[...] = dot(normed, wk[...]).astype(bf16)
+    v[...] = dot(normed, wv[...]).astype(bf16)
     gc[...] = dot_t(gb[...], wo[...]).astype(bf16)
     kt[...] = k[...].T
     gt[...] = gc[...].T
@@ -300,7 +308,8 @@
         out[j] = jnp.where(meta[4] == flip, stage[0], stage[1]).astype(bf16)
 
 
-def rest_kernel(meta, ctx, hid, wo, gproj, gmain, grest, blk_o, mine_o, stage, half):
+def rest_kernel(bucket, sizes, ctx, hid, wo, gproj, gmain, grest, blk_o, mine_o, stage, half):
+    meta = place_of(bucket, sizes)
     sy, sx = meta[2], meta[3]
     part = CELLS // 2
     at = pl.multiple_of(sy * part, part)
@@ -341,47 +350,24 @@
     return jax.ShapeDtypeStruct(dims, dtype)
 
 
-def fetch_kernel(*refs):
-    count = (len(refs) - 1) // 2
-    copies = [
-        pltpu.make_async_copy(refs[i], refs[count + i], refs[-1].at[i]) for i in range(count)
-    ]
-    for copy in copies:
-        copy.start()
-    for copy in copies:
-        copy.wait()
-
-
-def fetch(*arrays):
-    return pl.pallas_call(
-        fetch_kernel,
-        name="fetch",
-        out_shape=[shape(a.shape, a.dtype) for a in arrays],
-        in_specs=[HB] * len(arrays),
-        out_specs=[VM] * len(arrays),
-        scratch_shapes=[pltpu.SemaphoreType.DMA((len(arrays),))],
-        compiler_params=pltpu.CompilerParams(vmem_limit_bytes=16 * 2**20),
-    )(*arrays)
-
-
-def front(meta, xg, conv_weight, gain, wq, wk, wv):
+def front(sizes, xg, conv_weight, gain):
     flat = (CELLS, CH)
     return pl.pallas_call(
         front_kernel,
         name="front",
-        out_shape=[shape(flat, bf16), shape(flat, f32)] + [shape(flat, bf16)] * 5,
-        in_specs=[SM] + [VM] * 4 + [HB] + [VM] * 4,
-        out_specs=[VM] * 7,
+        out_shape=[shape(flat, bf16), shape(flat, f32)] + [shape(flat, bf16)] * 2,
+        in_specs=[SM, SM] + [VM] * 4 + [HB, VM],
+        out_specs=[VM] * 4,
         scratch_shapes=[
             pltpu.VMEM((CELLS + 2 * COLS, 3 * CH), bf16),
             pltpu.VMEM((9 * CH, CH), bf16),
             pltpu.SemaphoreType.DMA((3,)),
         ],
-        compiler_params=pltpu.CompilerParams(vmem_limit_bytes=42 * 2**20),
-    )(meta, *xg, conv_weight, gain, wq, wk, wv)
-
-
-def back(meta, og, xin, hid, nrm, pre, q, k, v, gain, wq, wk, wv, wo):
+        compiler_params=pltpu.CompilerParams(vmem_limit_bytes=46 * 2**20),
+    )(*sizes, *xg, conv_weight, gain)
+
+
+def back(sizes, og, xin, hid, nrm, pre, gain, wq, wk, wv, wo):
     flat, turned = (CELLS, CH), (CH, CELLS)
     return pl.pallas_call(
         back_kernel,
@@ -393,9 +379,12 @@
             shape((9 * CH, 128), f32),
             shape((9 * CH, 128), f32),
         ],
-        in_specs=[SM] + [VM] * 16,
+        in_specs=[SM, SM] + [VM] * 13,
         out_specs=[VM] * 5,
         scratch_shapes=[
+            pltpu.VMEM(flat, bf16),
+            pltpu.VMEM(flat, bf16),
+            pltpu.VMEM(flat, bf16),
             pltpu.VMEM(flat, bf16),
             pltpu.VMEM(flat, bf16),
             pltpu.VMEM(turned, bf16),
@@ -414,10 +403,10 @@
             pltpu.VMEM((2, PIECE, 128), f32),
         ],
         compiler_params=pltpu.CompilerParams(vmem_limit_bytes=32 * 2**20),
-    )(meta, *og, xin, hid, nrm, pre, q, k, v, gain, wq, wk, wv, wo)
-
-
-def rest(meta, ctx, hid, wo, gproj, gmain, grest):
+    )(*sizes, *og, xin, hid, nrm, pre, gain, wq, wk, wv, wo)
+
+
+def rest(sizes, ctx, hid, wo, gproj, gmain, grest):
     return pl.pallas_call(
         rest_kernel,
         name="rest",
@@ -425,14 +414,14 @@
             shape((TILE_ROWS * TILE_COLS, CH), bf16),
             shape((PIECES // 2, PIECE, 128), bf16),
         ],
-        in_specs=[SM] + [VM] * 6,
+        in_specs=[SM, SM] + [VM] * 6,
         out_specs=[VM] * 2,
         scratch_shapes=[
             pltpu.VMEM((2, PIECE, 128), f32),
             pltpu.VMEM((CELLS // 2, CH), f32),
         ],
         compiler_params=pltpu.CompilerParams(vmem_limit_bytes=20 * 2**20),
-    )(meta, ctx, hid, wo, gproj, gmain, grest)
+    )(*sizes, ctx, hid, wo, gproj, gmain, grest)
 
 
 def last(pieces):
@@ -462,28 +451,18 @@
     features, bucket_ids, bucket_sizes, conv_weight, norm_gain,
     query_weight, key_weight, value_weight, out_weight, out_grad,
 ):
-    chosen = jnp.arange(bucket_sizes.shape[0], dtype=jnp.int32) == bucket_ids[0]
-    size = jnp.sum(jnp.where(chosen[:, None], bucket_sizes, 0), axis=0)
-    core = lax.axis_index("dp") % 2
-    meta = jnp.stack([size[0], size[1], lax.axis_index("sy"), lax.axis_index("sx"), core])
-    meta = meta.astype(jnp.int32)
+    sizes = (bucket_ids, bucket_sizes)
     gain = norm_gain.reshape(1, CH)
     x, g = features.reshape(-1, CH), out_grad.reshape(-1, CH)
-    query_weight, key_weight, value_weight, out_weight, x_near, g_near = fetch(
-        query_weight, key_weight, value_weight, out_weight, x, g
-    )
-    xg = (x_near, *from_ring(x, False))
-    og = (g_near, *from_ring(g, True))
-    xin, pre, hid, nrm, q, k, v = front(
-        meta, xg, conv_weight, gain, query_weight, key_weight, value_weight
-    )
+    xg = (x, *from_ring(x, False))
+    og = (g, *from_ring(g, True))
+    xin, pre, hid, nrm = front(sizes, xg, conv_weight, gain)
     theirs, ctx, *grads = back(
-        meta, og, xin, hid, nrm, pre, q, k, v, gain,
-        query_weight, key_weight, value_weight, out_weight,
+        sizes, og, xin, hid, nrm, pre, gain, query_weight, key_weight, value_weight, out_weight
     )
     count = lax.axis_size("dp")
     other = lax.ppermute(theirs, "dp", [(i, i ^ 1) for i in range(count)])
-    block, mine = rest(meta, ctx, hid, out_weight, *grads)
+    block, mine = rest(sizes, ctx, hid, out_weight, *grads)
     both = (mine.astype(f32) + other.astype(f32)).astype(bf16)
     groups = [[c + 2 * i for i in range(count // 2)] for c in range(2)]
     pieces = lax.all_to_all(both, "dp", 0, 0, tiled=True, axis_index_groups=groups)

time: 87.2 us -> 81.6 us (0.936)
  local copies, waits for them, and re-layouts: 7.1 us -> 2.38 us
  Pallas kernels: 35.4 us -> 33.3 us
  waiting for transfers between devices: 1.06 us -> 2.66 us
  other arithmetic: 1.25 us -> 0.37 us
    unnamed x12 -> x13, local copies, waits for them, and re-layouts: 6.41 us -> 1.69 us
    pallas_call x1, Pallas kernels: 11.6 us -> 8.87 us  [front(): pl.pallas_call(front_kernel, name='front', out_shape=[shape(flat, bf16),...]
    ppermute x2, waiting for transfers between devices: 0.04 us -> 1.83 us  [from_ring(): ahead = lax.ppermute(own, ring, [(i, (i + 3) % 4) for i in range(4)])]
    pallas_call x1, Pallas kernels: 18.3 us -> 19.8 us  [back(): pl.pallas_call(back_kernel, name='back', out_shape=[shape((PIECES // 2, P...]
    pallas_call x1 -> x0, Pallas kernels: 1.04 us -> none  [fetch(): pl.pallas_call(fetch_kernel, name='fetch', out_shape=[shape(a.shape, a.dt...]
  transfers between devices with their start and end apart: 7 -> 7, of which waited for: 1 -> 3; matrix products, arithmetic and copies ran while one was open for 2% -> 2% of each run, Pallas kernels for 17% -> 14%
where the time goes in v4:
time: 81.6 us; the launch traced here: 80.8 us
  Pallas kernels  33.3 us (41%)
  blocking collectives  29.5 us (36%)
  starting transfers between devices  11.3 us (14%)
  waiting for transfers between devices  2.66 us (3%)
  local copies, waits for them, and re-layouts  2.38 us (3%)
  between operations  1.37 us (2%)
    all_to_all x1, blocking collectives, body(): lax.all_to_all(both, 'dp', 0, 0, tiled=True, axis_index_groups=groups)  29.5 us
    pallas_call x1, Pallas kernels, back(): pl.pallas_call(back_kernel, name='back', out_shape=[shape((PIECES // 2, P...  19.8 us
    pallas_call x1, Pallas kernels, front(): pl.pallas_call(front_kernel, name='front', out_shape=[shape(flat, bf16),...  8.87 us
    ppermute x2, starting transfers between devices, from_ring(): ahead = lax.ppermute(own, ring, [(i, (i + 3) % 4) for i in range(4)])  3.91 us
    ppermute x1, starting transfers between devices, from_ring(): across = lax.ppermute(ahead, ring, [(i, (i + 3) % 4) for i in range(4)])  3.77 us
    ppermute x2, starting transfers between devices, from_ring(): behind = lax.ppermute(own, ring, [(i, (i + 1) % 4) for i in range(4)])  3.24 us
    pallas_call x1, Pallas kernels, rest(): pl.pallas_call(rest_kernel, name='rest', out_shape=[shape((TILE_ROWS * TI...  2.38 us
    pallas_call x1, Pallas kernels, last(): pl.pallas_call(last_kernel, name='last', out_shape=[shape((PART, CONV_ROW...  2.26 us
  transfers between devices with their start and end apart: 7, of which 3 were waited for; matrix products, arithmetic and copies ran while one was open for 2% of the time, Pallas kernels for 14%

profile of v4, /device:TPU:0, one launch (start us, length us, event | category | flops | bytes accessed | tf_op | source)
XLA Modules:
  0.0 80.8 jit_solution(6080151877431861992)
XLA Ops:
  0.6 3.2 %collective-permute-start.1 = (bf16[128,640]{1,0:T(8,128)(2,1)}, bf16[128,640]{1,0:T(8,128)(2,1)S(1)}, u32[]{:S(2)}, u32[]{:S(2)}) collective-permute-start(bf16[128,640]{1,0:T(8,128)(2,1)} %bitcast.8), channel_id=1, source_target_pairs={{0,3},{1,0},{2,1},{3,2},{4,7},{5,4},{6,5},{7,6},{8,11},{9,8},{10,9... | collective-permute-start | bytes 491528 | tf_op jit(solution)/shard_map/ppermute | solution.py:441
  3.8 0.7 collective-permute-start.5
  4.5 0.3 collective-permute-start.4
  4.8 1.1 %collective-permute-start.3 = (bf16[128,640]{1,0:T(8,128)(2,1)}, bf16[128,640]{1,0:T(8,128)(2,1)S(1)}, u32[]{:S(2)}, u32[]{:S(2)}) collective-permute-start(bf16[128,640]{1,0:T(8,128)(2,1)} %bitcast.6), channel_id=1, source_target_pairs={{0,1},{1,2},{2,3},{3,0},{4,5},{5,6},{6,7},{7,4},{8,9},{9,10},{10,1... | collective-permute-start | bytes 491528 | tf_op jit(solution)/shard_map/ppermute | solution.py:446
  5.8 2.2 %collective-permute-start = (bf16[128,640]{1,0:T(8,128)(2,1)}, bf16[128,640]{1,0:T(8,128)(2,1)S(1)}, u32[]{:S(2)}, u32[]{:S(2)}) collective-permute-start(bf16[128,640]{1,0:T(8,128)(2,1)} %bitcast.9), channel_id=1, source_target_pairs={{0,1},{1,2},{2,3},{3,0},{4,5},{5,6},{6,7},{7,4},{8,9},{9,10},{10,1... | collective-permute-start | bytes 491528 | tf_op jit(solution)/shard_map/ppermute | solution.py:446
  8.0 0.7 collective-permute-done.1.og3
  8.7 3.8 %collective-permute-start.2 = (bf16[128,640]{1,0:T(8,128)(2,1)S(1)}, bf16[128,640]{1,0:T(8,128)(2,1)S(1)}, u32[]{:S(2)}, u32[]{:S(2)}) collective-permute-start(bf16[128,640]{1,0:T(8,128)(2,1)S(1)} %collective-permute-done.1.og3), channel_id=1, source_target_pairs={{0,3},{1,0},{2,1},{3,2},{4,7},{5,4},{6,5},{7,6},{8,11},{9,8},{10,9... | collective-permute-start | bytes 491528 | tf_op jit(solution)/shard_map/ppermute | solution.py:443
  13.2 0.7 reshape.26.gain
  13.8 0.8 copy.18.sizes
  14.6 0.0 copy-start
  14.6 0.0 copy-start.1
  14.6 0.0 copy-start.2
  14.6 0.0 copy-start.3
  14.6 1.1 %collective-permute-done.5.xg3 = bf16[128,640]{1,0:T(8,128)(2,1)S(1)} collective-permute-done((bf16[128,640]{1,0:T(8,128)(2,1)}, bf16[128,640]{1,0:T(8,128)(2,1)S(1)}, u32[]{:S(2)}, u32[]{:S(2)}) %collective-permute-start.5) | collective-permute-done | bytes 163872 | tf_op jit(solution)/shard_map/ppermute | solution.py:441
  15.7 0.0 collective-permute-done.4.xg2
  15.7 0.0 collective-permute-done.3.xg1
  15.7 0.0 copy-start.4
  15.7 0.9 %copy-done.4 = bf16[1,8,16,640]{3,2,1,0:T(8,128)(2,1)S(1)} copy-done((bf16[1,8,16,640]{3,2,1,0:T(8,128)(2,1)S(1)}, bf16[1,8,16,640]{3,2,1,0:T(8,128)(2,1)}, u32[]{:S(2)}) %copy-start.4) | copy-done | bytes 163864
  16.7 0.0 copy-start.5
  16.7 8.9 %front.1 = (bf16[512,640]{1,0:T(8,128)(2,1)S(1)}, f32[512,640]{1,0:T(8,128)S(1)}, bf16[512,640]{1,0:T(8,128)(2,1)S(1)}, bf16[512,640]{1,0:T(8,128)(2,1)S(1)}) custom-call(s32[1]{0:T(128)S(6)} %copy.19.bucket, s32[8,2]{1,0:T(8,128)S(1)} %copy.18.sizes, bf16[128,640]{1,0:T(8,128)(2,1)S(1)} %bitcast.7, bf16[128,640]{1,0:T(8,128)(2,1)S(1)} %collective-permute-done.3.xg1, ...), custom_call_target="tpu_custom_call" | custom-call | tf_op jit(solution)/shard_map/front/pallas_call | solution.py:355
  25.5 0.0 collective-permute-done.og1
  25.6 0.0 collective-permute-done.2.og2
  25.6 0.0 copy-done
  25.6 0.0 copy-done.1
  25.6 0.0 copy-done.2
  25.6 0.0 copy-done.3
  25.6 0.0 copy-done.5
  25.6 19.8 %back.1 = (bf16[16,352,128]{2,1,0:T(8,128)(2,1)S(1)}, bf16[256,640]{1,0:T(8,128)(2,1)S(1)}, f32[3200,128]{1,0:T(8,128)S(1)}, f32[5760,128]{1,0:T(8,128)S(1)}, f32[5760,128]{1,0:T(8,128)S(1)}) custom-call(s32[1]{0:T(128)S(6)} %copy.19.bucket, s32[8,2]{1,0:T(8,128)S(1)} %copy.18.sizes, bf16[128,640]{1,0:T(8,128)(2,1)S(1)} %bitcast.10, ...), custom_call_target="tpu_custom_call" | custom-call | tf_op jit(solution)/shard_map/back/pallas_call | solution.py:372
  45.4 0.1 collective-permute-start.6
  45.5 2.4 %rest.1 = (bf16[128,640]{1,0:T(8,128)(2,1)}, bf16[16,352,128]{2,1,0:T(8,128)(2,1)S(1)}) custom-call(s32[1]{0:T(128)S(6)} %copy.19.bucket, s32[8,2]{1,0:T(8,128)S(1)} %copy.18.sizes, bf16[256,640]{1,0:T(8,128)(2,1)S(1)} %get-tuple-element.26.ctx, bf16[512,640]{1,0:T(8,128)(2,1)S(1)} %get-tuple-element.23.hid, bf16[640,640]{1,0:T(8,128)(2,1)S(1)} %copy-done, ...), custom_call_target="tpu_custom_call" | custom-call | tf_op jit(solution)/shard_map/rest/pallas_call | solution.py:410
  47.9 0.8 %collective-permute-done.6 = bf16[16,352,128]{2,1,0:T(8,128)(2,1)S(1)} collective-permute-done((bf16[16,352,128]{2,1,0:T(8,128)(2,1)S(1)}, bf16[16,352,128]{2,1,0:T(8,128)(2,1)S(1)}, u32[]{:S(2)}, u32[]{:S(2)}) %collective-permute-start.6) | collective-permute-done | bytes 1441824 | tf_op jit(solution)/shard_map/ppermute | solution.py:464
  48.7 0.4 add_convert_fusion
  49.1 29.5 %all_to_all.5.pieces = bf16[16,352,128]{2,1,0:T(8,128)(2,1)} all-to-all(bf16[16,352,128]{2,1,0:T(8,128)(2,1)S(1)} %add_convert_fusion), channel_id=1, replica_groups={{0,8,16,24,32,40,48,56,64,72,80,88,96,104,112,120},{4,12,20,28,36,44,52..., dimensions={0} | all-to-all | bytes 2883584 | tf_op jit(solution)/shard_map/all_to_all | solution.py:468
  78.6 2.3 %last.1 = (f32[160,180]{1,0:T(8,128)}, f32[20,160]{1,0:T(8,128)}, f32[20,160]{1,0:T(8,128)}, f32[20,160]{1,0:T(8,128)}, f32[20,160]{1,0:T(8,128)}) custom-call(bf16[16,352,128]{2,1,0:T(8,128)(2,1)} %all_to_all.5.pieces), custom_call_target="tpu_custom_call" | custom-call | tf_op jit(solution)/shard_map/last/pallas_call | solution.py:429
Async XLA Ops:
  0.6 8.1 %collective-permute-start.1 = (bf16[128,640]{1,0:T(8,128)(2,1)}, bf16[128,640]{1,0:T(8,128)(2,1)S(1)}, u32[]{:S(2)}, u32[]{:S(2)}) collective-permute-start(bf16[128,640]{1,0:T(8,128)(2,1)} %bitcast.8), channel_id=1, source_target_pairs={{0,3},{1,0},{2,1},{3,2},{4,7},{5,4},{6,5},{7,6},{8,11},{9,8},{10,9... | collective-permute-start | bytes 491528 | tf_op jit(solution)/shard_map/ppermute | solution.py:441
  3.8 11.9 %collective-permute-start.5 = (bf16[128,640]{1,0:T(8,128)(2,1)}, bf16[128,640]{1,0:T(8,128)(2,1)S(1)}, u32[]{:S(2)}, u32[]{:S(2)}) collective-permute-start(bf16[128,640]{1,0:T(8,128)(2,1)} %bitcast.4), channel_id=1, source_target_pairs={{0,3},{1,0},{2,1},{3,2},{4,7},{5,4},{6,5},{7,6},{8,11},{9,8},{10,9... | collective-permute-start | bytes 491528 | tf_op jit(solution)/shard_map/ppermute | solution.py:441
  4.5 11.2 %collective-permute-start.4 = (bf16[128,640]{1,0:T(8,128)(2,1)}, bf16[128,640]{1,0:T(8,128)(2,1)S(1)}, u32[]{:S(2)}, u32[]{:S(2)}) collective-permute-start(bf16[128,640]{1,0:T(8,128)(2,1)} %bitcast.5), channel_id=1, source_target_pairs={{0,2},{1,3},{2,0},{3,1},{4,6},{5,7},{6,4},{7,5},{8,10},{9,11},{10,... | collective-permute-start | bytes 491528 | tf_op jit(solution)/shard_map/ppermute | solution.py:445
  4.8 11.0 %collective-permute-start.3 = (bf16[128,640]{1,0:T(8,128)(2,1)}, bf16[128,640]{1,0:T(8,128)(2,1)S(1)}, u32[]{:S(2)}, u32[]{:S(2)}) collective-permute-start(bf16[128,640]{1,0:T(8,128)(2,1)} %bitcast.6), channel_id=1, source_target_pairs={{0,1},{1,2},{2,3},{3,0},{4,5},{5,6},{6,7},{7,4},{8,9},{9,10},{10,1... | collective-permute-start | bytes 491528 | tf_op jit(solution)/shard_map/ppermute | solution.py:446
  5.8 19.7 %collective-permute-start = (bf16[128,640]{1,0:T(8,128)(2,1)}, bf16[128,640]{1,0:T(8,128)(2,1)S(1)}, u32[]{:S(2)}, u32[]{:S(2)}) collective-permute-start(bf16[128,640]{1,0:T(8,128)(2,1)} %bitcast.9), channel_id=1, source_target_pairs={{0,1},{1,2},{2,3},{3,0},{4,5},{5,6},{6,7},{7,4},{8,9},{9,10},{10,1... | collective-permute-start | bytes 491528 | tf_op jit(solution)/shard_map/ppermute | solution.py:446
  8.7 16.8 %collective-permute-start.2 = (bf16[128,640]{1,0:T(8,128)(2,1)S(1)}, bf16[128,640]{1,0:T(8,128)(2,1)S(1)}, u32[]{:S(2)}, u32[]{:S(2)}) collective-permute-start(bf16[128,640]{1,0:T(8,128)(2,1)S(1)} %collective-permute-done.1.og3), channel_id=1, source_target_pairs={{0,3},{1,0},{2,1},{3,2},{4,7},{5,4},{6,5},{7,6},{8,11},{9,8},{10,9... | collective-permute-start | bytes 491528 | tf_op jit(solution)/shard_map/ppermute | solution.py:443
  14.6 11.0 %copy-start = (bf16[640,640]{1,0:T(8,128)(2,1)S(1)}, bf16[640,640]{1,0:T(8,128)(2,1)}, u32[]{:S(2)}) copy-start(bf16[640,640]{1,0:T(8,128)(2,1)} %wo.3) | copy-start | bytes 2457604
  14.6 11.0 %copy-start.1 = (bf16[640,640]{1,0:T(8,128)(2,1)S(1)}, bf16[640,640]{1,0:T(8,128)(2,1)}, u32[]{:S(2)}) copy-start(bf16[640,640]{1,0:T(8,128)(2,1)} %wq.1) | copy-start | bytes 2457604
  14.6 11.0 %copy-start.2 = (bf16[640,640]{1,0:T(8,128)(2,1)S(1)}, bf16[640,640]{1,0:T(8,128)(2,1)}, u32[]{:S(2)}) copy-start(bf16[640,640]{1,0:T(8,128)(2,1)} %wk.1) | copy-start | bytes 2457604
  14.6 11.0 %copy-start.3 = (bf16[640,640]{1,0:T(8,128)(2,1)S(1)}, bf16[640,640]{1,0:T(8,128)(2,1)}, u32[]{:S(2)}) copy-start(bf16[640,640]{1,0:T(8,128)(2,1)} %wv.1) | copy-start | bytes 2457604
  15.7 0.9 %copy-start.4 = (bf16[1,8,16,640]{3,2,1,0:T(8,128)(2,1)S(1)}, bf16[1,8,16,640]{3,2,1,0:T(8,128)(2,1)}, u32[]{:S(2)}) copy-start(bf16[1,8,16,640]{3,2,1,0:T(8,128)(2,1)} %param.10) | copy-start | bytes 491524
  16.7 8.9 %copy-start.5 = (bf16[1,8,16,640]{3,2,1,0:T(8,128)(2,1)S(1)}, bf16[1,8,16,640]{3,2,1,0:T(8,128)(2,1)}, u32[]{:S(2)}) copy-start(bf16[1,8,16,640]{3,2,1,0:T(8,128)(2,1)} %param.19) | copy-start | bytes 491524
  45.4 3.3 %collective-permute-start.6 = (bf16[16,352,128]{2,1,0:T(8,128)(2,1)S(1)}, bf16[16,352,128]{2,1,0:T(8,128)(2,1)S(1)}, u32[]{:S(2)}, u32[]{:S(2)}) collective-permute-start(bf16[16,352,128]{2,1,0:T(8,128)(2,1)S(1)} %get-tuple-element.32), channel_id=1, source_target_pairs={{0,4},{4,0},{8,12},{12,8},{16,20},{20,16},{24,28},{28,24},{32,36},... | collective-permute-start | bytes 4325384 | tf_op jit(solution)/shard_map/ppermute | solution.py:464

commit v5 on v4

--- a/solution.py
+++ b/solution.py
@@ -20,9 +20,9 @@
 QUARTER = CONV_ROWS // 4
 PROJ_ROWS = CH // PIECES
 AT_PROJ_REST = 4 * PROJ_ROWS
-AT_CONV = 112
-AT_CONV_REST = 304
-PIECE = 352
+AT_CONV = 100
+AT_CONV_REST = 280
+PIECE = 336
 
 f32 = jnp.float32
 bf16 = jnp.bfloat16
@@ -150,8 +150,7 @@
         zero = jnp.zeros((), bf16)
         q2, g2 = q[:, lanes], gc[:, lanes]
         s = dot_t(jnp.where(own, k[:, lanes], bias[e]), jnp.where(own, q2, one))
-        dp = dot_t(v[:, lanes], jnp.where(own, g2, zero))
-        return dict(h=h, s=s, dp=dp, qm=jnp.where(own, q2, zero), gm=jnp.where(own, g2, zero))
+        return dict(h=h, s=s, qm=jnp.where(own, q2, zero), gm=jnp.where(own, g2, zero))
 
     def stage_b(t):
         s = t.pop("s")
@@ -169,6 +168,9 @@
         t["inv"] = inv
 
     def stage_d(t):
+        h = t["h"]
+        lanes = slice(h // 2 * 2 * WIDTH, (h // 2 + 1) * 2 * WIDTH)
+        t["dp"] = dot_t(v[:, lanes], t["gm"])
         t["ds"] = (t.pop("ex") * (t.pop("dp") - t.pop("delta"))).astype(bf16)
 
     def stage_e(t):
@@ -290,22 +292,19 @@
 
 def pack(meta, flip, gproj, gmain, grest, stage, out):
     stage[...] = jnp.zeros_like(stage)
+    side = meta[4] ^ flip
     for j in range(PIECES // 2):
-        for c in range(2):
-            d = 2 * j + c
-            for w in range(5):
-                stage[c, w * PROJ_ROWS : (w + 1) * PROJ_ROWS, :] = gproj[
-                    w * CH + d * PROJ_ROWS : w * CH + (d + 1) * PROJ_ROWS, :
-                ]
-            stage[c, AT_CONV : AT_CONV + CONV_ROWS, :] = gmain[d * CONV_ROWS : (d + 1) * CONV_ROWS, :]
-            stage[c, AT_CONV_REST : AT_CONV_REST + QUARTER, :] = jnp.concatenate(
-                [
-                    grest[d * CONV_ROWS + g * QUARTER : d * CONV_ROWS + (g + 1) * QUARTER, 0:REST]
-                    for g in range(4)
-                ],
-                axis=1,
-            )
-        out[j] = jnp.where(meta[4] == flip, stage[0], stage[1]).astype(bf16)
+        d = 2 * j + side
+        for w in range(5):
+            stage[w * PROJ_ROWS : (w + 1) * PROJ_ROWS, :] = gproj[
+                pl.ds(w * CH + d * PROJ_ROWS, PROJ_ROWS), :
+            ]
+        first = d * CONV_ROWS
+        stage[AT_CONV : AT_CONV + CONV_ROWS, :] = gmain[pl.ds(first, CONV_ROWS), :]
+        stage[AT_CONV_REST : AT_CONV_REST + QUARTER, :] = jnp.concatenate(
+            [grest[pl.ds(first + g * QUARTER, QUARTER), 0:REST] for g in range(4)], axis=1
+        )
+        out[j] = stage[...].astype(bf16)
 
 
 def rest_kernel(bucket, sizes, ctx, hid, wo, gproj, gmain, grest, blk_o, mine_o, stage, half):
@@ -400,7 +399,7 @@
             pltpu.VMEM((CELLS, 12 * 128), bf16),
             pltpu.VMEM((3, CELLS + 2 * COLS, 128), bf16),
             pltpu.VMEM((CELLS + 2 * COLS, 3 * 128), f32),
-            pltpu.VMEM((2, PIECE, 128), f32),
+            pltpu.VMEM((PIECE, 128), f32),
         ],
         compiler_params=pltpu.CompilerParams(vmem_limit_bytes=32 * 2**20),
     )(*sizes, *og, xin, hid, nrm, pre, gain, wq, wk, wv, wo)
@@ -417,7 +416,7 @@
         in_specs=[SM, SM] + [VM] * 6,
         out_specs=[VM] * 2,
         scratch_shapes=[
-            pltpu.VMEM((2, PIECE, 128), f32),
+            pltpu.VMEM((PIECE, 128), f32),
             pltpu.VMEM((CELLS // 2, CH), f32),
         ],
         compiler_params=pltpu.CompilerParams(vmem_limit_bytes=20 * 2**20),

time: 81.6 us -> 79.5 us (0.974)
  Pallas kernels: 33.3 us -> 31.6 us
    pallas_call x1, Pallas kernels: 19.8 us -> 18.4 us  [back(): pl.pallas_call(back_kernel, name='back', out_shape=[shape((PIECES // 2, P...]
where the time goes in v5:
time: 79.5 us; the launch traced here: 78.7 us
  Pallas kernels  31.6 us (40%)
  blocking collectives  28.7 us (36%)
  starting transfers between devices  11.3 us (14%)
  waiting for transfers between devices  2.86 us (4%)
  local copies, waits for them, and re-layouts  2.38 us (3%)
  between operations  1.38 us (2%)
    all_to_all x1, blocking collectives, body(): lax.all_to_all(both, 'dp', 0, 0, tiled=True, axis_index_groups=groups)  28.7 us
    pallas_call x1, Pallas kernels, back(): pl.pallas_call(back_kernel, name='back', out_shape=[shape((PIECES // 2, P...  18.4 us
    pallas_call x1, Pallas kernels, front(): pl.pallas_call(front_kernel, name='front', out_shape=[shape(flat, bf16),...  8.87 us
    ppermute x2, starting transfers between devices, from_ring(): ahead = lax.ppermute(own, ring, [(i, (i + 3) % 4) for i in range(4)])  3.91 us
    ppermute x1, starting transfers between devices, from_ring(): across = lax.ppermute(ahead, ring, [(i, (i + 3) % 4) for i in range(4)])  3.77 us
    ppermute x2, starting transfers between devices, from_ring(): behind = lax.ppermute(own, ring, [(i, (i + 1) % 4) for i in range(4)])  3.24 us
    pallas_call x1, Pallas kernels, last(): pl.pallas_call(last_kernel, name='last', out_shape=[shape((PART, CONV_ROW...  2.27 us
    pallas_call x1, Pallas kernels, rest(): pl.pallas_call(rest_kernel, name='rest', out_shape=[shape((TILE_ROWS * TI...  2.1 us
  transfers between devices with their start and end apart: 7, of which 3 were waited for; matrix products, arithmetic and copies ran while one was open for 2% of the time, Pallas kernels for 14%

profile of v5, /device:TPU:0, one launch (start us, length us, event | category | flops | bytes accessed | tf_op | source)
XLA Modules:
  0.0 78.7 jit_solution(7061468679768720293)
XLA Ops:
  0.6 3.2 %collective-permute-start.1 = (bf16[128,640]{1,0:T(8,128)(2,1)}, bf16[128,640]{1,0:T(8,128)(2,1)S(1)}, u32[]{:S(2)}, u32[]{:S(2)}) collective-permute-start(bf16[128,640]{1,0:T(8,128)(2,1)} %bitcast.8), channel_id=1, source_target_pairs={{0,3},{1,0},{2,1},{3,2},{4,7},{5,4},{6,5},{7,6},{8,11},{9,8},{10,9... | collective-permute-start | bytes 491528 | tf_op jit(solution)/shard_map/ppermute | solution.py:440
  3.8 0.7 collective-permute-start.5
  4.5 0.3 collective-permute-start.4
  4.8 1.1 %collective-permute-start.3 = (bf16[128,640]{1,0:T(8,128)(2,1)}, bf16[128,640]{1,0:T(8,128)(2,1)S(1)}, u32[]{:S(2)}, u32[]{:S(2)}) collective-permute-start(bf16[128,640]{1,0:T(8,128)(2,1)} %bitcast.6), channel_id=1, source_target_pairs={{0,1},{1,2},{2,3},{3,0},{4,5},{5,6},{6,7},{7,4},{8,9},{9,10},{10,1... | collective-permute-start | bytes 491528 | tf_op jit(solution)/shard_map/ppermute | solution.py:445
  5.8 2.2 %collective-permute-start = (bf16[128,640]{1,0:T(8,128)(2,1)}, bf16[128,640]{1,0:T(8,128)(2,1)S(1)}, u32[]{:S(2)}, u32[]{:S(2)}) collective-permute-start(bf16[128,640]{1,0:T(8,128)(2,1)} %bitcast.9), channel_id=1, source_target_pairs={{0,1},{1,2},{2,3},{3,0},{4,5},{5,6},{6,7},{7,4},{8,9},{9,10},{10,1... | collective-permute-start | bytes 491528 | tf_op jit(solution)/shard_map/ppermute | solution.py:445
  8.0 0.7 collective-permute-done.1.og3
  8.7 3.8 %collective-permute-start.2 = (bf16[128,640]{1,0:T(8,128)(2,1)S(1)}, bf16[128,640]{1,0:T(8,128)(2,1)S(1)}, u32[]{:S(2)}, u32[]{:S(2)}) collective-permute-start(bf16[128,640]{1,0:T(8,128)(2,1)S(1)} %collective-permute-done.1.og3), channel_id=1, source_target_pairs={{0,3},{1,0},{2,1},{3,2},{4,7},{5,4},{6,5},{7,6},{8,11},{9,8},{10,9... | collective-permute-start | bytes 491528 | tf_op jit(solution)/shard_map/ppermute | solution.py:442
  13.2 0.7 reshape.26.gain
  13.8 0.8 copy.18.sizes
  14.6 0.0 copy-start
  14.6 0.0 copy-start.1
  14.6 0.0 copy-start.2
  14.6 0.0 copy-start.3
  14.6 1.1 %collective-permute-done.5.xg3 = bf16[128,640]{1,0:T(8,128)(2,1)S(1)} collective-permute-done((bf16[128,640]{1,0:T(8,128)(2,1)}, bf16[128,640]{1,0:T(8,128)(2,1)S(1)}, u32[]{:S(2)}, u32[]{:S(2)}) %collective-permute-start.5) | collective-permute-done | bytes 163872 | tf_op jit(solution)/shard_map/ppermute | solution.py:440
  15.7 0.0 collective-permute-done.4.xg2
  15.7 0.0 collective-permute-done.3.xg1
  15.7 0.0 copy-start.4
  15.7 0.9 %copy-done.4 = bf16[1,8,16,640]{3,2,1,0:T(8,128)(2,1)S(1)} copy-done((bf16[1,8,16,640]{3,2,1,0:T(8,128)(2,1)S(1)}, bf16[1,8,16,640]{3,2,1,0:T(8,128)(2,1)}, u32[]{:S(2)}) %copy-start.4) | copy-done | bytes 163864
  16.7 0.0 copy-start.5
  16.7 8.9 %front.1 = (bf16[512,640]{1,0:T(8,128)(2,1)S(1)}, f32[512,640]{1,0:T(8,128)S(1)}, bf16[512,640]{1,0:T(8,128)(2,1)S(1)}, bf16[512,640]{1,0:T(8,128)(2,1)S(1)}) custom-call(s32[1]{0:T(128)S(6)} %copy.19.bucket, s32[8,2]{1,0:T(8,128)S(1)} %copy.18.sizes, bf16[128,640]{1,0:T(8,128)(2,1)S(1)} %bitcast.7, bf16[128,640]{1,0:T(8,128)(2,1)S(1)} %collective-permute-done.3.xg1, ...), custom_call_target="tpu_custom_call" | custom-call | tf_op jit(solution)/shard_map/front/pallas_call | solution.py:354
  25.5 0.0 collective-permute-done.og1
  25.6 0.0 collective-permute-done.2.og2
  25.6 0.0 copy-done
  25.6 0.0 copy-done.1
  25.6 0.0 copy-done.2
  25.6 0.0 copy-done.3
  25.6 0.0 copy-done.5
  25.6 18.4 %back.1 = (bf16[16,336,128]{2,1,0:T(8,128)(2,1)S(1)}, bf16[256,640]{1,0:T(8,128)(2,1)S(1)}, f32[3200,128]{1,0:T(8,128)S(1)}, f32[5760,128]{1,0:T(8,128)S(1)}, f32[5760,128]{1,0:T(8,128)S(1)}) custom-call(s32[1]{0:T(128)S(6)} %copy.19.bucket, s32[8,2]{1,0:T(8,128)S(1)} %copy.18.sizes, bf16[128,640]{1,0:T(8,128)(2,1)S(1)} %bitcast.10, ...), custom_call_target="tpu_custom_call" | custom-call | tf_op jit(solution)/shard_map/back/pallas_call | solution.py:371
  44.0 0.1 collective-permute-start.6
  44.1 2.1 %rest.1 = (bf16[128,640]{1,0:T(8,128)(2,1)}, bf16[16,336,128]{2,1,0:T(8,128)(2,1)S(1)}) custom-call(s32[1]{0:T(128)S(6)} %copy.19.bucket, s32[8,2]{1,0:T(8,128)S(1)} %copy.18.sizes, bf16[256,640]{1,0:T(8,128)(2,1)S(1)} %get-tuple-element.26.ctx, bf16[512,640]{1,0:T(8,128)(2,1)S(1)} %get-tuple-element.23.hid, bf16[640,640]{1,0:T(8,128)(2,1)S(1)} %copy-done, ...), custom_call_target="tpu_custom_call" | custom-call | tf_op jit(solution)/shard_map/rest/pallas_call | solution.py:409
  46.2 1.0 %collective-permute-done.6 = bf16[16,336,128]{2,1,0:T(8,128)(2,1)S(1)} collective-permute-done((bf16[16,336,128]{2,1,0:T(8,128)(2,1)S(1)}, bf16[16,336,128]{2,1,0:T(8,128)(2,1)S(1)}, u32[]{:S(2)}, u32[]{:S(2)}) %collective-permute-start.6) | collective-permute-done | bytes 1376288 | tf_op jit(solution)/shard_map/ppermute | solution.py:463
  47.2 0.5 add_convert_fusion
  47.7 28.7 %all_to_all.5.pieces = bf16[16,336,128]{2,1,0:T(8,128)(2,1)} all-to-all(bf16[16,336,128]{2,1,0:T(8,128)(2,1)S(1)} %add_convert_fusion), channel_id=1, replica_groups={{0,8,16,24,32,40,48,56,64,72,80,88,96,104,112,120},{4,12,20,28,36,44,52..., dimensions={0} | all-to-all | bytes 2752512 | tf_op jit(solution)/shard_map/all_to_all | solution.py:467
  76.4 2.3 %last.1 = (f32[160,180]{1,0:T(8,128)}, f32[20,160]{1,0:T(8,128)}, f32[20,160]{1,0:T(8,128)}, f32[20,160]{1,0:T(8,128)}, f32[20,160]{1,0:T(8,128)}) custom-call(bf16[16,336,128]{2,1,0:T(8,128)(2,1)} %all_to_all.5.pieces), custom_call_target="tpu_custom_call" | custom-call | tf_op jit(solution)/shard_map/last/pallas_call | solution.py:428
Async XLA Ops:
  0.6 8.1 %collective-permute-start.1 = (bf16[128,640]{1,0:T(8,128)(2,1)}, bf16[128,640]{1,0:T(8,128)(2,1)S(1)}, u32[]{:S(2)}, u32[]{:S(2)}) collective-permute-start(bf16[128,640]{1,0:T(8,128)(2,1)} %bitcast.8), channel_id=1, source_target_pairs={{0,3},{1,0},{2,1},{3,2},{4,7},{5,4},{6,5},{7,6},{8,11},{9,8},{10,9... | collective-permute-start | bytes 491528 | tf_op jit(solution)/shard_map/ppermute | solution.py:440
  3.8 11.9 %collective-permute-start.5 = (bf16[128,640]{1,0:T(8,128)(2,1)}, bf16[128,640]{1,0:T(8,128)(2,1)S(1)}, u32[]{:S(2)}, u32[]{:S(2)}) collective-permute-start(bf16[128,640]{1,0:T(8,128)(2,1)} %bitcast.4), channel_id=1, source_target_pairs={{0,3},{1,0},{2,1},{3,2},{4,7},{5,4},{6,5},{7,6},{8,11},{9,8},{10,9... | collective-permute-start | bytes 491528 | tf_op jit(solution)/shard_map/ppermute | solution.py:440
  4.5 11.2 %collective-permute-start.4 = (bf16[128,640]{1,0:T(8,128)(2,1)}, bf16[128,640]{1,0:T(8,128)(2,1)S(1)}, u32[]{:S(2)}, u32[]{:S(2)}) collective-permute-start(bf16[128,640]{1,0:T(8,128)(2,1)} %bitcast.5), channel_id=1, source_target_pairs={{0,2},{1,3},{2,0},{3,1},{4,6},{5,7},{6,4},{7,5},{8,10},{9,11},{10,... | collective-permute-start | bytes 491528 | tf_op jit(solution)/shard_map/ppermute | solution.py:444
  4.8 11.0 %collective-permute-start.3 = (bf16[128,640]{1,0:T(8,128)(2,1)}, bf16[128,640]{1,0:T(8,128)(2,1)S(1)}, u32[]{:S(2)}, u32[]{:S(2)}) collective-permute-start(bf16[128,640]{1,0:T(8,128)(2,1)} %bitcast.6), channel_id=1, source_target_pairs={{0,1},{1,2},{2,3},{3,0},{4,5},{5,6},{6,7},{7,4},{8,9},{9,10},{10,1... | collective-permute-start | bytes 491528 | tf_op jit(solution)/shard_map/ppermute | solution.py:445
  5.8 19.7 %collective-permute-start = (bf16[128,640]{1,0:T(8,128)(2,1)}, bf16[128,640]{1,0:T(8,128)(2,1)S(1)}, u32[]{:S(2)}, u32[]{:S(2)}) collective-permute-start(bf16[128,640]{1,0:T(8,128)(2,1)} %bitcast.9), channel_id=1, source_target_pairs={{0,1},{1,2},{2,3},{3,0},{4,5},{5,6},{6,7},{7,4},{8,9},{9,10},{10,1... | collective-permute-start | bytes 491528 | tf_op jit(solution)/shard_map/ppermute | solution.py:445
  8.7 16.8 %collective-permute-start.2 = (bf16[128,640]{1,0:T(8,128)(2,1)S(1)}, bf16[128,640]{1,0:T(8,128)(2,1)S(1)}, u32[]{:S(2)}, u32[]{:S(2)}) collective-permute-start(bf16[128,640]{1,0:T(8,128)(2,1)S(1)} %collective-permute-done.1.og3), channel_id=1, source_target_pairs={{0,3},{1,0},{2,1},{3,2},{4,7},{5,4},{6,5},{7,6},{8,11},{9,8},{10,9... | collective-permute-start | bytes 491528 | tf_op jit(solution)/shard_map/ppermute | solution.py:442
  14.6 11.0 %copy-start = (bf16[640,640]{1,0:T(8,128)(2,1)S(1)}, bf16[640,640]{1,0:T(8,128)(2,1)}, u32[]{:S(2)}) copy-start(bf16[640,640]{1,0:T(8,128)(2,1)} %wo.3) | copy-start | bytes 2457604
  14.6 11.0 %copy-start.1 = (bf16[640,640]{1,0:T(8,128)(2,1)S(1)}, bf16[640,640]{1,0:T(8,128)(2,1)}, u32[]{:S(2)}) copy-start(bf16[640,640]{1,0:T(8,128)(2,1)} %wq.1) | copy-start | bytes 2457604
  14.6 11.0 %copy-start.2 = (bf16[640,640]{1,0:T(8,128)(2,1)S(1)}, bf16[640,640]{1,0:T(8,128)(2,1)}, u32[]{:S(2)}) copy-start(bf16[640,640]{1,0:T(8,128)(2,1)} %wk.1) | copy-start | bytes 2457604
  14.6 11.0 %copy-start.3 = (bf16[640,640]{1,0:T(8,128)(2,1)S(1)}, bf16[640,640]{1,0:T(8,128)(2,1)}, u32[]{:S(2)}) copy-start(bf16[640,640]{1,0:T(8,128)(2,1)} %wv.1) | copy-start | bytes 2457604
  15.7 0.9 %copy-start.4 = (bf16[1,8,16,640]{3,2,1,0:T(8,128)(2,1)S(1)}, bf16[1,8,16,640]{3,2,1,0:T(8,128)(2,1)}, u32[]{:S(2)}) copy-start(bf16[1,8,16,640]{3,2,1,0:T(8,128)(2,1)} %param.10) | copy-start | bytes 491524
  16.7 8.9 %copy-start.5 = (bf16[1,8,16,640]{3,2,1,0:T(8,128)(2,1)S(1)}, bf16[1,8,16,640]{3,2,1,0:T(8,128)(2,1)}, u32[]{:S(2)}) copy-start(bf16[1,8,16,640]{3,2,1,0:T(8,128)(2,1)} %param.19) | copy-start | bytes 491524
  44.0 3.2 %collective-permute-start.6 = (bf16[16,336,128]{2,1,0:T(8,128)(2,1)S(1)}, bf16[16,336,128]{2,1,0:T(8,128)(2,1)S(1)}, u32[]{:S(2)}, u32[]{:S(2)}) collective-permute-start(bf16[16,336,128]{2,1,0:T(8,128)(2,1)S(1)} %get-tuple-element.32), channel_id=1, source_target_pairs={{0,4},{4,0},{8,12},{12,8},{16,20},{20,16},{24,28},{28,24},{32,36},... | collective-permute-start | bytes 4128776 | tf_op jit(solution)/shard_map/ppermute | solution.py:463

commit v6 on v5

--- a/solution.py
+++ b/solution.py
@@ -167,10 +167,12 @@
         t["delta"] = jnp.sum(gt[rows, :].astype(f32) * ctx, axis=0, keepdims=True)
         t["inv"] = inv
 
-    def stage_d(t):
+    def stage_p(t):
         h = t["h"]
         lanes = slice(h // 2 * 2 * WIDTH, (h // 2 + 1) * 2 * WIDTH)
         t["dp"] = dot_t(v[:, lanes], t["gm"])
+
+    def stage_d(t):
         t["ds"] = (t.pop("ex") * (t.pop("dp") - t.pop("delta"))).astype(bf16)
 
     def stage_e(t):
@@ -189,14 +191,16 @@
 
     heads = [stage_a(0)]
     for h in range(HEADS + 1):
-        if h + 1 < HEADS:
-            heads.append(stage_a(h + 1))
         if h < HEADS:
             stage_b(heads[h])
         if h > 0:
             stage_e(heads[h - 1])
         if h < HEADS:
             stage_c(heads[h])
+            stage_p(heads[h])
+        if h + 1 < HEADS:
+            heads.append(stage_a(h + 1))
+        if h < HEADS:
             stage_d(heads[h])
         if h > 0 and h % 2 == 0:
             stage_f(heads[h - 2], heads[h - 1])

time: 79.5 us -> 79.6 us (level)
  no operation moved by 1% of the time
where the time goes in v6:
time: 79.6 us; the launch traced here: 78.8 us
  Pallas kernels  31.8 us (40%)
  blocking collectives  28.7 us (36%)
  starting transfers between devices  11.3 us (14%)
  waiting for transfers between devices  2.86 us (4%)
  local copies, waits for them, and re-layouts  2.38 us (3%)
  between operations  1.38 us (2%)
    all_to_all x1, blocking collectives, body(): lax.all_to_all(both, 'dp', 0, 0, tiled=True, axis_index_groups=groups)  28.7 us
    pallas_call x1, Pallas kernels, back(): pl.pallas_call(back_kernel, name='back', out_shape=[shape((PIECES // 2, P...  18.5 us
    pallas_call x1, Pallas kernels, front(): pl.pallas_call(front_kernel, name='front', out_shape=[shape(flat, bf16),...  8.87 us
    ppermute x2, starting transfers between devices, from_ring(): ahead = lax.ppermute(own, ring, [(i, (i + 3) % 4) for i in range(4)])  3.91 us
    ppermute x1, starting transfers between devices, from_ring(): across = lax.ppermute(ahead, ring, [(i, (i + 3) % 4) for i in range(4)])  3.77 us
    ppermute x2, starting transfers between devices, from_ring(): behind = lax.ppermute(own, ring, [(i, (i + 1) % 4) for i in range(4)])  3.24 us
    pallas_call x1, Pallas kernels, last(): pl.pallas_call(last_kernel, name='last', out_shape=[shape((PART, CONV_ROW...  2.27 us
    pallas_call x1, Pallas kernels, rest(): pl.pallas_call(rest_kernel, name='rest', out_shape=[shape((TILE_ROWS * TI...  2.1 us
  transfers between devices with their start and end apart: 7, of which 3 were waited for; matrix products, arithmetic and copies ran while one was open for 2% of the time, Pallas kernels for 14%

profile of v6, /device:TPU:0, one launch (start us, length us, event | category | flops | bytes accessed | tf_op | source)
XLA Modules:
  0.0 78.8 jit_solution(16151238950400027670)
XLA Ops:
  0.6 3.2 %collective-permute-start.1 = (bf16[128,640]{1,0:T(8,128)(2,1)}, bf16[128,640]{1,0:T(8,128)(2,1)S(1)}, u32[]{:S(2)}, u32[]{:S(2)}) collective-permute-start(bf16[128,640]{1,0:T(8,128)(2,1)} %bitcast.8), channel_id=1, source_target_pairs={{0,3},{1,0},{2,1},{3,2},{4,7},{5,4},{6,5},{7,6},{8,11},{9,8},{10,9... | collective-permute-start | bytes 491528 | tf_op jit(solution)/shard_map/ppermute | solution.py:444
  3.8 0.7 collective-permute-start.5
  4.5 0.3 collective-permute-start.4
  4.8 1.1 %collective-permute-start.3 = (bf16[128,640]{1,0:T(8,128)(2,1)}, bf16[128,640]{1,0:T(8,128)(2,1)S(1)}, u32[]{:S(2)}, u32[]{:S(2)}) collective-permute-start(bf16[128,640]{1,0:T(8,128)(2,1)} %bitcast.6), channel_id=1, source_target_pairs={{0,1},{1,2},{2,3},{3,0},{4,5},{5,6},{6,7},{7,4},{8,9},{9,10},{10,1... | collective-permute-start | bytes 491528 | tf_op jit(solution)/shard_map/ppermute | solution.py:449
  5.8 2.2 %collective-permute-start = (bf16[128,640]{1,0:T(8,128)(2,1)}, bf16[128,640]{1,0:T(8,128)(2,1)S(1)}, u32[]{:S(2)}, u32[]{:S(2)}) collective-permute-start(bf16[128,640]{1,0:T(8,128)(2,1)} %bitcast.9), channel_id=1, source_target_pairs={{0,1},{1,2},{2,3},{3,0},{4,5},{5,6},{6,7},{7,4},{8,9},{9,10},{10,1... | collective-permute-start | bytes 491528 | tf_op jit(solution)/shard_map/ppermute | solution.py:449
  8.0 0.7 collective-permute-done.1.og3
  8.7 3.8 %collective-permute-start.2 = (bf16[128,640]{1,0:T(8,128)(2,1)S(1)}, bf16[128,640]{1,0:T(8,128)(2,1)S(1)}, u32[]{:S(2)}, u32[]{:S(2)}) collective-permute-start(bf16[128,640]{1,0:T(8,128)(2,1)S(1)} %collective-permute-done.1.og3), channel_id=1, source_target_pairs={{0,3},{1,0},{2,1},{3,2},{4,7},{5,4},{6,5},{7,6},{8,11},{9,8},{10,9... | collective-permute-start | bytes 491528 | tf_op jit(solution)/shard_map/ppermute | solution.py:446
  13.2 0.7 reshape.26.gain
  13.8 0.8 copy.18.sizes
  14.6 0.0 copy-start
  14.6 0.0 copy-start.1
  14.6 0.0 copy-start.2
  14.6 0.0 copy-start.3
  14.6 1.1 %collective-permute-done.5.xg3 = bf16[128,640]{1,0:T(8,128)(2,1)S(1)} collective-permute-done((bf16[128,640]{1,0:T(8,128)(2,1)}, bf16[128,640]{1,0:T(8,128)(2,1)S(1)}, u32[]{:S(2)}, u32[]{:S(2)}) %collective-permute-start.5) | collective-permute-done | bytes 163872 | tf_op jit(solution)/shard_map/ppermute | solution.py:444
  15.7 0.0 collective-permute-done.4.xg2
  15.7 0.0 collective-permute-done.3.xg1
  15.7 0.0 copy-start.4
  15.7 0.9 %copy-done.4 = bf16[1,8,16,640]{3,2,1,0:T(8,128)(2,1)S(1)} copy-done((bf16[1,8,16,640]{3,2,1,0:T(8,128)(2,1)S(1)}, bf16[1,8,16,640]{3,2,1,0:T(8,128)(2,1)}, u32[]{:S(2)}) %copy-start.4) | copy-done | bytes 163864
  16.7 0.0 copy-start.5
  16.7 8.9 %front.1 = (bf16[512,640]{1,0:T(8,128)(2,1)S(1)}, f32[512,640]{1,0:T(8,128)S(1)}, bf16[512,640]{1,0:T(8,128)(2,1)S(1)}, bf16[512,640]{1,0:T(8,128)(2,1)S(1)}) custom-call(s32[1]{0:T(128)S(6)} %copy.19.bucket, s32[8,2]{1,0:T(8,128)S(1)} %copy.18.sizes, bf16[128,640]{1,0:T(8,128)(2,1)S(1)} %bitcast.7, bf16[128,640]{1,0:T(8,128)(2,1)S(1)} %collective-permute-done.3.xg1, ...), custom_call_target="tpu_custom_call" | custom-call | tf_op jit(solution)/shard_map/front/pallas_call | solution.py:358
  25.5 0.0 collective-permute-done.og1
  25.6 0.0 collective-permute-done.2.og2
  25.6 0.0 copy-done
  25.6 0.0 copy-done.1
  25.6 0.0 copy-done.2
  25.6 0.0 copy-done.3
  25.6 0.0 copy-done.5
  25.6 18.5 %back.1 = (bf16[16,336,128]{2,1,0:T(8,128)(2,1)S(1)}, bf16[256,640]{1,0:T(8,128)(2,1)S(1)}, f32[3200,128]{1,0:T(8,128)S(1)}, f32[5760,128]{1,0:T(8,128)S(1)}, f32[5760,128]{1,0:T(8,128)S(1)}) custom-call(s32[1]{0:T(128)S(6)} %copy.19.bucket, s32[8,2]{1,0:T(8,128)S(1)} %copy.18.sizes, bf16[128,640]{1,0:T(8,128)(2,1)S(1)} %bitcast.10, ...), custom_call_target="tpu_custom_call" | custom-call | tf_op jit(solution)/shard_map/back/pallas_call | solution.py:375
  44.1 0.1 collective-permute-start.6
  44.2 2.1 %rest.1 = (bf16[128,640]{1,0:T(8,128)(2,1)}, bf16[16,336,128]{2,1,0:T(8,128)(2,1)S(1)}) custom-call(s32[1]{0:T(128)S(6)} %copy.19.bucket, s32[8,2]{1,0:T(8,128)S(1)} %copy.18.sizes, bf16[256,640]{1,0:T(8,128)(2,1)S(1)} %get-tuple-element.26.ctx, bf16[512,640]{1,0:T(8,128)(2,1)S(1)} %get-tuple-element.23.hid, bf16[640,640]{1,0:T(8,128)(2,1)S(1)} %copy-done, ...), custom_call_target="tpu_custom_call" | custom-call | tf_op jit(solution)/shard_map/rest/pallas_call | solution.py:413
  46.3 1.0 %collective-permute-done.6 = bf16[16,336,128]{2,1,0:T(8,128)(2,1)S(1)} collective-permute-done((bf16[16,336,128]{2,1,0:T(8,128)(2,1)S(1)}, bf16[16,336,128]{2,1,0:T(8,128)(2,1)S(1)}, u32[]{:S(2)}, u32[]{:S(2)}) %collective-permute-start.6) | collective-permute-done | bytes 1376288 | tf_op jit(solution)/shard_map/ppermute | solution.py:467
  47.3 0.5 add_convert_fusion
  47.8 28.7 %all_to_all.5.pieces = bf16[16,336,128]{2,1,0:T(8,128)(2,1)} all-to-all(bf16[16,336,128]{2,1,0:T(8,128)(2,1)S(1)} %add_convert_fusion), channel_id=1, replica_groups={{0,8,16,24,32,40,48,56,64,72,80,88,96,104,112,120},{4,12,20,28,36,44,52..., dimensions={0} | all-to-all | bytes 2752512 | tf_op jit(solution)/shard_map/all_to_all | solution.py:471
  76.6 2.3 %last.1 = (f32[160,180]{1,0:T(8,128)}, f32[20,160]{1,0:T(8,128)}, f32[20,160]{1,0:T(8,128)}, f32[20,160]{1,0:T(8,128)}, f32[20,160]{1,0:T(8,128)}) custom-call(bf16[16,336,128]{2,1,0:T(8,128)(2,1)} %all_to_all.5.pieces), custom_call_target="tpu_custom_call" | custom-call | tf_op jit(solution)/shard_map/last/pallas_call | solution.py:432
Async XLA Ops:
  0.6 8.1 %collective-permute-start.1 = (bf16[128,640]{1,0:T(8,128)(2,1)}, bf16[128,640]{1,0:T(8,128)(2,1)S(1)}, u32[]{:S(2)}, u32[]{:S(2)}) collective-permute-start(bf16[128,640]{1,0:T(8,128)(2,1)} %bitcast.8), channel_id=1, source_target_pairs={{0,3},{1,0},{2,1},{3,2},{4,7},{5,4},{6,5},{7,6},{8,11},{9,8},{10,9... | collective-permute-start | bytes 491528 | tf_op jit(solution)/shard_map/ppermute | solution.py:444
  3.8 11.9 %collective-permute-start.5 = (bf16[128,640]{1,0:T(8,128)(2,1)}, bf16[128,640]{1,0:T(8,128)(2,1)S(1)}, u32[]{:S(2)}, u32[]{:S(2)}) collective-permute-start(bf16[128,640]{1,0:T(8,128)(2,1)} %bitcast.4), channel_id=1, source_target_pairs={{0,3},{1,0},{2,1},{3,2},{4,7},{5,4},{6,5},{7,6},{8,11},{9,8},{10,9... | collective-permute-start | bytes 491528 | tf_op jit(solution)/shard_map/ppermute | solution.py:444
  4.5 11.2 %collective-permute-start.4 = (bf16[128,640]{1,0:T(8,128)(2,1)}, bf16[128,640]{1,0:T(8,128)(2,1)S(1)}, u32[]{:S(2)}, u32[]{:S(2)}) collective-permute-start(bf16[128,640]{1,0:T(8,128)(2,1)} %bitcast.5), channel_id=1, source_target_pairs={{0,2},{1,3},{2,0},{3,1},{4,6},{5,7},{6,4},{7,5},{8,10},{9,11},{10,... | collective-permute-start | bytes 491528 | tf_op jit(solution)/shard_map/ppermute | solution.py:448
  4.8 11.0 %collective-permute-start.3 = (bf16[128,640]{1,0:T(8,128)(2,1)}, bf16[128,640]{1,0:T(8,128)(2,1)S(1)}, u32[]{:S(2)}, u32[]{:S(2)}) collective-permute-start(bf16[128,640]{1,0:T(8,128)(2,1)} %bitcast.6), channel_id=1, source_target_pairs={{0,1},{1,2},{2,3},{3,0},{4,5},{5,6},{6,7},{7,4},{8,9},{9,10},{10,1... | collective-permute-start | bytes 491528 | tf_op jit(solution)/shard_map/ppermute | solution.py:449
  5.8 19.7 %collective-permute-start = (bf16[128,640]{1,0:T(8,128)(2,1)}, bf16[128,640]{1,0:T(8,128)(2,1)S(1)}, u32[]{:S(2)}, u32[]{:S(2)}) collective-permute-start(bf16[128,640]{1,0:T(8,128)(2,1)} %bitcast.9), channel_id=1, source_target_pairs={{0,1},{1,2},{2,3},{3,0},{4,5},{5,6},{6,7},{7,4},{8,9},{9,10},{10,1... | collective-permute-start | bytes 491528 | tf_op jit(solution)/shard_map/ppermute | solution.py:449
  8.7 16.8 %collective-permute-start.2 = (bf16[128,640]{1,0:T(8,128)(2,1)S(1)}, bf16[128,640]{1,0:T(8,128)(2,1)S(1)}, u32[]{:S(2)}, u32[]{:S(2)}) collective-permute-start(bf16[128,640]{1,0:T(8,128)(2,1)S(1)} %collective-permute-done.1.og3), channel_id=1, source_target_pairs={{0,3},{1,0},{2,1},{3,2},{4,7},{5,4},{6,5},{7,6},{8,11},{9,8},{10,9... | collective-permute-start | bytes 491528 | tf_op jit(solution)/shard_map/ppermute | solution.py:446
  14.6 11.0 %copy-start = (bf16[640,640]{1,0:T(8,128)(2,1)S(1)}, bf16[640,640]{1,0:T(8,128)(2,1)}, u32[]{:S(2)}) copy-start(bf16[640,640]{1,0:T(8,128)(2,1)} %wo.3) | copy-start | bytes 2457604
  14.6 11.0 %copy-start.1 = (bf16[640,640]{1,0:T(8,128)(2,1)S(1)}, bf16[640,640]{1,0:T(8,128)(2,1)}, u32[]{:S(2)}) copy-start(bf16[640,640]{1,0:T(8,128)(2,1)} %wq.1) | copy-start | bytes 2457604
  14.6 11.0 %copy-start.2 = (bf16[640,640]{1,0:T(8,128)(2,1)S(1)}, bf16[640,640]{1,0:T(8,128)(2,1)}, u32[]{:S(2)}) copy-start(bf16[640,640]{1,0:T(8,128)(2,1)} %wk.1) | copy-start | bytes 2457604
  14.6 11.0 %copy-start.3 = (bf16[640,640]{1,0:T(8,128)(2,1)S(1)}, bf16[640,640]{1,0:T(8,128)(2,1)}, u32[]{:S(2)}) copy-start(bf16[640,640]{1,0:T(8,128)(2,1)} %wv.1) | copy-start | bytes 2457604
  15.7 0.9 %copy-start.4 = (bf16[1,8,16,640]{3,2,1,0:T(8,128)(2,1)S(1)}, bf16[1,8,16,640]{3,2,1,0:T(8,128)(2,1)}, u32[]{:S(2)}) copy-start(bf16[1,8,16,640]{3,2,1,0:T(8,128)(2,1)} %param.10) | copy-start | bytes 491524
  16.7 8.9 %copy-start.5 = (bf16[1,8,16,640]{3,2,1,0:T(8,128)(2,1)S(1)}, bf16[1,8,16,640]{3,2,1,0:T(8,128)(2,1)}, u32[]{:S(2)}) copy-start(bf16[1,8,16,640]{3,2,1,0:T(8,128)(2,1)} %param.19) | copy-start | bytes 491524
  44.1 3.2 %collective-permute-start.6 = (bf16[16,336,128]{2,1,0:T(8,128)(2,1)S(1)}, bf16[16,336,128]{2,1,0:T(8,128)(2,1)S(1)}, u32[]{:S(2)}, u32[]{:S(2)}) collective-permute-start(bf16[16,336,128]{2,1,0:T(8,128)(2,1)S(1)} %get-tuple-element.32), channel_id=1, source_target_pairs={{0,4},{4,0},{8,12},{12,8},{16,20},{20,16},{24,28},{28,24},{32,36},... | collective-permute-start | bytes 4128776 | tf_op jit(solution)/shard_map/ppermute | solution.py:467
